TPU v7x, 32 devices: a whole 2x2x4 slice. The times are simulated.
32 devices in a mesh: dp: 4 (over y, x), proto: 8 (over z, core).
Axes of the slice: x: 2, y: 2, z: 4, core: 2. Of those that a mesh axis runs over, the one named last changes fastest.
Arguments:
- student_patch: bfloat16 [4, 1024, 256], P('dp', 'proto'), may hold values from -4 to 4
- teacher_patch: bfloat16 [4, 1024, 256], P('dp', 'proto'), may hold values from -4 to 4
- patch_image: int32 [4, 1024], P('dp', 'proto'), may hold values from 0 to 3, never falling along the last dimension, each value on 1 to 512 neighbouring positions
- masked_rows: int32 [4, 512], P('dp', 'proto'), may hold values from 0 to 127, as said below
- student_proto: float32 [256, 131072], P(None, 'proto'), as said below
- teacher_proto: float32 [256, 131072], P(None, 'proto'), as said below
- first_moment: float32 [256, 131072], P('dp', 'proto'), as said below
- second_moment: float32 [256, 131072], P('dp', 'proto'), as said below
- centre: float32 [131072], P('proto'), may hold values from -0.3 to 0.3
Outputs:
- row_grad: float32 [4, 512, 256], P('dp', 'proto')
- new_student: float32 [256, 131072], P('dp', 'proto')
- new_first: float32 [256, 131072], P('dp', 'proto')
- new_second: float32 [256, 131072], P('dp', 'proto')
- new_teacher: float32 [256, 131072], P('dp', 'proto')
- loss: float32 [], replicated
Inputs may be any that keep to these rules, and one draw needn't show every extreme that they name: `masked_rows`: for each data group and each index of proto in order, 64 distinct positions among that device's 128 patches, ascending; position 0 and position 127 of every device are always masked. `student_proto`: finite entries. `teacher_proto`: finite entries. `first_moment`: finite entries. `second_moment`: positive entries.
All inputs are finite; a program needn't handle non-finite values.
Results may differ from a plain program's by a relative error of at most 0.014.
Values may be sent and summed in bfloat16 or wider, within the bound.
No kernel may reach another device: no remote copies, remote signals or barrier semaphores. Data moves between devices by JAX's collectives and lax.ppermute only.
A program may use at most 256 MiB of HBM per device.

v0:
```python
import jax
import jax.numpy as jnp
from jax import lax
from jax.sharding import PartitionSpec as P

PATCH_IMG = 256


student_temp = 0.1
teacher_temp = 0.07
beta_one = 0.9
beta_two = 0.999
fix_one = 0.9999734386011124
fix_two = 0.09520785288629038
learn_rate = 0.002
decay_rate = 0.04
teacher_keep = 0.994


def unit_rows(raw_rows):
    inverse = lax.rsqrt(jnp.sum(raw_rows * raw_rows, axis=-1, keepdims=True) + 1e-06)
    return (raw_rows * inverse, inverse)


def local(
    student_patch,
    teacher_patch,
    patch_image,
    masked_rows,
    student_proto,
    teacher_proto,
    first_moment,
    second_moment,
    centre,
):
    picked = masked_rows[0]
    mask_count = picked.shape[0]
    patch_count = patch_image.shape[1]
    proto_count = lax.axis_size("proto")
    data_count = lax.axis_size("dp")
    raw_student = student_patch[0][picked].astype(jnp.float32)
    raw_teacher = teacher_patch[0][picked].astype(jnp.float32)
    unit_student, inv_student = unit_rows(raw_student)
    unit_teacher, inv_teacher = unit_rows(raw_teacher)
    stacked = jnp.stack([unit_student, unit_teacher]).astype(jnp.bfloat16)
    gathered, image_ids = (
        lax.all_gather(stacked, "proto", axis=1, tiled=True),
        lax.all_gather(patch_image[0][picked], "proto", axis=0, tiled=True),
    )
    rows_student = gathered[0]
    rows_teacher = gathered[1]
    student_w = student_proto.astype(jnp.bfloat16)
    teacher_w = teacher_proto.astype(jnp.bfloat16)
    student_logit = (
        jnp.dot(rows_student, student_w, preferred_element_type=jnp.float32) / student_temp
    )
    teacher_raw = jnp.dot(rows_teacher, teacher_w, preferred_element_type=jnp.float32)
    teacher_logit = (teacher_raw - centre) / teacher_temp
    peak_s, peak_t = lax.pmax(
        (jnp.max(student_logit, axis=1), jnp.max(teacher_logit, axis=1)), "proto"
    )
    exp_s = jnp.exp(student_logit - peak_s[:, None])
    exp_t = jnp.exp(teacher_logit - peak_t[:, None])
    total_s, total_t = lax.psum((jnp.sum(exp_s, axis=1), jnp.sum(exp_t, axis=1)), "proto")
    prob_s = exp_s / total_s[:, None]
    prob_t = exp_t / total_t[:, None]
    labels = jnp.arange(patch_count * proto_count // PATCH_IMG, dtype=jnp.int32)
    matches = (image_ids[:, None] == labels[None, :]).astype(jnp.float32)
    counts = jnp.sum(matches, axis=0)
    per_row = jnp.dot(matches, counts, precision=lax.Precision.HIGHEST)
    row_ratio = mask_count * PATCH_IMG / patch_count
    weights = row_ratio / per_row
    log_total = peak_s + jnp.log(total_s)
    partial_loss = jnp.sum(weights * jnp.sum(prob_t * (log_total[:, None] - student_logit), axis=1))
    grad_logit = (weights[:, None] * (prob_s - prob_t) / student_temp).astype(jnp.bfloat16)
    unit_grad = lax.psum_scatter(
        lax.dot_general(
            grad_logit, student_w, (((1,), (1,)), ((), ())), preferred_element_type=jnp.float32
        ).astype(jnp.bfloat16),
        "proto",
        scatter_dimension=0,
        tiled=True,
    ).astype(jnp.float32)
    row_grad = (
        inv_student * unit_grad
        - inv_student
        * inv_student
        * inv_student
        * raw_student
        * jnp.sum(raw_student * unit_grad, axis=-1, keepdims=True)
    )
    slab_rows = first_moment.shape[0]
    slab_start = lax.axis_index("dp") * slab_rows
    proto_grad = lax.psum_scatter(
        lax.dot_general(
            rows_student, grad_logit, (((0,), (0,)), ((), ())), preferred_element_type=jnp.float32
        ).astype(jnp.bfloat16),
        "dp",
        scatter_dimension=0,
        tiled=True,
    ).astype(jnp.float32)
    loss_sum = lax.psum(partial_loss, ("dp", "proto"))
    rows_total = mask_count * proto_count * data_count
    own_student = lax.dynamic_slice_in_dim(student_proto, slab_start, slab_rows, 0)
    own_teacher = lax.dynamic_slice_in_dim(teacher_proto, slab_start, slab_rows, 0)
    new_first = beta_one * first_moment + (1.0 - beta_one) * proto_grad
    new_second = beta_two * second_moment + (1.0 - beta_two) * proto_grad * proto_grad
    step_size = new_first / fix_one / (jnp.sqrt(new_second / fix_two) + 1e-08)
    new_student = own_student - learn_rate * (step_size + decay_rate * own_student)
    new_teacher = teacher_keep * own_teacher + (1.0 - teacher_keep) * new_student
    loss = loss_sum / rows_total
    return (row_grad[None], new_student, new_first, new_second, new_teacher, loss)


def solution(mesh):
    in_specs = (
        P("dp", "proto", None),
        P("dp", "proto", None),
        P("dp", "proto"),
        P("dp", "proto"),
        P(None, "proto"),
        P(None, "proto"),
        P("dp", "proto"),
        P("dp", "proto"),
        P("proto"),
    )
    out_specs = (
        P("dp", "proto", None),
        P("dp", "proto"),
        P("dp", "proto"),
        P("dp", "proto"),
        P("dp", "proto"),
        P(),
    )
    return jax.shard_map(local, mesh=mesh, in_specs=in_specs, out_specs=out_specs, check_vma=False)
```

profile of v0, /device:TPU:0, one launch (start us, length us, event | category | flops | bytes accessed | tf_op | source)
XLA Modules:
  0.0 317.6 jit_solution(5616256129621701009)
XLA Ops:
  7.2 0.0 copy-start
  7.2 0.0 reduce-scatter.3.cloned.1.call-start
  7.2 0.7 fusion.27
  7.9 1.2 dynamic-slice
  9.8 1.4 gather_fusion.1
  11.2 0.2 dynamic-update-slice
  11.5 10.6 %all-reduce = s32[512]{0:T(512)S(1)} all-reduce(s32[512]{0:T(512)S(1)} %dynamic-update-slice), channel_id=2, replica_groups=mesh['dp'=4,'proto'=8] {'proto'}, use_global_device_ids=true, to_apply=%add | all-reduce | flops 512 | bytes 4096
  22.1 0.1 convert_reduce_fusion
  22.2 0.1 fusion.25
  22.3 0.0 copy-done
  22.4 0.7 gather_fusion
  23.1 0.1 fusion.20
  23.2 1.5 gather_fusion.2
  24.7 0.1 fusion.19
  24.8 0.1 fusion.18
  24.9 14.8 %all_gather.7 = bf16[2,512,256]{2,1,0:T(8,128)(2,1)S(1)} all-gather(bf16[2,64,256]{2,1,0:T(8,128)(2,1)S(1)} %pad_maximum_fusion), channel_id=1, replica_groups=mesh['dp'=4,'proto'=8] {'proto'}, dimensions={1}, use_global_device_ids=true | all-gather | bytes 589824 | tf_op jit(solution)/shard_map/all_gather | solution.py:47
  39.8 0.0 copy-start.3
  39.8 18.9 %multiply_reduce_fusion.1 = (f32[512]{0:T(512)S(1)}, f32[512,16384]{1,0:T(8,128)}) fusion(f32[256,16384]{1,0:T(8,128)} %param.13, bf16[2,512,256]{2,1,0:T(8,128)(2,1)S(1)} %all_gather.7), kind=kOutput, calls=%fused_computation.10 | convolution fusion | flops 4315938304 | bytes 50595840 | tf_op jit(solution)/shard_map/dot_general | solution.py:55
  58.7 0.0 copy-done.3
  58.7 19.1 %fusion.1 = (f32[512]{0:T(512)S(1)}, f32[512,16384]{1,0:T(8,128)}) fusion(f32[16384]{0:T(1024)S(1)} %copy-done.3, f32[256,16384]{1,0:T(8,128)} %param.14, bf16[2,512,256]{2,1,0:T(8,128)(2,1)S(1)} %all_gather.7), kind=kOutput, calls=%fused_computation.9 | convolution fusion | flops 4324326912 | bytes 50661376 | tf_op jit(solution)/shard_map/dot_general | solution.py:57
  77.7 14.5 %all-reduce.2 = (f32[512]{0:T(512)S(1)}, f32[512]{0:T(512)S(1)}) all-reduce(f32[512]{0:T(512)S(1)} %get-tuple-element.18, f32[512]{0:T(512)S(1)} %get-tuple-element.20), channel_id=1, replica_groups=mesh['dp'=4,'proto'=8] {'proto'}, use_global_device_ids=true, to_apply=%region_4.0 | all-reduce | flops 1024 | bytes 8192 | tf_op jit(solution)/shard_map/pmax | solution.py:59
  92.2 0.0 copy-start.2
  92.2 15.2 %fusion.3 = f32[512]{0:T(512)S(1)} fusion(f32[512,16384]{1,0:T(8,128)} %get-tuple-element.21, f32[512]{0:T(512)S(1)} %get-tuple-element.9, f32[16384]{0:T(1024)S(1)} %copy-done.3), kind=kLoop, calls=%fused_computation.12 | loop fusion | flops 33553920 | bytes 33624064 | tf_op jit(solution)/shard_map/reduce_sum | solution.py:64
  107.4 4.9 %copy-done.2 = f32[512,16384]{1,0:T(8,128)S(1)} copy-done((f32[512,16384]{1,0:T(8,128)S(1)}, f32[512,16384]{1,0:T(8,128)}, u32[]{:S(2)}) %copy-start.2) | copy-done | bytes 33554456
  112.4 6.7 %fusion = f32[512]{0:T(512)S(1)} fusion(f32[512,16384]{1,0:T(8,128)S(1)} %copy-done.2, f32[512]{0:T(512)S(1)} %get-tuple-element.8), kind=kLoop, calls=%fused_computation.8 | loop fusion | flops 25165312 | bytes 33558528 | tf_op jit(solution)/shard_map/reduce_sum | solution.py:64
  119.0 13.8 %all-reduce.1 = (f32[512]{0:T(512)S(1)}, f32[512]{0:T(512)S(1)}) all-reduce(f32[512]{0:T(512)S(1)} %fusion, f32[512]{0:T(512)S(1)} %fusion.3), channel_id=1, replica_groups=mesh['dp'=4,'proto'=8] {'proto'}, use_global_device_ids=true, to_apply=%region_6.0 | all-reduce | flops 1024 | bytes 8192 | tf_op jit(solution)/shard_map/psum | solution.py:64
  132.8 30.7 %multiply_reduce_fusion = (f32[512]{0:T(512)S(1)}, bf16[512,16384]{1,0:T(8,128)(2,1)}) fusion(f32[512,16384]{1,0:T(8,128)} %get-tuple-element.19, f32[512]{0:T(512)S(1)} %log_add_fusion, f32[512]{0:T(512)S(1)} %get-tuple-element.7, f32[512]{0:T(512)S(1)} %get-tuple-element.9, f32[512,16384]{1,0:T(8,128)} %get-tuple-element.21, f32[16384]{0:T(1024)S(1)} %copy-done.3, ...), kind=kLoop, calls=%fused_computation.3 | loop fusion | flops 117440000 | bytes 83965952 | tf_op jit(solution)/shard_map/reduce_sum | solution.py:74
  163.5 15.8 %fusion.12 = bf16[512,256]{1,0:T(8,128)(2,1)} fusion(bf16[512,16384]{1,0:T(8,128)(2,1)} %get-tuple-element.15, f32[256,16384]{1,0:T(8,128)} %param.13), kind=kOutput, calls=%fused_computation.26 | convolution fusion | flops 4299292672 | bytes 33816576 | tf_op jit(solution)/shard_map/dot_general | solution.py:77
  179.2 0.0 reduce-scatter.3.cloned.1.call-update
  179.2 0.0 reduce-scatter.5.cloned.1.call-start
  179.3 12.7 %convolution_convert_fusion = bf16[256,16384]{1,0:T(8,128)(2,1)} fusion(bf16[512,16384]{1,0:T(8,128)(2,1)} %get-tuple-element.15, bf16[2,512,256]{2,1,0:T(8,128)(2,1)S(1)} %all_gather.7), kind=kOutput, calls=%fused_computation.13 | convolution fusion | flops 4299161600 | bytes 25427968 | tf_op jit(solution)/shard_map/dot_general | solution.py:95
  192.0 0.0 reduce-scatter.5.cloned.1.call-update
  192.0 0.6 multiply_reduce_fusion.2
  192.6 38.5 %psum.23 = f32[]{:T(128)} all-reduce(f32[]{:T(128)} %multiply_reduce_fusion.2), channel_id=1, replica_groups=mesh['dp'=4,'proto'=8] {'dp','proto'}, use_global_device_ids=true, to_apply=%region_16.0 | all-reduce | flops 1 | bytes 8 | tf_op jit(solution)/shard_map/psum | solution.py:102
  231.8 0.0 reduce-scatter.3.cloned.1.call-done
  231.8 0.9 fusion.22
  232.7 0.0 copy-start.1
  232.7 1.5 fusion.16
  234.2 62.4 %reduce-scatter.5.cloned.1.call-done = bf16[64,16384]{1,0:T(8,128)(2,1)} async-done(((bf16[256,16384]{1,0:T(8,128)(2,1)}), bf16[64,16384]{1,0:T(8,128)(2,1)}) %reduce-scatter.5.cloned.1.call-update) | async-done | bytes 2097168 | tf_op jit(solution)/shard_map/reduce_scatter | solution.py:94
  296.5 13.1 %multiply_add_fusion = (f32[64,16384]{1,0:T(8,128)}, f32[64,16384]{1,0:T(8,128)}, f32[64,16384]{1,0:T(8,128)}, f32[64,16384]{1,0:T(8,128)}) fusion(f32[256,16384]{1,0:T(8,128)} %param.14, s32[]{:T(128)S(6)} %select_n.17, f32[256,16384]{1,0:T(8,128)} %param.13, bf16[64,16384]{1,0:T(8,128)(2,1)} %reduce-scatter.5.cloned.1.call-done, f32[64,16384]{1,0:T(8,128)} %param.15, ...), kind=kLoop, calls=%fused_computation.20 | loop fusion | flops 19922944 | bytes 35651588 | tf_op jit(solution)/shard_map/add | solution.py:110
  309.6 0.0 copy-done.1
  (7 shorter events, 0.0 us)
Async XLA Ops:
  7.2 15.2 %copy-start = (bf16[1,128,256]{2,1,0:T(8,128)(2,1)S(1)}, bf16[1,128,256]{2,1,0:T(8,128)(2,1)}, u32[]{:S(2)}) copy-start(bf16[1,128,256]{2,1,0:T(8,128)(2,1)} %param.9) | copy-start | bytes 196612
  7.2 224.6 %reduce-scatter.3.cloned.1.call-start = ((), (), s32[]{:S(2)}) async-start(), calls=%async_computation.2 | async-start | bytes 294912 | tf_op jit(solution)/shard_map/reduce_scatter | solution.py:76
  39.8 18.9 %copy-start.3 = (f32[16384]{0:T(1024)S(1)}, f32[16384]{0:T(1024)}, u32[]{:S(2)}) copy-start(f32[16384]{0:T(1024)} %param.17) | copy-start | bytes 196612
  92.2 20.2 %copy-start.2 = (f32[512,16384]{1,0:T(8,128)S(1)}, f32[512,16384]{1,0:T(8,128)}, u32[]{:S(2)}) copy-start(f32[512,16384]{1,0:T(8,128)} %get-tuple-element.19) | copy-start | bytes 100663296
  179.2 117.3 %reduce-scatter.5.cloned.1.call-start = ((), (), s32[]{:S(2)}) async-start(), calls=%async_computation.3 | async-start | bytes 10485760 | tf_op jit(solution)/shard_map/reduce_scatter | solution.py:94
  232.7 77.0 %copy-start.1 = (bf16[1,128,256]{2,1,0:T(8,128)(2,1)S(1)}, bf16[1,128,256]{2,1,0:T(8,128)(2,1)}, u32[]{:S(2)}) copy-start(bf16[1,128,256]{2,1,0:T(8,128)(2,1)} %param.9) | copy-start | bytes 196612
Sparse Core Ops, SparseCore 0:
  179.4 28.5 reduce-scatter.2
  211.3 85.1 reduce-scatter.4
where the time goes:
time: 318 us
  blocking collectives  92.2 us (29%)
  other arithmetic  69.8 us (22%)
  matrix products  66.5 us (21%)
  waiting for transfers between devices  62.4 us (20%)
  between operations  16.6 us (5%)
  local copies, waits for them, and re-layouts  10.1 us (3%)
    reduce_scatter x1, waiting for transfers between devices, local(): lax.psum_scatter(lax.dot_general(rows_student, grad_logit, (((0,), (0,)),...  62.4 us
    psum x1, blocking collectives, local(): loss_sum = lax.psum(partial_loss, ('dp', 'proto'))  38.5 us
    reduce_sum x1, other arithmetic, local(): jnp.sum(prob_t * (log_total[:, None] - student_logit), axis=1)  30.7 us
    dot_general x1, matrix products, local(): jnp.dot(rows_teacher, teacher_w, preferred_element_type=jnp.float32)  19.1 us
    dot_general x1, matrix products, local(): jnp.dot(rows_student, student_w, preferred_element_type=jnp.float32)  18.9 us
    dot_general x1, matrix products, local(): lax.dot_general(grad_logit, student_w, (((1,), (1,)), ((), ())), preferre...  15.8 us
    reduce_sum x1, other arithmetic, local(): jnp.sum(exp_t, axis=1)  15.2 us
    all_gather x1, blocking collectives, local(): lax.all_gather(stacked, 'proto', axis=1, tiled=True)  14.8 us
  transfers between devices with their start and end apart: 2, of which 1 were waited for; matrix products, arithmetic and copies ran while one was open for 5% of the time, Pallas kernels for 0%

commit v1 on v0

v1 whole, which is shorter than its diff:
```python
import functools

import jax
import jax.numpy as jnp
from jax import lax
from jax.experimental import pallas as pl
from jax.experimental.pallas import tpu as pltpu
from jax.sharding import PartitionSpec as P

PATCH_IMG = 256

student_temp = 0.1
teacher_temp = 0.07
beta_one = 0.9
beta_two = 0.999
fix_one = 0.9999734386011124
fix_two = 0.09520785288629038
learn_rate = 0.002
decay_rate = 0.04
teacher_keep = 0.994

log2_e = 1.4426950408889634
ln_2 = 0.6931471805599453
scale_s = log2_e / student_temp
scale_t = log2_e / teacher_temp

f32 = jnp.float32
bf16 = jnp.bfloat16
PAD = 16
VMEM_LIMIT = 56 << 20
CHUNKS = 2


def params(**more):
    return pltpu.CompilerParams(vmem_limit_bytes=VMEM_LIMIT, **more)


def whole(shape):
    return pl.BlockSpec(shape, lambda *_: (0,) * len(shape))


def xor_pairs(size, k):
    return [(i, i ^ k) for i in range(size)]


def pick_kernel(rows_ref, image_ref, student_ref, teacher_ref, pack_ref, raw_ref, inv_ref):
    patches, width = student_ref.shape
    count = rows_ref.shape[1]
    hot = lax.broadcasted_iota(jnp.int32, (patches, count), 0) == rows_ref[...]
    hot = jnp.where(hot, 1.0, 0.0).astype(bf16)

    def pick(table):
        return lax.dot_general(hot, table, (((0,), (0,)), ((), ())), preferred_element_type=f32)

    def unit(raw):
        inverse = lax.rsqrt(jnp.sum(raw * raw, axis=-1, keepdims=True) + 1e-06)
        return raw * inverse, inverse

    raw_s = pick(student_ref[...])
    unit_s, inv_s = unit(raw_s)
    unit_t, _ = unit(pick(teacher_ref[...]))
    raw_ref[...] = raw_s
    inv_ref[...] = jnp.broadcast_to(inv_s, inv_ref.shape)
    pack_ref[0:count, :] = unit_s.astype(bf16)
    pack_ref[count : 2 * count, :] = unit_t.astype(bf16)
    images = jnp.broadcast_to(image_ref[...].astype(f32), (PAD, patches)).astype(bf16)
    ids = jnp.dot(images, hot, preferred_element_type=f32)
    pack_ref[2 * count :, :] = jnp.zeros((PAD, width), bf16)
    pack_ref[2 * count :, 0:count] = ids.astype(bf16)


def pick_rows(rows, image, student, teacher):
    patches, width = student.shape
    count = rows.shape[1]
    return pl.pallas_call(
        pick_kernel,
        out_shape=[
            jax.ShapeDtypeStruct((2 * count + PAD, width), bf16),
            jax.ShapeDtypeStruct((count, width), f32),
            jax.ShapeDtypeStruct((count, 128), f32),
        ],
        compiler_params=params(),
        name="pick_rows",
    )(rows, image, student, teacher)


def first_kernel(own_ref, other_ref, ws_ref, wt_ref, centre_ref, out_ref, us, ut, ms, ss, mt, st, *, count):
    step = pl.program_id(0)
    pack = 2 * count + PAD
    rows = us.shape[0]
    half = rows // 2
    cols = ws_ref.shape[1]

    @pl.when(step == 0)
    def _():
        for c, ref in enumerate((own_ref, other_ref)):
            for z in range(half // count):
                at = c * half + z * count
                us[at : at + count, :] = ref[z * pack : z * pack + count, :]
                ut[at : at + count, :] = ref[z * pack + count : z * pack + 2 * count, :]
        for m, s in ((ms, ss), (mt, st)):
            m[...] = jnp.full_like(m, -jnp.inf)
            s[...] = jnp.zeros_like(s)

    def update(parts, m_ref, s_ref, at):
        old = m_ref[at, :]
        new = functools.reduce(jnp.maximum, parts, old)
        total = functools.reduce(jnp.add, [jnp.exp2(part - new) for part in parts])
        s_ref[at, :] = s_ref[at, :] * jnp.exp2(old - new) + total
        m_ref[at, :] = new

    block = min(rows, 512)
    tile = min(cols, 1024)
    for t in range(cols // tile):
        span = slice(t * tile, (t + 1) * tile)
        ws = ws_ref[:, span].astype(bf16)
        wt = wt_ref[:, span].astype(bf16)
        shift = centre_ref[:, span] * scale_t
        for r in range(rows // block):
            at = slice(r * block, (r + 1) * block)
            zs = jnp.dot(us[at, :], ws, preferred_element_type=f32)
            update([zs[:, i : i + 128] * scale_s for i in range(0, tile, 128)], ms, ss, at)
            zt = jnp.dot(ut[at, :], wt, preferred_element_type=f32)
            update([zt[:, i : i + 128] * scale_t - shift[:, i : i + 128] for i in range(0, tile, 128)], mt, st, at)

    @pl.when(step == pl.num_programs(0) - 1)
    def _():
        out_ref[...] = jnp.zeros_like(out_ref)
        for k, (m, s) in enumerate(((ms, ss), (mt, st))):
            lanes = m[...]
            peak = jnp.max(lanes, axis=1, keepdims=True)
            total = jnp.sum(s[...] * jnp.exp2(lanes - peak), axis=1, keepdims=True)
            lse = jnp.broadcast_to(peak + jnp.log2(total), lanes.shape)
            out_ref[k : k + 1, :] = jnp.transpose(lse)[0:1, :]


def first_pass(own, other, ws, wt, centre, count):
    width, cols = ws.shape
    rows = 2 * own.shape[0] // (2 * count + PAD) * count
    tile = min(cols, 2048)
    return pl.pallas_call(
        functools.partial(first_kernel, count=count),
        grid=(cols // tile,),
        in_specs=[
            whole(own.shape),
            whole(other.shape),
            pl.BlockSpec((width, tile), lambda j: (0, j)),
            pl.BlockSpec((width, tile), lambda j: (0, j)),
            pl.BlockSpec((1, tile), lambda j: (0, j)),
        ],
        out_specs=whole((8, rows)),
        out_shape=jax.ShapeDtypeStruct((8, rows), f32),
        scratch_shapes=[pltpu.VMEM((rows, width), bf16)] * 2 + [pltpu.VMEM((rows, 128), f32)] * 4,
        compiler_params=params(),
        cost_estimate=pl.CostEstimate(flops=4 * rows * width * cols, bytes_accessed=8 * width * cols, transcendentals=2 * rows * cols),
        name="first_pass",
    )(own, other, ws, wt, centre)


def join(parts):
    peak = functools.reduce(jnp.maximum, parts)
    total = functools.reduce(jnp.add, [jnp.exp2(part - peak) for part in parts])
    return peak + jnp.log2(total)


def swap_blocks(x, k, size):
    n = x.shape[1] // size
    return jnp.concatenate([x[:, (j ^ k) * size : ((j ^ k) + 1) * size] for j in range(n)], axis=1)


def core_join_kernel(own_ref, other_ref, out_ref):
    half = own_ref.shape[1] // 2
    out_ref[...] = join([own_ref[...], swap_blocks(other_ref[...], 1, half)])


def final_join_kernel(*refs, count, images, ratio):
    stats, (own_ref, other_ref), (out_ref, loss_ref) = refs[:-4], refs[-4:-2], refs[-2:]
    rows = stats[0].shape[1]
    pack = 2 * count + PAD
    lse = join([swap_blocks(ref[...], k, count) for k, ref in enumerate(stats)])
    ids = jnp.concatenate(
        [
            ref[z * pack + 2 * count : (z + 1) * pack, 0:count].astype(f32)[0:8, :]
            for ref in (own_ref, other_ref)
            for z in range(rows // (2 * count))
        ],
        axis=1,
    )
    per_row = jnp.zeros_like(ids)
    for label in range(images):
        match = jnp.where(ids == label, 1.0, 0.0)
        per_row += match * jnp.sum(match, axis=1, keepdims=True)
    weight = ratio / per_row
    out_ref[...] = lse - jnp.log2(weight / student_temp)
    own = jnp.sum(weight[0:1, 0:count] * lse[0:1, 0:count] * ln_2, axis=1, keepdims=True)
    loss_ref[...] = jnp.broadcast_to(own, loss_ref.shape)


def lay_kernel(slab_ref, *refs, count, groups):
    packs, us, ut, flipped, turned = refs[: 2 * groups], refs[-4], refs[-3], refs[-2], refs[-1]
    pack = 2 * count + PAD
    zs = packs[0].shape[0] // pack
    at = 0
    for g in range(groups):
        for c in range(2):
            ref = packs[2 * g + c]
            for z in range(zs):
                us[at : at + count, :] = ref[z * pack : z * pack + count, :]
                ut[at : at + count, :] = ref[z * pack + count : z * pack + 2 * count, :]
                at += count
    width = us.shape[1]
    turned[...] = jnp.transpose(us[...])
    slab = width // groups
    for k in range(groups):
        start = pl.multiple_of((slab_ref[0] ^ k) * slab, slab)
        flipped[k * slab : (k + 1) * slab, :] = turned[pl.ds(start, slab), :]


def lay_rows(slab, packs, count):
    groups = len(packs) // 2
    width = packs[0].shape[1]
    rows = 2 * groups * (packs[0].shape[0] // (2 * count + PAD)) * count
    return pl.pallas_call(
        functools.partial(lay_kernel, count=count, groups=groups),
        in_specs=[pl.BlockSpec(memory_space=pltpu.SMEM)] + [pl.BlockSpec(memory_space=pltpu.VMEM)] * len(packs),
        out_shape=[jax.ShapeDtypeStruct((rows, width), bf16)] * 2 + [jax.ShapeDtypeStruct((width, rows), bf16)],
        scratch_shapes=[pltpu.VMEM((width, rows), bf16)],
        compiler_params=params(),
        name="lay_rows",
    )(slab, *packs)


def second_kernel(place_ref, us, ut, flipped, ws_ref, wt_ref, centre_ref, *refs, groups, first, last, count):
    stats = refs[:groups]
    refs = refs[groups:]
    if first:
        carry_ref = seed_ref = None
    else:
        carry_ref, seed_ref = refs[:2]
        refs = refs[2:]
    grads, refs = refs[:groups], refs[groups:]
    if last:
        keep_ref, send_ref, loss_ref, total, loss_sum, shift_s, shift_t = refs
    else:
        total, loss_ref, loss_sum, shift_s, shift_t = refs
    step = pl.program_id(0)
    rows, width = us.shape
    group_rows = rows // groups
    tile = ws_ref.shape[1]

    @pl.when(step == 0)
    def _():
        total[...] = jnp.zeros_like(total) if first else carry_ref[...]
        loss_sum[...] = jnp.zeros_like(loss_sum)
        for g in range(groups):
            at = slice(g * group_rows, (g + 1) * group_rows)
            for k, shift in enumerate((shift_s, shift_t)):
                line = jnp.broadcast_to(stats[g][k : k + 1, :], (128, group_rows))
                shift[at, :] = jnp.transpose(line)

    ws = ws_ref[...].astype(bf16)
    wt = wt_ref[...].astype(bf16)
    centre = centre_ref[...] * scale_t
    block = min(group_rows, 512)
    grad = None
    for r in range(rows // block):
        at = slice(r * block, (r + 1) * block)
        zs = jnp.dot(us[at, :], ws, preferred_element_type=f32)
        zt = jnp.dot(ut[at, :], wt, preferred_element_type=f32)
        as_, at_ = shift_s[at, :], shift_t[at, :]
        parts = []
        loss = None
        for i in range(0, tile, 128):
            zsi = zs[:, i : i + 128]
            ps = jnp.exp2(zsi * scale_s - as_)
            pt = jnp.exp2(zt[:, i : i + 128] * scale_t - centre[:, i : i + 128] - at_)
            cross = pt * zsi
            loss = cross if loss is None else loss + cross
            parts.append((ps - pt).astype(bf16))
        loss_sum[...] += jnp.sum(loss.reshape(block // 8, 8, 128), axis=0)
        logit = jnp.concatenate(parts, axis=1)
        total[at, :] += lax.dot_general(logit, ws, (((1,), (1,)), ((), ())), preferred_element_type=f32)
        part = jnp.dot(flipped[:, at], logit, preferred_element_type=f32)
        grad = part if grad is None else grad + part
    slab = width // groups
    for k in range(groups):
        grads[k][...] = grad[k * slab : (k + 1) * slab, :].astype(bf16)

    @pl.when(step == pl.num_programs(0) - 1)
    def _():
        done = jnp.sum(jnp.sum(loss_sum[...], axis=1, keepdims=True), axis=0, keepdims=True)
        loss = jnp.broadcast_to(done, loss_ref.shape)
        if not first:
            loss += seed_ref[...]
        loss_ref[...] = loss
        if last:
            zs_count = group_rows // (2 * count)
            for g in range(groups):
                for c, ref in enumerate((keep_ref, send_ref)):
                    for z in range(zs_count):
                        src = g * group_rows + (c * zs_count + z) * count
                        dst = (z * groups + g) * count
                        ref[dst : dst + count, :] = total[src : src + count, :].astype(ref.dtype)


def second_pass(place, us, ut, flipped, ws, wt, centre, stats, carry, index, chunks, share, count):
    rows, width = us.shape
    groups = len(stats)
    slab = width // groups
    chunk = share // chunks
    tile = min(chunk, 512)
    steps = chunk // tile
    first, last = index == 0, index == chunks - 1
    column = lambda j, place_ref: (0, place_ref[0] * (share // tile) + index * steps + j)
    in_specs = [whole(us.shape), whole(ut.shape), whole(flipped.shape)]
    in_specs += [pl.BlockSpec((width, tile), column)] * 2 + [pl.BlockSpec((1, tile), column)]
    in_specs += [whole(stats[0].shape)] * groups
    args = [us, ut, flipped, ws, wt, centre, *stats]
    if not first:
        in_specs += [whole(carry[0].shape), whole(carry[1].shape)]
        args += list(carry)
    out_specs = [pl.BlockSpec((slab, tile), lambda j, place_ref: (0, j))] * groups
    out_shape = [jax.ShapeDtypeStruct((slab, chunk), bf16)] * groups
    scratch = [pltpu.VMEM((8, 128), f32)] + [pltpu.VMEM((rows, 128), f32)] * 2
    if last:
        out_specs += [whole((rows // 2, width))] * 2
        out_shape += [jax.ShapeDtypeStruct((rows // 2, width), f32), jax.ShapeDtypeStruct((rows // 2, width), bf16)]
        scratch = [pltpu.VMEM((rows, width), f32)] + scratch
    else:
        out_specs += [whole((rows, width))]
        out_shape += [jax.ShapeDtypeStruct((rows, width), f32)]
    out_specs += [whole((8, 128))]
    out_shape += [jax.ShapeDtypeStruct((8, 128), f32)]
    return pl.pallas_call(
        functools.partial(second_kernel, groups=groups, first=first, last=last, count=count),
        grid_spec=pltpu.PrefetchScalarGridSpec(
            num_scalar_prefetch=1, grid=(steps,), in_specs=in_specs, out_specs=out_specs, scratch_shapes=scratch
        ),
        out_shape=out_shape,
        compiler_params=params(),
        cost_estimate=pl.CostEstimate(flops=8 * rows * width * chunk, bytes_accessed=8 * width * chunk, transcendentals=2 * rows * chunk),
        name="second_pass",
    )(place, *args)


def pieces(value):
    rows = lax.broadcasted_iota(jnp.int32, (PAD, 256), 0)
    out = jnp.zeros((PAD, 256), f32)
    for k in range(3):
        piece = value.astype(bf16).astype(f32)
        out = jnp.where(rows == k, piece, out)
        value = value - piece
    return out.astype(bf16)


def joined(block):
    return jnp.sum(block[:, 0:1].astype(f32), axis=0, keepdims=True)


def core_sum_kernel(keep_ref, got_ref, loss_ref, other_ref, *outs, blocks):
    size = keep_ref.shape[0] // blocks
    loss = loss_ref[0:1, 0:1] + other_ref[0:1, 0:1]
    for k in range(blocks):
        at = slice(k * size, (k + 1) * size)
        outs[k][0:size, :] = (keep_ref[at, :] + got_ref[at, :].astype(f32)).astype(outs[k].dtype)
        if k:
            outs[k][size:, :] = pieces(loss)
    outs[-1][...] = jnp.broadcast_to(loss, outs[-1].shape)


def core_sum(keep, got, loss, other, blocks):
    rows, width = keep.shape
    size = rows // blocks
    return pl.pallas_call(
        functools.partial(core_sum_kernel, blocks=blocks),
        out_shape=[jax.ShapeDtypeStruct((size, width), f32)]
        + [jax.ShapeDtypeStruct((size + PAD, width), bf16)] * (blocks - 1)
        + [jax.ShapeDtypeStruct((8, 128), f32)],
        compiler_params=params(),
        name="core_sum",
    )(keep, got, loss, other)


def axis_sum_kernel(keep_ref, loss_ref, *refs, blocks, sources):
    got, outs = refs[:sources], refs[sources:]
    rows = keep_ref.shape[0]
    size = rows // blocks
    loss = loss_ref[0:1, 0:1]
    for ref in got:
        loss = loss + joined(ref[rows:, :])
    for k in range(blocks):
        at = slice(k * size, (k + 1) * size)
        total = keep_ref[at, :]
        for ref in got:
            total = total + ref[at, :].astype(f32)
        outs[k][0:size, :] = total.astype(outs[k].dtype)
        if k:
            outs[k][size:, :] = pieces(loss)
    outs[-1][...] = jnp.broadcast_to(loss, outs[-1].shape)


def axis_sum(keep, loss, got, blocks):
    rows, width = keep.shape
    size = rows // blocks
    return pl.pallas_call(
        functools.partial(axis_sum_kernel, blocks=blocks, sources=len(got)),
        out_shape=[jax.ShapeDtypeStruct((size, width), f32)]
        + [jax.ShapeDtypeStruct((size + PAD, width), bf16)] * (blocks - 1)
        + [jax.ShapeDtypeStruct((8, 128), f32)],
        compiler_params=params(),
        name="axis_sum",
    )(keep, loss, *got)


def row_kernel(keep_ref, loss_ref, raw_ref, inv_ref, *refs, sources, rows_total):
    got, (out_ref, total_ref) = refs[:sources], refs[sources:]
    rows = keep_ref.shape[0]
    loss = loss_ref[0:1, 0:1]
    grad = keep_ref[...]
    for ref in got:
        loss = loss + joined(ref[rows:, :])
        grad = grad + ref[0:rows, :].astype(f32)
    raw = raw_ref[...]
    inv = inv_ref[:, 0:1]
    out_ref[...] = inv * grad - inv * inv * inv * raw * jnp.sum(raw * grad, axis=-1, keepdims=True)
    total_ref[...] = jnp.broadcast_to(loss / rows_total, total_ref.shape)


def step_kernel(place_ref, *refs, groups):
    grads = refs[:groups]
    student_ref, teacher_ref, first_ref, second_ref = refs[groups : groups + 4]
    out_student, out_first, out_second, out_teacher = refs[-4:]
    source = pl.program_id(0)
    for k in range(groups):

        @pl.when(source == k)
        def _(k=k):
            grad = grads[k][...].astype(f32)
            first = beta_one * first_ref[...] + (1.0 - beta_one) * grad
            second = beta_two * second_ref[...] + (1.0 - beta_two) * grad * grad
            step = first / fix_one / (jnp.sqrt(second / fix_two) + 1e-08)
            student = student_ref[...]
            student = student - learn_rate * (step + decay_rate * student)
            out_student[...] = student
            out_first[...] = first
            out_second[...] = second
            out_teacher[...] = teacher_keep * teacher_ref[...] + (1.0 - teacher_keep) * student


def optimizer(place, grads, student, teacher, first, second, done, index, chunks, share):
    groups = len(grads)
    slab, total = first.shape
    chunk = share // chunks
    tile = min(chunk, 2048)
    steps = chunk // tile
    column = lambda k, j, place_ref: (place_ref[0] ^ k) * (share // tile) + index * steps + j
    sliced = pl.BlockSpec((slab, tile), lambda k, j, place_ref: (place_ref[0], column(k, j, place_ref)))
    local = pl.BlockSpec((slab, tile), lambda k, j, place_ref: (0, column(k, j, place_ref)))
    grad_specs = [
        pl.BlockSpec((slab, tile), lambda k, j, place_ref, g=g: (0, jnp.where(k == g, j, jnp.where(k < g, 0, steps - 1))))
        for g in range(groups)
    ]
    in_specs = grad_specs + [sliced, sliced, local, local]
    args = [*grads, student, teacher, first, second]
    aliases = {}
    if done is not None:
        aliases = {1 + len(args) + i: i for i in range(4)}
        in_specs += [pl.BlockSpec(memory_space=pl.ANY)] * 4
        args += list(done)
    return pl.pallas_call(
        functools.partial(step_kernel, groups=groups),
        grid_spec=pltpu.PrefetchScalarGridSpec(
            num_scalar_prefetch=1, grid=(groups, steps), in_specs=in_specs, out_specs=[local] * 4
        ),
        out_shape=[jax.ShapeDtypeStruct((slab, total), f32)] * 4,
        input_output_aliases=aliases,
        compiler_params=params(),
        cost_estimate=pl.CostEstimate(flops=20 * slab * groups * chunk, bytes_accessed=34 * slab * groups * chunk, transcendentals=0),
        name="optimizer",
    )(place, *args)


def local(
    student_patch,
    teacher_patch,
    patch_image,
    masked_rows,
    student_proto,
    teacher_proto,
    first_moment,
    second_moment,
    centre,
):
    count = masked_rows.shape[1]
    patches, width = student_patch.shape[1:]
    protos = lax.axis_size("proto")
    groups = lax.axis_size("dp")
    columns = student_proto.shape[1]
    share = columns // groups
    images = patches * protos // PATCH_IMG
    ratio = count * PATCH_IMG / patches
    rows_total = count * protos * groups
    place = lax.axis_index("dp").astype(jnp.int32).reshape(1)
    centre = centre.reshape(1, columns)

    def proto_swap(x, k):
        return lax.ppermute(x, "proto", xor_pairs(protos, k))

    def dp_swap(x, k):
        return lax.ppermute(x, "dp", xor_pairs(groups, k))

    pack, raw, inv = pick_rows(masked_rows, patch_image, student_patch[0], teacher_patch[0])
    own = jnp.concatenate([pack] + [proto_swap(pack, k) for k in range(2, protos, 2)], axis=0)
    other = proto_swap(own, 1)
    far = [dp_swap(own, k) for k in range(1, groups)]

    stats = first_pass(own, other, student_proto, teacher_proto, centre, count)
    far_other = [proto_swap(x, 1) for x in far]
    packs = [own, other]
    for pair in zip(far, far_other):
        packs += list(pair)
    us, ut, flipped = lay_rows(place, packs, count)

    rows = stats.shape[1]
    stats = pl.pallas_call(
        core_join_kernel, out_shape=jax.ShapeDtypeStruct(stats.shape, f32), compiler_params=params(), name="core_join"
    )(stats, proto_swap(stats, 1))
    stats, loss_own = pl.pallas_call(
        functools.partial(final_join_kernel, count=count, images=images, ratio=ratio),
        out_shape=[jax.ShapeDtypeStruct(stats.shape, f32), jax.ShapeDtypeStruct((8, 128), f32)],
        compiler_params=params(),
        name="final_join",
    )(stats, *[proto_swap(stats, k) for k in range(2, protos, 2)], own, other)
    all_stats = [stats] + [dp_swap(stats, k) for k in range(1, groups)]

    carry = None
    sent = []
    for index in range(CHUNKS):
        out = second_pass(
            place, us, ut, flipped, student_proto, teacher_proto, centre, all_stats, carry, index, CHUNKS, share, count
        )
        grads, carry = out[:groups], out[groups:]
        sent.append([grads[0]] + [dp_swap(grads[k], k) for k in range(1, groups)])
    keep, send, cross = carry
    loss = loss_own - cross

    zs_count = protos // 2
    out = core_sum(keep, proto_swap(send, 1), loss, proto_swap(loss, 1), zs_count)
    out = axis_sum(out[0], out[-1], [proto_swap(out[k], 2 * k) for k in range(1, zs_count)], groups)
    got = [dp_swap(out[k], k) for k in range(1, groups)]
    row_grad, total = pl.pallas_call(
        functools.partial(row_kernel, sources=len(got), rows_total=rows_total),
        out_shape=[jax.ShapeDtypeStruct((count, width), f32), jax.ShapeDtypeStruct((8, 128), f32)],
        compiler_params=params(),
        name="row_grad",
    )(out[0], out[-1], raw, inv, *got)

    done = None
    for index in range(CHUNKS):
        done = optimizer(
            place, sent[index], student_proto, teacher_proto, first_moment, second_moment, done, index, CHUNKS, share
        )
    new_student, new_first, new_second, new_teacher = done
    return (row_grad[None], new_student, new_first, new_second, new_teacher, total[0, 0])


def solution(mesh):
    in_specs = (
        P("dp", "proto", None),
        P("dp", "proto", None),
        P("dp", "proto"),
        P("dp", "proto"),
        P(None, "proto"),
        P(None, "proto"),
        P("dp", "proto"),
        P("dp", "proto"),
        P("proto"),
    )
    out_specs = (
        P("dp", "proto", None),
        P("dp", "proto"),
        P("dp", "proto"),
        P("dp", "proto"),
        P("dp", "proto"),
        P(),
    )
    return jax.shard_map(local, mesh=mesh, in_specs=in_specs, out_specs=out_specs, check_vma=False)
```

time: 318 us -> 165 us (0.52)
  blocking collectives: 92.2 us -> 0 us
  Pallas kernels: 0 us -> 85.9 us
  other arithmetic: 69.8 us -> 0.67 us
  matrix products: 66.5 us -> 0 us
  starting transfers between devices: 0.08 us -> 33.3 us
  waiting for transfers between devices: 62.4 us -> 35.4 us
  between operations: 16.6 us -> 0.91 us
    pallas_call x0 -> x12, Pallas kernels: none -> 85.9 us  [the longest x2 32.8 us: second_pass(): pl.pallas_call(functools.partial(second_kernel, groups=groups, first=firs...]
    dot_general x5 -> x0, matrix products: 66.5 us -> none  [the longest x1 19.1 us: local(): jnp.dot(rows_teacher, teacher_w, preferred_element_type=jnp.float32)]
    reduce_scatter x2 -> x0, waiting for transfers between devices: 62.4 us -> none  [the longest x1 62.4 us: local(): lax.psum_scatter(lax.dot_general(rows_student, grad_logit, (((0,), (0,)),...]
    reduce_sum x8 -> x0, other arithmetic: 54.3 us -> none  [the longest x1 30.7 us: local(): jnp.sum(prob_t * (log_total[:, None] - student_logit), axis=1)]
    psum x2 -> x0, blocking collectives: 52.3 us -> none  [the longest x1 38.5 us: local(): loss_sum = lax.psum(partial_loss, ('dp', 'proto'))]
    ppermute x0 -> x31, waiting for transfers between devices: none -> 35.4 us  [the longest x16 20.6 us: proto_swap(): return lax.ppermute(x, 'proto', xor_pairs(protos, k))]
    ppermute x0 -> x31, starting transfers between devices: none -> 33.3 us  [the longest x15 20.7 us: dp_swap(): return lax.ppermute(x, 'dp', xor_pairs(groups, k))]
    all_gather x1 -> x0, blocking collectives: 14.8 us -> none  [local(): lax.all_gather(stacked, 'proto', axis=1, tiled=True)]
  transfers between devices with their start and end apart: 2 -> 31, of which waited for: 1 -> 13; matrix products, arithmetic and copies ran while one was open for 5% -> 1% of each run, Pallas kernels for 0% -> 30%
where the time goes in v1:
time: 165 us; the launch traced here: 164 us
  Pallas kernels  85.9 us (52%)
  waiting for transfers between devices  35.4 us (21%)
  starting transfers between devices  33.3 us (20%)
  local copies, waits for them, and re-layouts  7.91 us (5%)
    pallas_call x2, Pallas kernels, second_pass(): pl.pallas_call(functools.partial(second_kernel, groups=groups, first=firs...  32.8 us
    pallas_call x1, Pallas kernels, first_pass(): pl.pallas_call(functools.partial(first_kernel, count=count), grid=(cols /...  22.8 us
    ppermute x15, starting transfers between devices, dp_swap(): return lax.ppermute(x, 'dp', xor_pairs(groups, k))  20.7 us
    ppermute x16, waiting for transfers between devices, proto_swap(): return lax.ppermute(x, 'proto', xor_pairs(protos, k))  20.6 us
    pallas_call x2, Pallas kernels, optimizer(): pl.pallas_call(functools.partial(step_kernel, groups=groups), grid_spec=p...  15.9 us
    ppermute x15, waiting for transfers between devices, dp_swap(): return lax.ppermute(x, 'dp', xor_pairs(groups, k))  14.8 us
    ppermute x16, starting transfers between devices, proto_swap(): return lax.ppermute(x, 'proto', xor_pairs(protos, k))  12.7 us
    unnamed x71, local copies, waits for them, and re-layouts  6.73 us
  transfers between devices with their start and end apart: 31, of which 13 were waited for; matrix products, arithmetic and copies ran while one was open for 1% of the time, Pallas kernels for 30%

profile of v1, /device:TPU:0, one launch (start us, length us, event | category | flops | bytes accessed | tf_op | source)
XLA Modules:
  0.0 164.0 jit_solution(1357826977773036375)
XLA Ops:
  0.6 1.8 %pick_rows.1 = (bf16[144,256]{1,0:T(8,128)(2,1)}, f32[64,256]{1,0:T(8,128)}, f32[64,128]{1,0:T(8,128)}) custom-call(s32[1,64]{1,0:T(1,128)} %rows_ref.1, s32[1,128]{1,0:T(1,128)} %image_ref.1, bf16[128,256]{1,0:T(8,128)(2,1)} %bitcast.9, bf16[128,256]{1,0:T(8,128)(2,1)} %bitcast.10), custom_call_target="tpu_custom_call" | custom-call | tf_op jit(solution)/shard_map/pick_rows/pallas_call | solution.py:75
  2.5 5.0 %collective-permute-start.2 = (bf16[144,256]{1,0:T(8,128)(2,1)}, bf16[144,256]{1,0:T(8,128)(2,1)S(1)}, u32[]{:S(2)}, u32[]{:S(2)}) collective-permute-start(bf16[144,256]{1,0:T(8,128)(2,1)} %get-tuple-element.47), channel_id=1, source_target_pairs={{0,6},{1,7},{2,4},{3,5},{4,2},{5,3},{6,0},{7,1},{8,14},{9,15},{10,... | collective-permute-start | bytes 221192 | tf_op jit(solution)/shard_map/ppermute | solution.py:507
  7.5 0.6 collective-permute-start
  8.1 0.9 constant_dynamic-update-slice_fusion.3
  9.0 3.6 %collective-permute-done = bf16[144,256]{1,0:T(8,128)(2,1)S(1)} collective-permute-done((bf16[144,256]{1,0:T(8,128)(2,1)}, bf16[144,256]{1,0:T(8,128)(2,1)S(1)}, u32[]{:S(2)}, u32[]{:S(2)}) %collective-permute-start) | collective-permute-done | bytes 73760 | tf_op jit(solution)/shard_map/ppermute | solution.py:507
  12.6 1.4 collective-permute-done.1
  14.0 2.5 %collective-permute-start.8 = (bf16[576,256]{1,0:T(8,128)(2,1)S(1)}, bf16[576,256]{1,0:T(8,128)(2,1)S(1)}, u32[]{:S(2)}, u32[]{:S(2)}) collective-permute-start(bf16[576,256]{1,0:T(8,128)(2,1)S(1)} %constant_dynamic-update-slice_fusion.refs_0_.own_ref.refs_4_), channel_id=1, source_target_pairs={{0,24},{8,16},{16,8},{24,0},{1,25},{9,17},{17,9},{25,1},{2,26},{10... | collective-permute-start | bytes 884744 | tf_op jit(solution)/shard_map/ppermute | solution.py:510
  16.5 0.5 collective-permute-start.6
  17.0 0.5 collective-permute-start.4
  17.5 7.4 %collective-permute-done.8.refs_6_ = bf16[576,256]{1,0:T(8,128)(2,1)S(1)} collective-permute-done((bf16[576,256]{1,0:T(8,128)(2,1)S(1)}, bf16[576,256]{1,0:T(8,128)(2,1)S(1)}, u32[]{:S(2)}, u32[]{:S(2)}) %collective-permute-start.8) | collective-permute-done | bytes 294944 | tf_op jit(solution)/shard_map/ppermute | solution.py:510
  24.9 4.7 %collective-permute-done.6.refs_4_ = bf16[576,256]{1,0:T(8,128)(2,1)S(1)} collective-permute-done((bf16[576,256]{1,0:T(8,128)(2,1)S(1)}, bf16[576,256]{1,0:T(8,128)(2,1)S(1)}, u32[]{:S(2)}, u32[]{:S(2)}) %collective-permute-start.6) | collective-permute-done | bytes 294944 | tf_op jit(solution)/shard_map/ppermute | solution.py:510
  29.7 0.3 collective-permute-done.4.refs_2_
  29.9 0.2 collective-permute-start.5
  30.2 0.7 copy-done.1
  30.9 22.8 %first_pass.1.own_ref = f32[8,512]{1,0:T(8,128)} custom-call(bf16[576,256]{1,0:T(8,128)(2,1)} %copy-done, bf16[576,256]{1,0:T(8,128)(2,1)} %copy-done.1, f32[256,16384]{1,0:T(8,128)} %refs_4_.3, f32[256,16384]{1,0:T(8,128)} %refs_5_.3, f32[1,16384]{1,0:T(1,128)} %bitcast.6), custom_call_target="tpu_custom_call" | custom-call | flops 8589934592 | bytes 33554432 | tf_op jit(solution)/shard_map/first_pass/pallas_call | solution.py:141
  53.7 0.4 collective-permute-start.10
  54.1 1.1 collective-permute-done.10.other_ref
  55.2 0.6 copy-done.28
  55.8 1.4 core_join.1.refs_0_
  57.1 1.5 collective-permute-start.13
  58.6 0.3 collective-permute-start.12
  58.9 3.9 %collective-permute-done.13.refs_3_ = f32[8,512]{1,0:T(8,128)S(1)} collective-permute-done((f32[8,512]{1,0:T(8,128)}, f32[8,512]{1,0:T(8,128)S(1)}, u32[]{:S(2)}, u32[]{:S(2)}) %collective-permute-start.13) | collective-permute-done | bytes 16416 | tf_op jit(solution)/shard_map/ppermute | solution.py:507
  62.9 0.6 collective-permute-done.12.refs_2_
  63.5 3.3 %collective-permute-done.11.refs_1_ = f32[8,512]{1,0:T(8,128)S(1)} collective-permute-done((f32[8,512]{1,0:T(8,128)}, f32[8,512]{1,0:T(8,128)S(1)}, u32[]{:S(2)}, u32[]{:S(2)}) %collective-permute-start.11) | collective-permute-done | bytes 16416 | tf_op jit(solution)/shard_map/ppermute | solution.py:507
  66.8 0.6 copy-done.27
  67.4 2.0 %final_join.1 = (f32[8,512]{1,0:T(8,128)}, f32[8,128]{1,0:T(8,128)}) custom-call(f32[8,512]{1,0:T(8,128)} %core_join.1.refs_0_, f32[8,512]{1,0:T(8,128)} %copy-done.27, f32[8,512]{1,0:T(8,128)} %copy-done.26, f32[8,512]{1,0:T(8,128)} %copy-done.25, bf16[576,256]{1,0:T(8,128)(2,1)} %copy-done, bf16[576,256]{1,0:T(8,128)(2,1)} %copy-done.1), custom_call_target="tpu_custom_call" | custom-call | tf_op jit(solution)/shard_map/final_join/pallas_call | solution.py:528
  69.4 1.8 %collective-permute-start.16 = (f32[8,512]{1,0:T(8,128)}, f32[8,512]{1,0:T(8,128)S(1)}, u32[]{:S(2)}, u32[]{:S(2)}) collective-permute-start(f32[8,512]{1,0:T(8,128)} %get-tuple-element.51.refs_0_), channel_id=1, source_target_pairs={{0,24},{8,16},{16,8},{24,0},{1,25},{9,17},{17,9},{25,1},{2,26},{10... | collective-permute-start | bytes 49160 | tf_op jit(solution)/shard_map/ppermute | solution.py:510
  71.2 1.3 collective-permute-start.15
  72.6 0.3 collective-permute-start.14
  72.9 0.4 copy-done.6
  73.3 0.3 copy-done.7
  73.7 3.5 %lay_rows.1 = (bf16[2048,256]{1,0:T(8,128)(2,1)}, bf16[2048,256]{1,0:T(8,128)(2,1)}, bf16[256,2048]{1,0:T(8,128)(2,1)}) custom-call(s32[1]{0:T(128)} %bitcast.slab_ref.place_ref, bf16[576,256]{1,0:T(8,128)(2,1)} %copy-done, bf16[576,256]{1,0:T(8,128)(2,1)} %copy-done.1, bf16[576,256]{1,0:T(8,128)(2,1)} %copy-done.5, bf16[576,256]{1,0:T(8,128)(2,1)} %copy-done.8, ...), custom_call_target="tpu_custom_call" | custom-call | tf_op jit(solution)/shard_map/lay_rows/pallas_call | solution.py:223
  77.2 0.6 copy-done.18
  77.8 16.0 %second_pass.2 = (bf16[64,2048]{1,0:T(8,128)(2,1)}, bf16[64,2048]{1,0:T(8,128)(2,1)}, bf16[64,2048]{1,0:T(8,128)(2,1)}, bf16[64,2048]{1,0:T(8,128)(2,1)}, f32[2048,256]{1,0:T(8,128)}, /*index=5*/f32[8,128]{1,0:T(8,128)}) custom-call(s32[1]{0:T(128)} %bitcast.slab_ref.place_ref, bf16[2048,256]{1,0:T(8,128)(2,1)} %get-tuple-element.48.us, ...), custom_call_target="tpu_custom_call" | custom-call | flops 8589934592 | bytes 4194304 | tf_op jit(solution)/shard_map/second_pass/pallas_call | solution.py:334
  93.9 16.8 %second_pass.3 = (bf16[64,2048]{1,0:T(8,128)(2,1)}, bf16[64,2048]{1,0:T(8,128)(2,1)}, bf16[64,2048]{1,0:T(8,128)(2,1)}, bf16[64,2048]{1,0:T(8,128)(2,1)}, f32[10...) custom-call(s32[1]{0:T(128)} %bitcast.slab_ref.place_ref, bf16[2048,256]{1,0:T(8,128)(2,1)} %get-tuple-element.48.us, ...), custom_call_target="tpu_custom_call" | custom-call | flops 8589934592 | bytes 4194304 | tf_op jit(solution)/shard_map/second_pass/pallas_call | solution.py:334
  110.8 1.7 %collective-permute-start.25 = (bf16[64,2048]{1,0:T(8,128)(2,1)}, bf16[64,2048]{1,0:T(8,128)(2,1)S(1)}, u32[]{:S(2)}, u32[]{:S(2)}) collective-permute-start(bf16[64,2048]{1,0:T(8,128)(2,1)} %get-tuple-element.72), channel_id=1, source_target_pairs={{0,8},{8,0},{16,24},{24,16},{1,9},{9,1},{17,25},{25,17},{2,10},{10... | collective-permute-start | bytes 786440 | tf_op jit(solution)/shard_map/ppermute | solution.py:510
  112.5 0.7 sub.3.loss_ref
  113.2 0.2 collective-permute-start.18
  113.4 1.0 collective-permute-done.18.other_ref
  114.4 0.6 copy-done.29
  115.0 0.2 copy-done.2
  115.2 2.3 %core_sum.1 = (f32[256,256]{1,0:T(8,128)}, bf16[272,256]{1,0:T(8,128)(2,1)}, bf16[272,256]{1,0:T(8,128)(2,1)}, bf16[272,256]{1,0:T(8,128)(2,1)}, f32[8,128]{1,0:T(8,128)}) custom-call(f32[1024,256]{1,0:T(8,128)} %get-tuple-element.54.keep_ref, bf16[1024,256]{1,0:T(8,128)(2,1)} %copy-done.2, f32[8,128]{1,0:T(8,128)} %copy-done.24, f32[8,128]{1,0:T(8,128)} %copy-done.29), custom_call_target="tpu_custom_call" | custom-call | tf_op jit(solution)/shard_map/core_sum/pallas_call | solution.py:374
  117.4 1.9 %collective-permute-start.20 = (bf16[272,256]{1,0:T(8,128)(2,1)}, bf16[272,256]{1,0:T(8,128)(2,1)S(1)}, u32[]{:S(2)}, u32[]{:S(2)}) collective-permute-start(bf16[272,256]{1,0:T(8,128)(2,1)} %get-tuple-element.61), channel_id=1, source_target_pairs={{0,4},{1,5},{2,6},{3,7},{4,0},{5,1},{6,2},{7,3},{8,12},{9,13},{10,... | collective-permute-start | bytes 417800 | tf_op jit(solution)/shard_map/ppermute | solution.py:507
  119.3 2.5 %collective-permute-start.21 = (bf16[272,256]{1,0:T(8,128)(2,1)}, bf16[272,256]{1,0:T(8,128)(2,1)S(1)}, u32[]{:S(2)}, u32[]{:S(2)}) collective-permute-start(bf16[272,256]{1,0:T(8,128)(2,1)} %get-tuple-element.62), channel_id=1, source_target_pairs={{0,6},{1,7},{2,4},{3,5},{4,2},{5,3},{6,0},{7,1},{8,14},{9,15},{10,... | collective-permute-start | bytes 417800 | tf_op jit(solution)/shard_map/ppermute | solution.py:507
  121.8 0.3 collective-permute-start.28
  122.2 1.8 %collective-permute-start.29 = (bf16[64,2048]{1,0:T(8,128)(2,1)S(1)}, bf16[64,2048]{1,0:T(8,128)(2,1)S(1)}, u32[]{:S(2)}, u32[]{:S(2)}) collective-permute-start(bf16[64,2048]{1,0:T(8,128)(2,1)S(1)} %copy-done.32), channel_id=1, source_target_pairs={{0,16},{8,24},{16,0},{24,8},{1,17},{9,25},{17,1},{25,9},{2,18},{10... | collective-permute-start | bytes 786440 | tf_op jit(solution)/shard_map/ppermute | solution.py:510
  123.9 1.1 collective-permute-done.19.refs_0_
  125.1 1.5 collective-permute-start.30
  126.6 4.5 %collective-permute-done.20.refs_1_ = bf16[272,256]{1,0:T(8,128)(2,1)S(1)} collective-permute-done((bf16[272,256]{1,0:T(8,128)(2,1)}, bf16[272,256]{1,0:T(8,128)(2,1)S(1)}, u32[]{:S(2)}, u32[]{:S(2)}) %collective-permute-start.20) | collective-permute-done | bytes 139296 | tf_op jit(solution)/shard_map/ppermute | solution.py:507
  131.1 0.7 collective-permute-start.26
  131.8 1.1 collective-permute-start.27
  132.9 1.9 %axis_sum.1 = (f32[64,256]{1,0:T(8,128)}, bf16[80,256]{1,0:T(8,128)(2,1)}, bf16[80,256]{1,0:T(8,128)(2,1)}, bf16[80,256]{1,0:T(8,128)(2,1)}, f32[8,128]{1,0:T(8,128)}) custom-call(f32[256,256]{1,0:T(8,128)} %get-tuple-element.58.keep_ref, f32[8,128]{1,0:T(8,128)} %get-tuple-element.59.loss_ref, bf16[272,256]{1,0:T(8,128)(2,1)} %copy-done.15, ...), custom_call_target="tpu_custom_call" | custom-call | tf_op jit(solution)/shard_map/axis_sum/pallas_call | solution.py:405
  134.7 1.7 %collective-permute-start.22 = (bf16[80,256]{1,0:T(8,128)(2,1)}, bf16[80,256]{1,0:T(8,128)(2,1)S(1)}, u32[]{:S(2)}, u32[]{:S(2)}) collective-permute-start(bf16[80,256]{1,0:T(8,128)(2,1)} %get-tuple-element.67), channel_id=1, source_target_pairs={{0,8},{8,0},{16,24},{24,16},{1,9},{9,1},{17,25},{25,17},{2,10},{10... | collective-permute-start | bytes 122888 | tf_op jit(solution)/shard_map/ppermute | solution.py:510
  136.5 2.4 %collective-permute-done.29.refs_2_ = bf16[64,2048]{1,0:T(8,128)(2,1)S(1)} collective-permute-done((bf16[64,2048]{1,0:T(8,128)(2,1)S(1)}, bf16[64,2048]{1,0:T(8,128)(2,1)S(1)}, u32[]{:S(2)}, u32[]{:S(2)}) %collective-permute-start.29) | collective-permute-done | bytes 262176 | tf_op jit(solution)/shard_map/ppermute | solution.py:510
  138.9 4.2 %collective-permute-start.23 = (bf16[80,256]{1,0:T(8,128)(2,1)}, bf16[80,256]{1,0:T(8,128)(2,1)S(1)}, u32[]{:S(2)}, u32[]{:S(2)}) collective-permute-start(bf16[80,256]{1,0:T(8,128)(2,1)} %get-tuple-element.68), channel_id=1, source_target_pairs={{0,16},{8,24},{16,0},{24,8},{1,17},{9,25},{17,1},{25,9},{2,18},{10... | collective-permute-start | bytes 122888 | tf_op jit(solution)/shard_map/ppermute | solution.py:510
  143.1 0.5 collective-permute-start.24
  143.6 0.2 copy-done.14
  143.8 7.9 %optimizer.2 = (f32[64,16384]{1,0:T(8,128)}, f32[64,16384]{1,0:T(8,128)}, f32[64,16384]{1,0:T(8,128)}, f32[64,16384]{1,0:T(8,128)}) custom-call(s32[1]{0:T(128)} %bitcast.slab_ref.place_ref, bf16[64,2048]{1,0:T(8,128)(2,1)} %get-tuple-element.75.refs_0_, bf16[64,2048]{1,0:T(8,128)(2,1)} %copy-done.10, bf16[64,2048]{1,0:T(8,128)(2,1)} %copy-done.12, ...), custom_call_target="tpu_custom_call" | custom-call | flops 10485760 | bytes 17825792 | tf_op jit(solution)/shard_map/optimizer/pallas_call | solution.py:470
  151.8 0.7 copy-done.11
  152.5 0.1 copy-done.13
  152.6 7.9 %optimizer.3 = (f32[64,16384]{1,0:T(8,128)}, f32[64,16384]{1,0:T(8,128)}, f32[64,16384]{1,0:T(8,128)}, f32[64,16384]{1,0:T(8,128)}) custom-call(s32[1]{0:T(128)} %bitcast.slab_ref.place_ref, bf16[64,2048]{1,0:T(8,128)(2,1)} %get-tuple-element.71.refs_0_, ...), custom_call_target="tpu_custom_call", output_to_operand_aliasing={{0}: (9, {}), {1}: (10, {}), {2}: (11, {}), {3}: (12, {})} | custom-call | flops 10485760 | bytes 17825792 | tf_op jit(solution)/shard_map/optimizer/pallas_call | solution.py:470
  160.6 0.6 copy-done.21
  161.2 1.7 %row_grad.1 = (f32[64,256]{1,0:T(8,128)}, f32[8,128]{1,0:T(8,128)}) custom-call(f32[64,256]{1,0:T(8,128)} %get-tuple-element.63.keep_ref, f32[8,128]{1,0:T(8,128)} %get-tuple-element.64.loss_ref, f32[64,256]{1,0:T(8,128)} %get-tuple-element.65.raw_ref, f32[64,128]{1,0:T(8,128)} %get-tuple-element.66.inv_ref, bf16[80,256]{1,0:T(8,128)(2,1)} %copy-done.21, ...), custom_call_target="tpu_custom_call" | custom-call | tf_op jit(solution)/shard_map/row_grad/pallas_call | solution.py:551
  162.9 1.2 slice.3
  (84 shorter events, 0.4 us)
Async XLA Ops:
  2.5 11.5 %collective-permute-start.2 = (bf16[144,256]{1,0:T(8,128)(2,1)}, bf16[144,256]{1,0:T(8,128)(2,1)S(1)}, u32[]{:S(2)}, u32[]{:S(2)}) collective-permute-start(bf16[144,256]{1,0:T(8,128)(2,1)} %get-tuple-element.47), channel_id=1, source_target_pairs={{0,6},{1,7},{2,4},{3,5},{4,2},{5,3},{6,0},{7,1},{8,14},{9,15},{10,... | collective-permute-start | bytes 221192 | tf_op jit(solution)/shard_map/ppermute | solution.py:507
  7.5 6.4 %collective-permute-start.1 = (bf16[144,256]{1,0:T(8,128)(2,1)}, bf16[144,256]{1,0:T(8,128)(2,1)S(1)}, u32[]{:S(2)}, u32[]{:S(2)}) collective-permute-start(bf16[144,256]{1,0:T(8,128)(2,1)} %get-tuple-element.47), channel_id=1, source_target_pairs={{0,4},{1,5},{2,6},{3,7},{4,0},{5,1},{6,2},{7,3},{8,12},{9,13},{10,... | collective-permute-start | bytes 221192 | tf_op jit(solution)/shard_map/ppermute | solution.py:507
  7.5 5.0 %collective-permute-start = (bf16[144,256]{1,0:T(8,128)(2,1)}, bf16[144,256]{1,0:T(8,128)(2,1)S(1)}, u32[]{:S(2)}, u32[]{:S(2)}) collective-permute-start(bf16[144,256]{1,0:T(8,128)(2,1)} %get-tuple-element.47), channel_id=1, source_target_pairs={{0,2},{1,3},{2,0},{3,1},{4,6},{5,7},{6,4},{7,5},{8,10},{9,11},{10,... | collective-permute-start | bytes 221192 | tf_op jit(solution)/shard_map/ppermute | solution.py:507
  14.0 16.2 %copy-start = (bf16[576,256]{1,0:T(8,128)(2,1)}, bf16[576,256]{1,0:T(8,128)(2,1)S(1)}, u32[]{:S(2)}) copy-start(bf16[576,256]{1,0:T(8,128)(2,1)S(1)} %constant_dynamic-update-slice_fusion.refs_0_.own_ref.refs_4_) | copy-start | bytes 884740
  14.0 11.0 %collective-permute-start.8 = (bf16[576,256]{1,0:T(8,128)(2,1)S(1)}, bf16[576,256]{1,0:T(8,128)(2,1)S(1)}, u32[]{:S(2)}, u32[]{:S(2)}) collective-permute-start(bf16[576,256]{1,0:T(8,128)(2,1)S(1)} %constant_dynamic-update-slice_fusion.refs_0_.own_ref.refs_4_), channel_id=1, source_target_pairs={{0,24},{8,16},{16,8},{24,0},{1,25},{9,17},{17,9},{25,1},{2,26},{10... | collective-permute-start | bytes 884744 | tf_op jit(solution)/shard_map/ppermute | solution.py:510
  16.5 13.1 %collective-permute-start.6 = (bf16[576,256]{1,0:T(8,128)(2,1)S(1)}, bf16[576,256]{1,0:T(8,128)(2,1)S(1)}, u32[]{:S(2)}, u32[]{:S(2)}) collective-permute-start(bf16[576,256]{1,0:T(8,128)(2,1)S(1)} %constant_dynamic-update-slice_fusion.refs_0_.own_ref.refs_4_), channel_id=1, source_target_pairs={{0,16},{8,24},{16,0},{24,8},{1,17},{9,25},{17,1},{25,9},{2,18},{10... | collective-permute-start | bytes 884744 | tf_op jit(solution)/shard_map/ppermute | solution.py:510
  17.0 12.9 %collective-permute-start.4 = (bf16[576,256]{1,0:T(8,128)(2,1)S(1)}, bf16[576,256]{1,0:T(8,128)(2,1)S(1)}, u32[]{:S(2)}, u32[]{:S(2)}) collective-permute-start(bf16[576,256]{1,0:T(8,128)(2,1)S(1)} %constant_dynamic-update-slice_fusion.refs_0_.own_ref.refs_4_), channel_id=1, source_target_pairs={{0,8},{8,0},{16,24},{24,16},{1,9},{9,1},{17,25},{25,17},{2,10},{10... | collective-permute-start | bytes 884744 | tf_op jit(solution)/shard_map/ppermute | solution.py:510
  17.5 12.6 %collective-permute-start.3 = (bf16[576,256]{1,0:T(8,128)(2,1)S(1)}, bf16[576,256]{1,0:T(8,128)(2,1)S(1)}, u32[]{:S(2)}, u32[]{:S(2)}) collective-permute-start(bf16[576,256]{1,0:T(8,128)(2,1)S(1)} %constant_dynamic-update-slice_fusion.refs_0_.own_ref.refs_4_), channel_id=1, source_target_pairs={{0,1},{1,0},{2,3},{3,2},{4,5},{5,4},{6,7},{7,6},{8,9},{9,8},{10,11... | collective-permute-start | bytes 884744 | tf_op jit(solution)/shard_map/ppermute | solution.py:507
  24.9 28.8 %copy-start.3 = (bf16[576,256]{1,0:T(8,128)(2,1)}, bf16[576,256]{1,0:T(8,128)(2,1)S(1)}, u32[]{:S(2)}) copy-start(bf16[576,256]{1,0:T(8,128)(2,1)S(1)} %collective-permute-done.8.refs_6_) | copy-start | bytes 884740
  24.9 47.6 %collective-permute-start.9 = (bf16[576,256]{1,0:T(8,128)(2,1)S(1)}, bf16[576,256]{1,0:T(8,128)(2,1)S(1)}, u32[]{:S(2)}, u32[]{:S(2)}) collective-permute-start(bf16[576,256]{1,0:T(8,128)(2,1)S(1)} %collective-permute-done.8.refs_6_), channel_id=1, source_target_pairs={{0,1},{1,0},{2,3},{3,2},{4,5},{5,4},{6,7},{7,6},{8,9},{9,8},{10,11... | collective-permute-start | bytes 884744 | tf_op jit(solution)/shard_map/ppermute | solution.py:507
  29.6 24.0 %copy-start.4 = (bf16[576,256]{1,0:T(8,128)(2,1)}, bf16[576,256]{1,0:T(8,128)(2,1)S(1)}, u32[]{:S(2)}) copy-start(bf16[576,256]{1,0:T(8,128)(2,1)S(1)} %collective-permute-done.6.refs_4_) | copy-start | bytes 884740
  29.7 43.3 %collective-permute-start.7 = (bf16[576,256]{1,0:T(8,128)(2,1)S(1)}, bf16[576,256]{1,0:T(8,128)(2,1)S(1)}, u32[]{:S(2)}, u32[]{:S(2)}) collective-permute-start(bf16[576,256]{1,0:T(8,128)(2,1)S(1)} %collective-permute-done.6.refs_4_), channel_id=1, source_target_pairs={{0,1},{1,0},{2,3},{3,2},{4,5},{5,4},{6,7},{7,6},{8,9},{9,8},{10,11... | collective-permute-start | bytes 884744 | tf_op jit(solution)/shard_map/ppermute | solution.py:507
  29.9 23.8 %copy-start.5 = (bf16[576,256]{1,0:T(8,128)(2,1)}, bf16[576,256]{1,0:T(8,128)(2,1)S(1)}, u32[]{:S(2)}) copy-start(bf16[576,256]{1,0:T(8,128)(2,1)S(1)} %collective-permute-done.4.refs_2_) | copy-start | bytes 884740
  29.9 43.0 %collective-permute-start.5 = (bf16[576,256]{1,0:T(8,128)(2,1)S(1)}, bf16[576,256]{1,0:T(8,128)(2,1)S(1)}, u32[]{:S(2)}, u32[]{:S(2)}) collective-permute-start(bf16[576,256]{1,0:T(8,128)(2,1)S(1)} %collective-permute-done.4.refs_2_), channel_id=1, source_target_pairs={{0,1},{1,0},{2,3},{3,2},{4,5},{5,4},{6,7},{7,6},{8,9},{9,8},{10,11... | collective-permute-start | bytes 884744 | tf_op jit(solution)/shard_map/ppermute | solution.py:507
  30.2 0.7 copy-start.1
  53.7 1.5 collective-permute-start.10
  55.2 0.6 copy-start.28
  57.1 5.7 %collective-permute-start.13 = (f32[8,512]{1,0:T(8,128)}, f32[8,512]{1,0:T(8,128)S(1)}, u32[]{:S(2)}, u32[]{:S(2)}) collective-permute-start(f32[8,512]{1,0:T(8,128)} %core_join.1.refs_0_), channel_id=1, source_target_pairs={{0,6},{1,7},{2,4},{3,5},{4,2},{5,3},{6,0},{7,1},{8,14},{9,15},{10,... | collective-permute-start | bytes 49160 | tf_op jit(solution)/shard_map/ppermute | solution.py:507
  58.6 4.8 %collective-permute-start.12 = (f32[8,512]{1,0:T(8,128)}, f32[8,512]{1,0:T(8,128)S(1)}, u32[]{:S(2)}, u32[]{:S(2)}) collective-permute-start(f32[8,512]{1,0:T(8,128)} %core_join.1.refs_0_), channel_id=1, source_target_pairs={{0,4},{1,5},{2,6},{3,7},{4,0},{5,1},{6,2},{7,3},{8,12},{9,13},{10,... | collective-permute-start | bytes 49160 | tf_op jit(solution)/shard_map/ppermute | solution.py:507
  62.9 4.0 %copy-start.25 = (f32[8,512]{1,0:T(8,128)}, f32[8,512]{1,0:T(8,128)S(1)}, u32[]{:S(2)}) copy-start(f32[8,512]{1,0:T(8,128)S(1)} %collective-permute-done.13.refs_3_) | copy-start | bytes 49156
  62.9 3.9 %collective-permute-start.11 = (f32[8,512]{1,0:T(8,128)}, f32[8,512]{1,0:T(8,128)S(1)}, u32[]{:S(2)}, u32[]{:S(2)}) collective-permute-start(f32[8,512]{1,0:T(8,128)} %core_join.1.refs_0_), channel_id=1, source_target_pairs={{0,2},{1,3},{2,0},{3,1},{4,6},{5,7},{6,4},{7,5},{8,10},{9,11},{10,... | collective-permute-start | bytes 49160 | tf_op jit(solution)/shard_map/ppermute | solution.py:507
  63.5 3.4 %copy-start.26 = (f32[8,512]{1,0:T(8,128)}, f32[8,512]{1,0:T(8,128)S(1)}, u32[]{:S(2)}) copy-start(f32[8,512]{1,0:T(8,128)S(1)} %collective-permute-done.12.refs_2_) | copy-start | bytes 49156
  66.8 0.6 copy-start.27
  69.4 7.8 %collective-permute-start.16 = (f32[8,512]{1,0:T(8,128)}, f32[8,512]{1,0:T(8,128)S(1)}, u32[]{:S(2)}, u32[]{:S(2)}) collective-permute-start(f32[8,512]{1,0:T(8,128)} %get-tuple-element.51.refs_0_), channel_id=1, source_target_pairs={{0,24},{8,16},{16,8},{24,0},{1,25},{9,17},{17,9},{25,1},{2,26},{10... | collective-permute-start | bytes 49160 | tf_op jit(solution)/shard_map/ppermute | solution.py:510
  71.2 6.0 %collective-permute-start.15 = (f32[8,512]{1,0:T(8,128)}, f32[8,512]{1,0:T(8,128)S(1)}, u32[]{:S(2)}, u32[]{:S(2)}) collective-permute-start(f32[8,512]{1,0:T(8,128)} %get-tuple-element.51.refs_0_), channel_id=1, source_target_pairs={{0,16},{8,24},{16,0},{24,8},{1,17},{9,25},{17,1},{25,9},{2,18},{10... | collective-permute-start | bytes 49160 | tf_op jit(solution)/shard_map/ppermute | solution.py:510
  72.6 0.7 copy-start.6
  72.6 4.6 %collective-permute-start.14 = (f32[8,512]{1,0:T(8,128)}, f32[8,512]{1,0:T(8,128)S(1)}, u32[]{:S(2)}, u32[]{:S(2)}) collective-permute-start(f32[8,512]{1,0:T(8,128)} %get-tuple-element.51.refs_0_), channel_id=1, source_target_pairs={{0,8},{8,0},{16,24},{24,16},{1,9},{9,1},{17,25},{25,17},{2,10},{10... | collective-permute-start | bytes 49160 | tf_op jit(solution)/shard_map/ppermute | solution.py:510
  72.9 0.7 copy-start.7
  72.9 0.8 copy-start.8
  77.2 0.6 copy-start.18
  77.2 0.6 copy-start.19
  77.2 0.6 copy-start.20
  93.8 18.7 %copy-start.30 = (f32[8,128]{1,0:T(8,128)S(1)}, f32[8,128]{1,0:T(8,128)}, u32[]{:S(2)}) copy-start(f32[8,128]{1,0:T(8,128)} %get-tuple-element.56) | copy-start | bytes 12292
  93.8 28.0 %copy-start.33 = (bf16[64,2048]{1,0:T(8,128)(2,1)S(1)}, bf16[64,2048]{1,0:T(8,128)(2,1)}, u32[]{:S(2)}) copy-start(bf16[64,2048]{1,0:T(8,128)(2,1)} %get-tuple-element.76) | copy-start | bytes 786436
  93.8 28.3 %copy-start.32 = (bf16[64,2048]{1,0:T(8,128)(2,1)S(1)}, bf16[64,2048]{1,0:T(8,128)(2,1)}, u32[]{:S(2)}) copy-start(bf16[64,2048]{1,0:T(8,128)(2,1)} %get-tuple-element.77) | copy-start | bytes 786436
  93.8 31.2 %copy-start.31 = (bf16[64,2048]{1,0:T(8,128)(2,1)S(1)}, bf16[64,2048]{1,0:T(8,128)(2,1)}, u32[]{:S(2)}) copy-start(bf16[64,2048]{1,0:T(8,128)(2,1)} %get-tuple-element.78) | copy-start | bytes 786436
  110.7 3.7 %collective-permute-start.17 = (bf16[1024,256]{1,0:T(8,128)(2,1)}, bf16[1024,256]{1,0:T(8,128)(2,1)S(1)}, u32[]{:S(2)}, u32[]{:S(2)}) collective-permute-start(bf16[1024,256]{1,0:T(8,128)(2,1)} %get-tuple-element.55), channel_id=1, source_target_pairs={{0,1},{1,0},{2,3},{3,2},{4,5},{5,4},{6,7},{7,6},{8,9},{9,8},{10,11... | collective-permute-start | bytes 1572872 | tf_op jit(solution)/shard_map/ppermute | solution.py:507
  110.8 11.4 %collective-permute-start.25 = (bf16[64,2048]{1,0:T(8,128)(2,1)}, bf16[64,2048]{1,0:T(8,128)(2,1)S(1)}, u32[]{:S(2)}, u32[]{:S(2)}) collective-permute-start(bf16[64,2048]{1,0:T(8,128)(2,1)} %get-tuple-element.72), channel_id=1, source_target_pairs={{0,8},{8,0},{16,24},{24,16},{1,9},{9,1},{17,25},{25,17},{2,10},{10... | collective-permute-start | bytes 786440 | tf_op jit(solution)/shard_map/ppermute | solution.py:510
  113.2 1.2 copy-start.24
  113.2 1.2 collective-permute-start.18
  114.4 0.8 copy-start.2
  117.4 7.7 %collective-permute-start.19 = (bf16[272,256]{1,0:T(8,128)(2,1)}, bf16[272,256]{1,0:T(8,128)(2,1)S(1)}, u32[]{:S(2)}, u32[]{:S(2)}) collective-permute-start(bf16[272,256]{1,0:T(8,128)(2,1)} %get-tuple-element.60), channel_id=1, source_target_pairs={{0,2},{1,3},{2,0},{3,1},{4,6},{5,7},{6,4},{7,5},{8,10},{9,11},{10,... | collective-permute-start | bytes 417800 | tf_op jit(solution)/shard_map/ppermute | solution.py:507
  117.4 13.6 %collective-permute-start.20 = (bf16[272,256]{1,0:T(8,128)(2,1)}, bf16[272,256]{1,0:T(8,128)(2,1)S(1)}, u32[]{:S(2)}, u32[]{:S(2)}) collective-permute-start(bf16[272,256]{1,0:T(8,128)(2,1)} %get-tuple-element.61), channel_id=1, source_target_pairs={{0,4},{1,5},{2,6},{3,7},{4,0},{5,1},{6,2},{7,3},{8,12},{9,13},{10,... | collective-permute-start | bytes 417800 | tf_op jit(solution)/shard_map/ppermute | solution.py:507
  119.3 12.5 %collective-permute-start.21 = (bf16[272,256]{1,0:T(8,128)(2,1)}, bf16[272,256]{1,0:T(8,128)(2,1)S(1)}, u32[]{:S(2)}, u32[]{:S(2)}) collective-permute-start(bf16[272,256]{1,0:T(8,128)(2,1)} %get-tuple-element.62), channel_id=1, source_target_pairs={{0,6},{1,7},{2,4},{3,5},{4,2},{5,3},{6,0},{7,1},{8,14},{9,15},{10,... | collective-permute-start | bytes 417800 | tf_op jit(solution)/shard_map/ppermute | solution.py:507
  121.8 12.9 %collective-permute-start.28 = (bf16[64,2048]{1,0:T(8,128)(2,1)S(1)}, bf16[64,2048]{1,0:T(8,128)(2,1)S(1)}, u32[]{:S(2)}, u32[]{:S(2)}) collective-permute-start(bf16[64,2048]{1,0:T(8,128)(2,1)S(1)} %copy-done.33), channel_id=1, source_target_pairs={{0,8},{8,0},{16,24},{24,16},{1,9},{9,1},{17,25},{25,17},{2,10},{10... | collective-permute-start | bytes 786440 | tf_op jit(solution)/shard_map/ppermute | solution.py:510
  122.2 29.6 %copy-start.9 = (bf16[64,2048]{1,0:T(8,128)(2,1)}, bf16[64,2048]{1,0:T(8,128)(2,1)S(1)}, u32[]{:S(2)}) copy-start(bf16[64,2048]{1,0:T(8,128)(2,1)S(1)} %collective-permute-done.25.refs_1_) | copy-start | bytes 786436
  122.2 16.7 %collective-permute-start.29 = (bf16[64,2048]{1,0:T(8,128)(2,1)S(1)}, bf16[64,2048]{1,0:T(8,128)(2,1)S(1)}, u32[]{:S(2)}, u32[]{:S(2)}) collective-permute-start(bf16[64,2048]{1,0:T(8,128)(2,1)S(1)} %copy-done.32), channel_id=1, source_target_pairs={{0,16},{8,24},{16,0},{24,8},{1,17},{9,25},{17,1},{25,9},{2,18},{10... | collective-permute-start | bytes 786440 | tf_op jit(solution)/shard_map/ppermute | solution.py:510
  125.1 7.8 %copy-start.15 = (bf16[272,256]{1,0:T(8,128)(2,1)}, bf16[272,256]{1,0:T(8,128)(2,1)S(1)}, u32[]{:S(2)}) copy-start(bf16[272,256]{1,0:T(8,128)(2,1)S(1)} %collective-permute-done.19.refs_0_) | copy-start | bytes 417796
  125.1 18.0 %collective-permute-start.30 = (bf16[64,2048]{1,0:T(8,128)(2,1)S(1)}, bf16[64,2048]{1,0:T(8,128)(2,1)S(1)}, u32[]{:S(2)}, u32[]{:S(2)}) collective-permute-start(bf16[64,2048]{1,0:T(8,128)(2,1)S(1)} %copy-done.31), channel_id=1, source_target_pairs={{0,24},{8,16},{16,8},{24,0},{1,25},{9,17},{17,9},{25,1},{2,26},{10... | collective-permute-start | bytes 786440 | tf_op jit(solution)/shard_map/ppermute | solution.py:510
  131.1 1.8 %copy-start.16 = (bf16[272,256]{1,0:T(8,128)(2,1)}, bf16[272,256]{1,0:T(8,128)(2,1)S(1)}, u32[]{:S(2)}) copy-start(bf16[272,256]{1,0:T(8,128)(2,1)S(1)} %collective-permute-done.20.refs_1_) | copy-start | bytes 417796
  131.1 20.7 %collective-permute-start.26 = (bf16[64,2048]{1,0:T(8,128)(2,1)}, bf16[64,2048]{1,0:T(8,128)(2,1)S(1)}, u32[]{:S(2)}, u32[]{:S(2)}) collective-permute-start(bf16[64,2048]{1,0:T(8,128)(2,1)} %get-tuple-element.73), channel_id=1, source_target_pairs={{0,16},{8,24},{16,0},{24,8},{1,17},{9,25},{17,1},{25,9},{2,18},{10... | collective-permute-start | bytes 786440 | tf_op jit(solution)/shard_map/ppermute | solution.py:510
  131.8 1.1 copy-start.17
  131.8 20.0 %collective-permute-start.27 = (bf16[64,2048]{1,0:T(8,128)(2,1)}, bf16[64,2048]{1,0:T(8,128)(2,1)S(1)}, u32[]{:S(2)}, u32[]{:S(2)}) collective-permute-start(bf16[64,2048]{1,0:T(8,128)(2,1)} %get-tuple-element.74), channel_id=1, source_target_pairs={{0,24},{8,16},{16,8},{24,0},{1,25},{9,17},{17,9},{25,1},{2,26},{10... | collective-permute-start | bytes 786440 | tf_op jit(solution)/shard_map/ppermute | solution.py:510
  134.7 8.9 %copy-start.10 = (bf16[64,2048]{1,0:T(8,128)(2,1)}, bf16[64,2048]{1,0:T(8,128)(2,1)S(1)}, u32[]{:S(2)}) copy-start(bf16[64,2048]{1,0:T(8,128)(2,1)S(1)} %collective-permute-done.28.refs_1_) | copy-start | bytes 786436
  134.7 25.8 %collective-permute-start.22 = (bf16[80,256]{1,0:T(8,128)(2,1)}, bf16[80,256]{1,0:T(8,128)(2,1)S(1)}, u32[]{:S(2)}, u32[]{:S(2)}) collective-permute-start(bf16[80,256]{1,0:T(8,128)(2,1)} %get-tuple-element.67), channel_id=1, source_target_pairs={{0,8},{8,0},{16,24},{24,16},{1,9},{9,1},{17,25},{25,17},{2,10},{10... | collective-permute-start | bytes 122888 | tf_op jit(solution)/shard_map/ppermute | solution.py:510
  138.9 4.7 %copy-start.12 = (bf16[64,2048]{1,0:T(8,128)(2,1)}, bf16[64,2048]{1,0:T(8,128)(2,1)S(1)}, u32[]{:S(2)}) copy-start(bf16[64,2048]{1,0:T(8,128)(2,1)S(1)} %collective-permute-done.29.refs_2_) | copy-start | bytes 786436
  138.9 21.6 %collective-permute-start.23 = (bf16[80,256]{1,0:T(8,128)(2,1)}, bf16[80,256]{1,0:T(8,128)(2,1)S(1)}, u32[]{:S(2)}, u32[]{:S(2)}) collective-permute-start(bf16[80,256]{1,0:T(8,128)(2,1)} %get-tuple-element.68), channel_id=1, source_target_pairs={{0,16},{8,24},{16,0},{24,8},{1,17},{9,25},{17,1},{25,9},{2,18},{10... | collective-permute-start | bytes 122888 | tf_op jit(solution)/shard_map/ppermute | solution.py:510
  143.1 0.7 copy-start.14
  143.1 17.5 %collective-permute-start.24 = (bf16[80,256]{1,0:T(8,128)(2,1)}, bf16[80,256]{1,0:T(8,128)(2,1)S(1)}, u32[]{:S(2)}, u32[]{:S(2)}) collective-permute-start(bf16[80,256]{1,0:T(8,128)(2,1)} %get-tuple-element.69), channel_id=1, source_target_pairs={{0,24},{8,16},{16,8},{24,0},{1,25},{9,17},{17,9},{25,1},{2,26},{10... | collective-permute-start | bytes 122888 | tf_op jit(solution)/shard_map/ppermute | solution.py:510
  151.8 0.7 copy-start.11
  151.8 0.8 copy-start.13
  160.5 0.6 copy-start.21
  160.5 0.6 copy-start.22
  160.6 0.6 copy-start.23
  (1 other events, 0.6 us)

commit v2 on v1

--- a/solution.py
+++ b/solution.py
@@ -27,12 +27,15 @@
 f32 = jnp.float32
 bf16 = jnp.bfloat16
 PAD = 16
-VMEM_LIMIT = 56 << 20
 CHUNKS = 2
 
 
-def params(**more):
-    return pltpu.CompilerParams(vmem_limit_bytes=VMEM_LIMIT, **more)
+def params(mebibytes):
+    return pltpu.CompilerParams(vmem_limit_bytes=mebibytes << 20)
+
+
+def cost(flops, moved):
+    return pl.CostEstimate(flops=flops, bytes_accessed=moved, transcendentals=0)
 
 
 def whole(shape):
@@ -79,7 +82,8 @@
             jax.ShapeDtypeStruct((count, width), f32),
             jax.ShapeDtypeStruct((count, 128), f32),
         ],
-        compiler_params=params(),
+        compiler_params=params(8),
+        cost_estimate=cost(0, 1 << 20),
         name="pick_rows",
     )(rows, image, student, teacher)
 
@@ -151,8 +155,8 @@
         out_specs=whole((8, rows)),
         out_shape=jax.ShapeDtypeStruct((8, rows), f32),
         scratch_shapes=[pltpu.VMEM((rows, width), bf16)] * 2 + [pltpu.VMEM((rows, 128), f32)] * 4,
-        compiler_params=params(),
-        cost_estimate=pl.CostEstimate(flops=4 * rows * width * cols, bytes_accessed=8 * width * cols, transcendentals=2 * rows * cols),
+        compiler_params=params(24),
+        cost_estimate=cost(4 * rows * width * cols, 8 * width * cols),
         name="first_pass",
     )(own, other, ws, wt, centre)
 
@@ -225,7 +229,8 @@
         in_specs=[pl.BlockSpec(memory_space=pltpu.SMEM)] + [pl.BlockSpec(memory_space=pltpu.VMEM)] * len(packs),
         out_shape=[jax.ShapeDtypeStruct((rows, width), bf16)] * 2 + [jax.ShapeDtypeStruct((width, rows), bf16)],
         scratch_shapes=[pltpu.VMEM((width, rows), bf16)],
-        compiler_params=params(),
+        compiler_params=params(16),
+        cost_estimate=cost(0, 4 << 20),
         name="lay_rows",
     )(slab, *packs)
 
@@ -337,8 +342,8 @@
             num_scalar_prefetch=1, grid=(steps,), in_specs=in_specs, out_specs=out_specs, scratch_shapes=scratch
         ),
         out_shape=out_shape,
-        compiler_params=params(),
-        cost_estimate=pl.CostEstimate(flops=8 * rows * width * chunk, bytes_accessed=8 * width * chunk, transcendentals=2 * rows * chunk),
+        compiler_params=params(32),
+        cost_estimate=cost(8 * rows * width * chunk, 8 * width * chunk),
         name="second_pass",
     )(place, *args)
 
@@ -376,7 +381,8 @@
         out_shape=[jax.ShapeDtypeStruct((size, width), f32)]
         + [jax.ShapeDtypeStruct((size + PAD, width), bf16)] * (blocks - 1)
         + [jax.ShapeDtypeStruct((8, 128), f32)],
-        compiler_params=params(),
+        compiler_params=params(8),
+        cost_estimate=cost(0, 1 << 20),
         name="core_sum",
     )(keep, got, loss, other)
 
@@ -407,7 +413,8 @@
         out_shape=[jax.ShapeDtypeStruct((size, width), f32)]
         + [jax.ShapeDtypeStruct((size + PAD, width), bf16)] * (blocks - 1)
         + [jax.ShapeDtypeStruct((8, 128), f32)],
-        compiler_params=params(),
+        compiler_params=params(8),
+        cost_estimate=cost(0, 1 << 20),
         name="axis_sum",
     )(keep, loss, *got)
 
@@ -474,8 +481,8 @@
         ),
         out_shape=[jax.ShapeDtypeStruct((slab, total), f32)] * 4,
         input_output_aliases=aliases,
-        compiler_params=params(),
-        cost_estimate=pl.CostEstimate(flops=20 * slab * groups * chunk, bytes_accessed=34 * slab * groups * chunk, transcendentals=0),
+        compiler_params=params(16),
+        cost_estimate=cost(20 * slab * groups * chunk, 34 * slab * groups * chunk),
         name="optimizer",
     )(place, *args)
 
@@ -515,20 +522,25 @@
     far = [dp_swap(own, k) for k in range(1, groups)]
 
     stats = first_pass(own, other, student_proto, teacher_proto, centre, count)
+    stats, *far = lax.optimization_barrier((stats, *far))
     far_other = [proto_swap(x, 1) for x in far]
     packs = [own, other]
     for pair in zip(far, far_other):
         packs += list(pair)
     us, ut, flipped = lay_rows(place, packs, count)
 
-    rows = stats.shape[1]
     stats = pl.pallas_call(
-        core_join_kernel, out_shape=jax.ShapeDtypeStruct(stats.shape, f32), compiler_params=params(), name="core_join"
+        core_join_kernel,
+        out_shape=jax.ShapeDtypeStruct(stats.shape, f32),
+        compiler_params=params(8),
+        cost_estimate=cost(0, 1 << 20),
+        name="core_join",
     )(stats, proto_swap(stats, 1))
     stats, loss_own = pl.pallas_call(
         functools.partial(final_join_kernel, count=count, images=images, ratio=ratio),
         out_shape=[jax.ShapeDtypeStruct(stats.shape, f32), jax.ShapeDtypeStruct((8, 128), f32)],
-        compiler_params=params(),
+        compiler_params=params(8),
+        cost_estimate=cost(0, 1 << 20),
         name="final_join",
     )(stats, *[proto_swap(stats, k) for k in range(2, protos, 2)], own, other)
     all_stats = [stats] + [dp_swap(stats, k) for k in range(1, groups)]
@@ -542,6 +554,7 @@
         grads, carry = out[:groups], out[groups:]
         sent.append([grads[0]] + [dp_swap(grads[k], k) for k in range(1, groups)])
     keep, send, cross = carry
+    send, sent[:-1] = lax.optimization_barrier((send, sent[:-1]))
     loss = loss_own - cross
 
     zs_count = protos // 2
@@ -551,7 +564,8 @@
     row_grad, total = pl.pallas_call(
         functools.partial(row_kernel, sources=len(got), rows_total=rows_total),
         out_shape=[jax.ShapeDtypeStruct((count, width), f32), jax.ShapeDtypeStruct((8, 128), f32)],
-        compiler_params=params(),
+        compiler_params=params(8),
+        cost_estimate=cost(0, 1 << 20),
         name="row_grad",
     )(out[0], out[-1], raw, inv, *got)
 

time: 165 us -> 137 us (0.83)
  Pallas kernels: 85.9 us -> 64.1 us
  waiting for transfers between devices: 35.4 us -> 25.9 us
  local copies, waits for them, and re-layouts: 7.91 us -> 12.3 us
    ppermute x15, waiting for transfers between devices: 14.8 us -> 2.74 us  [dp_swap(): return lax.ppermute(x, 'dp', xor_pairs(groups, k))]
    unnamed x71 -> x29, local copies, waits for them, and re-layouts: 6.73 us -> 11.8 us
    pallas_call x2, Pallas kernels: 32.8 us -> 28.1 us  [second_pass(): pl.pallas_call(functools.partial(second_kernel, groups=groups, first=firs...]
    pallas_call x2, Pallas kernels: 15.9 us -> 12.3 us  [optimizer(): pl.pallas_call(functools.partial(step_kernel, groups=groups), grid_spec=p...]
    pallas_call x1, Pallas kernels: 3.47 us -> 0.47 us  [lay_rows(): pl.pallas_call(functools.partial(lay_kernel, count=count, groups=groups),...]
    ppermute x15, starting transfers between devices: 20.7 us -> 17.7 us  [dp_swap(): return lax.ppermute(x, 'dp', xor_pairs(groups, k))]
    ppermute x16, waiting for transfers between devices: 20.6 us -> 23.1 us  [proto_swap(): return lax.ppermute(x, 'proto', xor_pairs(protos, k))]
    ppermute x16, starting transfers between devices: 12.7 us -> 15.2 us  [proto_swap(): return lax.ppermute(x, 'proto', xor_pairs(protos, k))]
  transfers between devices with their start and end apart: 31 -> 31, of which waited for: 13 -> 11; matrix products, arithmetic and copies ran while one was open for 1% -> 0% of each run, Pallas kernels for 30% -> 36%
where the time goes in v2:
time: 137 us; the launch traced here: 136 us
  Pallas kernels  64.1 us (47%)
  starting transfers between devices  32.9 us (24%)
  waiting for transfers between devices  25.9 us (19%)
  local copies, waits for them, and re-layouts  12.3 us (9%)
    pallas_call x2, Pallas kernels, second_pass(): pl.pallas_call(functools.partial(second_kernel, groups=groups, first=firs...  28.1 us
    ppermute x16, waiting for transfers between devices, proto_swap(): return lax.ppermute(x, 'proto', xor_pairs(protos, k))  23.1 us
    pallas_call x1, Pallas kernels, first_pass(): pl.pallas_call(functools.partial(first_kernel, count=count), grid=(cols /...  21.7 us
    ppermute x15, starting transfers between devices, dp_swap(): return lax.ppermute(x, 'dp', xor_pairs(groups, k))  17.7 us
    ppermute x16, starting transfers between devices, proto_swap(): return lax.ppermute(x, 'proto', xor_pairs(protos, k))  15.2 us
    pallas_call x2, Pallas kernels, optimizer(): pl.pallas_call(functools.partial(step_kernel, groups=groups), grid_spec=p...  12.3 us
    unnamed x29, local copies, waits for them, and re-layouts  11.8 us
    ppermute x15, waiting for transfers between devices, dp_swap(): return lax.ppermute(x, 'dp', xor_pairs(groups, k))  2.74 us
  transfers between devices with their start and end apart: 31, of which 11 were waited for; matrix products, arithmetic and copies ran while one was open for 0% of the time, Pallas kernels for 36%

profile of v2, /device:TPU:0, one launch (start us, length us, event | category | flops | bytes accessed | tf_op | source)
XLA Modules:
  0.0 136.1 jit_solution(8006701926561568670)
XLA Ops:
  0.6 0.8 copy-done.5
  1.5 0.8 copy-done.6
  2.3 0.7 copy-done.7
  3.0 0.7 copy-done.8
  3.6 0.3 pick_rows.1
  3.9 5.1 %collective-permute-start.2 = (bf16[144,256]{1,0:T(8,128)(2,1)S(1)}, bf16[144,256]{1,0:T(8,128)(2,1)S(1)}, u32[]{:S(2)}, u32[]{:S(2)}) collective-permute-start(bf16[144,256]{1,0:T(8,128)(2,1)S(1)} %get-tuple-element.56), channel_id=1, source_target_pairs={{0,6},{1,7},{2,4},{3,5},{4,2},{5,3},{6,0},{7,1},{8,14},{9,15},{10,... | collective-permute-start | bytes 221192 | tf_op jit(solution)/shard_map/ppermute | solution.py:514
  9.0 0.6 collective-permute-start
  9.7 4.1 %collective-permute-done = bf16[144,256]{1,0:T(8,128)(2,1)S(1)} collective-permute-done((bf16[144,256]{1,0:T(8,128)(2,1)S(1)}, bf16[144,256]{1,0:T(8,128)(2,1)S(1)}, u32[]{:S(2)}, u32[]{:S(2)}) %collective-permute-start) | collective-permute-done | bytes 73760 | tf_op jit(solution)/shard_map/ppermute | solution.py:514
  13.8 1.5 %collective-permute-done.1 = bf16[144,256]{1,0:T(8,128)(2,1)S(1)} collective-permute-done((bf16[144,256]{1,0:T(8,128)(2,1)S(1)}, bf16[144,256]{1,0:T(8,128)(2,1)S(1)}, u32[]{:S(2)}, u32[]{:S(2)}) %collective-permute-start.1) | collective-permute-done | bytes 73760 | tf_op jit(solution)/shard_map/ppermute | solution.py:514
  15.3 0.0 collective-permute-done.2
  15.3 0.1 collective-permute-start.3
  15.4 2.5 %collective-permute-start.6 = (bf16[576,256]{1,0:T(8,128)(2,1)S(1)}, bf16[576,256]{1,0:T(8,128)(2,1)S(1)}, u32[]{:S(2)}, u32[]{:S(2)}) collective-permute-start(bf16[576,256]{1,0:T(8,128)(2,1)S(1)} %constant_dynamic-update-slice_fusion.own_ref.refs_0_.refs_4_), channel_id=1, source_target_pairs={{0,24},{8,16},{16,8},{24,0},{1,25},{9,17},{17,9},{25,1},{2,26},{10... | collective-permute-start | bytes 884744 | tf_op jit(solution)/shard_map/ppermute | solution.py:517
  17.9 0.5 collective-permute-start.5
  18.4 0.5 collective-permute-start.4
  18.9 5.8 %copy-done = f32[256,16384]{1,0:T(8,128)S(1)} copy-done((f32[256,16384]{1,0:T(8,128)S(1)}, f32[256,16384]{1,0:T(8,128)}, u32[]{:S(2)}) %copy-start) | copy-done | bytes 16777240
  24.7 0.8 copy-done.3
  25.5 21.7 %first_pass.1.own_ref = f32[8,512]{1,0:T(8,128)S(1)} custom-call(bf16[576,256]{1,0:T(8,128)(2,1)S(1)} %constant_dynamic-update-slice_fusion.own_ref.refs_0_.refs_4_, bf16[576,256]{1,0:T(8,128)(2,1)S(1)} %collective-permute-done.3.other_ref.refs_1_.refs_5_, f32[256,16384]{1,0:T(8,128)S(1)} %copy-done, f32[256,16384]{1,0:T(8,128)} %refs_5_.3, ...), custom_call_target="tpu_custom_call" | custom-call | flops 8589934592 | bytes 33554432 | tf_op jit(solution)/shard_map/first_pass/pallas_call | solution.py:145
  47.2 0.0 collective-permute-done.5.refs_4_
  47.3 0.1 collective-permute-start.7
  47.3 0.5 collective-permute-start.8
  47.8 0.1 collective-permute-start.9
  47.9 0.4 collective-permute-start.10
  48.4 1.4 %collective-permute-done.10.other_ref = f32[8,512]{1,0:T(8,128)S(1)} collective-permute-done((f32[8,512]{1,0:T(8,128)S(1)}, f32[8,512]{1,0:T(8,128)S(1)}, u32[]{:S(2)}, u32[]{:S(2)}) %collective-permute-start.10) | collective-permute-done | bytes 16416 | tf_op jit(solution)/shard_map/ppermute | solution.py:514
  49.8 2.8 %collective-permute-start.13 = (f32[8,512]{1,0:T(8,128)S(1)}, f32[8,512]{1,0:T(8,128)S(1)}, u32[]{:S(2)}, u32[]{:S(2)}) collective-permute-start(f32[8,512]{1,0:T(8,128)S(1)} %core_join.1.refs_0_), channel_id=1, source_target_pairs={{0,6},{1,7},{2,4},{3,5},{4,2},{5,3},{6,0},{7,1},{8,14},{9,15},{10,... | collective-permute-start | bytes 49160 | tf_op jit(solution)/shard_map/ppermute | solution.py:514
  52.6 0.0 collective-permute-start.12
  52.6 2.8 %collective-permute-done.13.refs_3_ = f32[8,512]{1,0:T(8,128)S(1)} collective-permute-done((f32[8,512]{1,0:T(8,128)S(1)}, f32[8,512]{1,0:T(8,128)S(1)}, u32[]{:S(2)}, u32[]{:S(2)}) %collective-permute-start.13) | collective-permute-done | bytes 16416 | tf_op jit(solution)/shard_map/ppermute | solution.py:514
  55.4 1.9 %collective-permute-done.12.refs_2_ = f32[8,512]{1,0:T(8,128)S(1)} collective-permute-done((f32[8,512]{1,0:T(8,128)S(1)}, f32[8,512]{1,0:T(8,128)S(1)}, u32[]{:S(2)}, u32[]{:S(2)}) %collective-permute-start.12) | collective-permute-done | bytes 16416 | tf_op jit(solution)/shard_map/ppermute | solution.py:514
  57.3 1.8 %collective-permute-done.11.refs_1_ = f32[8,512]{1,0:T(8,128)S(1)} collective-permute-done((f32[8,512]{1,0:T(8,128)S(1)}, f32[8,512]{1,0:T(8,128)S(1)}, u32[]{:S(2)}, u32[]{:S(2)}) %collective-permute-start.11) | collective-permute-done | bytes 16416 | tf_op jit(solution)/shard_map/ppermute | solution.py:514
  59.1 0.2 final_join.1
  59.4 2.5 %collective-permute-start.16 = (f32[8,512]{1,0:T(8,128)S(1)}, f32[8,512]{1,0:T(8,128)S(1)}, u32[]{:S(2)}, u32[]{:S(2)}) collective-permute-start(f32[8,512]{1,0:T(8,128)S(1)} %get-tuple-element.64.refs_0_), channel_id=1, source_target_pairs={{0,24},{8,16},{16,8},{24,0},{1,25},{9,17},{17,9},{25,1},{2,26},{10... | collective-permute-start | bytes 49160 | tf_op jit(solution)/shard_map/ppermute | solution.py:517
  61.8 0.5 collective-permute-start.15
  62.4 0.5 collective-permute-start.14
  62.9 0.5 lay_rows.1
  63.4 0.7 collective-permute-done.16.refs_3_
  64.0 1.5 %collective-permute-done.15.refs_2_ = f32[8,512]{1,0:T(8,128)S(1)} collective-permute-done((f32[8,512]{1,0:T(8,128)S(1)}, f32[8,512]{1,0:T(8,128)S(1)}, u32[]{:S(2)}, u32[]{:S(2)}) %collective-permute-start.15) | collective-permute-done | bytes 16416 | tf_op jit(solution)/shard_map/ppermute | solution.py:517
  65.6 0.5 collective-permute-done.14.refs_1_
  66.1 13.9 %second_pass.2 = (bf16[64,2048]{1,0:T(8,128)(2,1)S(1)}, bf16[64,2048]{1,0:T(8,128)(2,1)S(1)}, bf16[64,2048]{1,0:T(8,128)(2,1)S(1)}, bf16[64,2048]{1,0:T(8,128)(2...) custom-call(s32[1]{0:T(128)} %bitcast.slab_ref.place_ref, bf16[2048,256]{1,0:T(8,128)(2,1)S(1)} %get-tuple-element.60.us, ...), custom_call_target="tpu_custom_call" | custom-call | flops 8589934592 | bytes 4194304 | tf_op jit(solution)/shard_map/second_pass/pallas_call | solution.py:339
  80.0 0.6 collective-permute-start.17
  80.6 1.5 %collective-permute-start.18 = (bf16[64,2048]{1,0:T(8,128)(2,1)S(1)}, bf16[64,2048]{1,0:T(8,128)(2,1)S(1)}, u32[]{:S(2)}, u32[]{:S(2)}) collective-permute-start(bf16[64,2048]{1,0:T(8,128)(2,1)S(1)} %get-tuple-element.71), channel_id=1, source_target_pairs={{0,16},{8,24},{16,0},{24,8},{1,17},{9,25},{17,1},{25,9},{2,18},{10... | collective-permute-start | bytes 786440 | tf_op jit(solution)/shard_map/ppermute | solution.py:517
  82.1 1.4 %collective-permute-start.19 = (bf16[64,2048]{1,0:T(8,128)(2,1)S(1)}, bf16[64,2048]{1,0:T(8,128)(2,1)S(1)}, u32[]{:S(2)}, u32[]{:S(2)}) collective-permute-start(bf16[64,2048]{1,0:T(8,128)(2,1)S(1)} %get-tuple-element.72), channel_id=1, source_target_pairs={{0,24},{8,16},{16,8},{24,0},{1,25},{9,17},{17,9},{25,1},{2,26},{10... | collective-permute-start | bytes 786440 | tf_op jit(solution)/shard_map/ppermute | solution.py:517
  83.6 0.0 copy-start.1
  83.6 14.2 %second_pass.3 = (bf16[64,2048]{1,0:T(8,128)(2,1)S(1)}, bf16[64,2048]{1,0:T(8,128)(2,1)S(1)}, bf16[64,2048]{1,0:T(8,128)(2,1)S(1)}, bf16[64,2048]{1,0:T(8,128)(2...) custom-call(s32[1]{0:T(128)} %bitcast.slab_ref.place_ref, ...), custom_call_target="tpu_custom_call" | custom-call | flops 8589934592 | bytes 4194304 | tf_op jit(solution)/shard_map/second_pass/pallas_call | solution.py:339
  97.8 0.0 collective-permute-done.18.refs_2_
  97.9 0.1 collective-permute-start.20
  98.0 0.5 collective-permute-start.21
  98.5 1.4 %collective-permute-done.21.other_ref = f32[8,128]{1,0:T(8,128)S(1)} collective-permute-done((f32[8,128]{1,0:T(8,128)S(1)}, f32[8,128]{1,0:T(8,128)S(1)}, u32[]{:S(2)}, u32[]{:S(2)}) %collective-permute-start.21) | collective-permute-done | bytes 4128 | tf_op jit(solution)/shard_map/ppermute | solution.py:514
  99.9 0.1 core_sum.1
  100.0 0.1 collective-permute-start.22
  100.1 0.6 collective-permute-start.28
  100.7 1.5 %collective-permute-start.29 = (bf16[64,2048]{1,0:T(8,128)(2,1)S(1)}, bf16[64,2048]{1,0:T(8,128)(2,1)S(1)}, u32[]{:S(2)}, u32[]{:S(2)}) collective-permute-start(bf16[64,2048]{1,0:T(8,128)(2,1)S(1)} %get-tuple-element.91), channel_id=1, source_target_pairs={{0,16},{8,24},{16,0},{24,8},{1,17},{9,25},{17,1},{25,9},{2,18},{10... | collective-permute-start | bytes 786440 | tf_op jit(solution)/shard_map/ppermute | solution.py:517
  102.2 1.4 %collective-permute-start.30 = (bf16[64,2048]{1,0:T(8,128)(2,1)S(1)}, bf16[64,2048]{1,0:T(8,128)(2,1)S(1)}, u32[]{:S(2)}, u32[]{:S(2)}) collective-permute-start(bf16[64,2048]{1,0:T(8,128)(2,1)S(1)} %get-tuple-element.92), channel_id=1, source_target_pairs={{0,24},{8,16},{16,8},{24,0},{1,25},{9,17},{17,9},{25,1},{2,26},{10... | collective-permute-start | bytes 786440 | tf_op jit(solution)/shard_map/ppermute | solution.py:517
  103.6 3.2 %collective-permute-start.23 = (bf16[272,256]{1,0:T(8,128)(2,1)S(1)}, bf16[272,256]{1,0:T(8,128)(2,1)S(1)}, u32[]{:S(2)}, u32[]{:S(2)}) collective-permute-start(bf16[272,256]{1,0:T(8,128)(2,1)S(1)} %get-tuple-element.79), channel_id=1, source_target_pairs={{0,4},{1,5},{2,6},{3,7},{4,0},{5,1},{6,2},{7,3},{8,12},{9,13},{10,... | collective-permute-start | bytes 417800 | tf_op jit(solution)/shard_map/ppermute | solution.py:514
  106.8 1.7 %collective-permute-start.24 = (bf16[272,256]{1,0:T(8,128)(2,1)S(1)}, bf16[272,256]{1,0:T(8,128)(2,1)S(1)}, u32[]{:S(2)}, u32[]{:S(2)}) collective-permute-start(bf16[272,256]{1,0:T(8,128)(2,1)S(1)} %get-tuple-element.80), channel_id=1, source_target_pairs={{0,6},{1,7},{2,4},{3,5},{4,2},{5,3},{6,0},{7,1},{8,14},{9,15},{10,... | collective-permute-start | bytes 417800 | tf_op jit(solution)/shard_map/ppermute | solution.py:514
  108.5 8.1 %collective-permute-done.23.refs_1_ = bf16[272,256]{1,0:T(8,128)(2,1)S(1)} collective-permute-done((bf16[272,256]{1,0:T(8,128)(2,1)S(1)}, bf16[272,256]{1,0:T(8,128)(2,1)S(1)}, u32[]{:S(2)}, u32[]{:S(2)}) %collective-permute-start.23) | collective-permute-done | bytes 139296 | tf_op jit(solution)/shard_map/ppermute | solution.py:514
  116.6 0.1 axis_sum.1
  116.7 0.6 collective-permute-start.25
  117.3 1.5 %collective-permute-start.26 = (bf16[80,256]{1,0:T(8,128)(2,1)S(1)}, bf16[80,256]{1,0:T(8,128)(2,1)S(1)}, u32[]{:S(2)}, u32[]{:S(2)}) collective-permute-start(bf16[80,256]{1,0:T(8,128)(2,1)S(1)} %get-tuple-element.86), channel_id=1, source_target_pairs={{0,16},{8,24},{16,0},{24,8},{1,17},{9,25},{17,1},{25,9},{2,18},{10... | collective-permute-start | bytes 122888 | tf_op jit(solution)/shard_map/ppermute | solution.py:517
  118.9 1.4 %collective-permute-start.27 = (bf16[80,256]{1,0:T(8,128)(2,1)S(1)}, bf16[80,256]{1,0:T(8,128)(2,1)S(1)}, u32[]{:S(2)}, u32[]{:S(2)}) collective-permute-start(bf16[80,256]{1,0:T(8,128)(2,1)S(1)} %get-tuple-element.87), channel_id=1, source_target_pairs={{0,24},{8,16},{16,8},{24,0},{1,25},{9,17},{17,9},{25,1},{2,26},{10... | collective-permute-start | bytes 122888 | tf_op jit(solution)/shard_map/ppermute | solution.py:517
  120.3 0.0 copy-start.2
  120.3 2.2 %copy-done.2 = f32[64,16384]{1,0:T(8,128)S(1)} copy-done((f32[64,16384]{1,0:T(8,128)S(1)}, f32[64,16384]{1,0:T(8,128)}, u32[]{:S(2)}) %copy-start.2) | copy-done | bytes 4194328
  122.5 6.1 %optimizer.2 = (f32[64,16384]{1,0:T(8,128)}, f32[64,16384]{1,0:T(8,128)}, f32[64,16384]{1,0:T(8,128)}, f32[64,16384]{1,0:T(8,128)}) custom-call(s32[1]{0:T(128)} %bitcast.slab_ref.place_ref, bf16[64,2048]{1,0:T(8,128)(2,1)S(1)} %get-tuple-element.93.refs_0_, bf16[64,2048]{1,0:T(8,128)(2,1)S(1)} %collective-permute-done.17.refs_1_, ...), custom_call_target="tpu_custom_call" | custom-call | flops 10485760 | bytes 17825792 | tf_op jit(solution)/shard_map/optimizer/pallas_call | solution.py:477
  128.6 6.2 %optimizer.3 = (f32[64,16384]{1,0:T(8,128)}, f32[64,16384]{1,0:T(8,128)}, f32[64,16384]{1,0:T(8,128)}, f32[64,16384]{1,0:T(8,128)}) custom-call(s32[1]{0:T(128)} %bitcast.slab_ref.place_ref, bf16[64,2048]{1,0:T(8,128)(2,1)S(1)} %get-tuple-element.89.refs_0_, ...), custom_call_target="tpu_custom_call", output_to_operand_aliasing={{0}: (9, {}), {1}: (10, {}), {2}: (11, {}), {3}: (12, {})} | custom-call | flops 10485760 | bytes 17825792 | tf_op jit(solution)/shard_map/optimizer/pallas_call | solution.py:477
  134.8 0.8 row_grad.1
  135.5 0.5 slice.3
  (43 shorter events, 0.1 us)
Async XLA Ops:
  0.6 0.8 copy-start.5
  1.5 0.8 copy-start.6
  2.3 0.7 copy-start.7
  3.0 0.7 copy-start.8
  3.9 11.3 %collective-permute-start.2 = (bf16[144,256]{1,0:T(8,128)(2,1)S(1)}, bf16[144,256]{1,0:T(8,128)(2,1)S(1)}, u32[]{:S(2)}, u32[]{:S(2)}) collective-permute-start(bf16[144,256]{1,0:T(8,128)(2,1)S(1)} %get-tuple-element.56), channel_id=1, source_target_pairs={{0,6},{1,7},{2,4},{3,5},{4,2},{5,3},{6,0},{7,1},{8,14},{9,15},{10,... | collective-permute-start | bytes 221192 | tf_op jit(solution)/shard_map/ppermute | solution.py:514
  9.0 6.2 %collective-permute-start.1 = (bf16[144,256]{1,0:T(8,128)(2,1)S(1)}, bf16[144,256]{1,0:T(8,128)(2,1)S(1)}, u32[]{:S(2)}, u32[]{:S(2)}) collective-permute-start(bf16[144,256]{1,0:T(8,128)(2,1)S(1)} %get-tuple-element.56), channel_id=1, source_target_pairs={{0,4},{1,5},{2,6},{3,7},{4,0},{5,1},{6,2},{7,3},{8,12},{9,13},{10,... | collective-permute-start | bytes 221192 | tf_op jit(solution)/shard_map/ppermute | solution.py:514
  9.0 4.7 %collective-permute-start = (bf16[144,256]{1,0:T(8,128)(2,1)S(1)}, bf16[144,256]{1,0:T(8,128)(2,1)S(1)}, u32[]{:S(2)}, u32[]{:S(2)}) collective-permute-start(bf16[144,256]{1,0:T(8,128)(2,1)S(1)} %get-tuple-element.56), channel_id=1, source_target_pairs={{0,2},{1,3},{2,0},{3,1},{4,6},{5,7},{6,4},{7,5},{8,10},{9,11},{10,... | collective-permute-start | bytes 221192 | tf_op jit(solution)/shard_map/ppermute | solution.py:514
  15.3 3.6 %collective-permute-start.3 = (bf16[576,256]{1,0:T(8,128)(2,1)S(1)}, bf16[576,256]{1,0:T(8,128)(2,1)S(1)}, u32[]{:S(2)}, u32[]{:S(2)}) collective-permute-start(bf16[576,256]{1,0:T(8,128)(2,1)S(1)} %constant_dynamic-update-slice_fusion.own_ref.refs_0_.refs_4_), channel_id=1, source_target_pairs={{0,1},{1,0},{2,3},{3,2},{4,5},{5,4},{6,7},{7,6},{8,9},{9,8},{10,11... | collective-permute-start | bytes 884744 | tf_op jit(solution)/shard_map/ppermute | solution.py:514
  15.4 31.9 %collective-permute-start.6 = (bf16[576,256]{1,0:T(8,128)(2,1)S(1)}, bf16[576,256]{1,0:T(8,128)(2,1)S(1)}, u32[]{:S(2)}, u32[]{:S(2)}) collective-permute-start(bf16[576,256]{1,0:T(8,128)(2,1)S(1)} %constant_dynamic-update-slice_fusion.own_ref.refs_0_.refs_4_), channel_id=1, source_target_pairs={{0,24},{8,16},{16,8},{24,0},{1,25},{9,17},{17,9},{25,1},{2,26},{10... | collective-permute-start | bytes 884744 | tf_op jit(solution)/shard_map/ppermute | solution.py:517
  17.9 29.4 %collective-permute-start.5 = (bf16[576,256]{1,0:T(8,128)(2,1)S(1)}, bf16[576,256]{1,0:T(8,128)(2,1)S(1)}, u32[]{:S(2)}, u32[]{:S(2)}) collective-permute-start(bf16[576,256]{1,0:T(8,128)(2,1)S(1)} %constant_dynamic-update-slice_fusion.own_ref.refs_0_.refs_4_), channel_id=1, source_target_pairs={{0,16},{8,24},{16,0},{24,8},{1,17},{9,25},{17,1},{25,9},{2,18},{10... | collective-permute-start | bytes 884744 | tf_op jit(solution)/shard_map/ppermute | solution.py:517
  18.4 28.9 %collective-permute-start.4 = (bf16[576,256]{1,0:T(8,128)(2,1)S(1)}, bf16[576,256]{1,0:T(8,128)(2,1)S(1)}, u32[]{:S(2)}, u32[]{:S(2)}) collective-permute-start(bf16[576,256]{1,0:T(8,128)(2,1)S(1)} %constant_dynamic-update-slice_fusion.own_ref.refs_0_.refs_4_), channel_id=1, source_target_pairs={{0,8},{8,0},{16,24},{24,16},{1,9},{9,1},{17,25},{25,17},{2,10},{10... | collective-permute-start | bytes 884744 | tf_op jit(solution)/shard_map/ppermute | solution.py:517
  18.9 5.8 %copy-start = (f32[256,16384]{1,0:T(8,128)S(1)}, f32[256,16384]{1,0:T(8,128)}, u32[]{:S(2)}) copy-start(f32[256,16384]{1,0:T(8,128)} %refs_4_.3) | copy-start | bytes 50331652
  24.7 0.8 copy-start.3
  25.5 40.6 %copy-start.4 = (f32[16384]{0:T(1024)S(1)}, f32[16384]{0:T(1024)}, u32[]{:S(2)}) copy-start(f32[16384]{0:T(1024)} %param.17) | copy-start | bytes 196612
  47.3 15.1 %collective-permute-start.7 = (bf16[576,256]{1,0:T(8,128)(2,1)S(1)}, bf16[576,256]{1,0:T(8,128)(2,1)S(1)}, u32[]{:S(2)}, u32[]{:S(2)}) collective-permute-start(bf16[576,256]{1,0:T(8,128)(2,1)S(1)} %collective-permute-done.4.refs_2_), channel_id=1, source_target_pairs={{0,1},{1,0},{2,3},{3,2},{4,5},{5,4},{6,7},{7,6},{8,9},{9,8},{10,11... | collective-permute-start | bytes 884744 | tf_op jit(solution)/shard_map/ppermute | solution.py:514
  47.3 15.6 %collective-permute-start.8 = (bf16[576,256]{1,0:T(8,128)(2,1)S(1)}, bf16[576,256]{1,0:T(8,128)(2,1)S(1)}, u32[]{:S(2)}, u32[]{:S(2)}) collective-permute-start(bf16[576,256]{1,0:T(8,128)(2,1)S(1)} %collective-permute-done.5.refs_4_), channel_id=1, source_target_pairs={{0,1},{1,0},{2,3},{3,2},{4,5},{5,4},{6,7},{7,6},{8,9},{9,8},{10,11... | collective-permute-start | bytes 884744 | tf_op jit(solution)/shard_map/ppermute | solution.py:514
  47.8 15.1 %collective-permute-start.9 = (bf16[576,256]{1,0:T(8,128)(2,1)S(1)}, bf16[576,256]{1,0:T(8,128)(2,1)S(1)}, u32[]{:S(2)}, u32[]{:S(2)}) collective-permute-start(bf16[576,256]{1,0:T(8,128)(2,1)S(1)} %collective-permute-done.6.refs_6_), channel_id=1, source_target_pairs={{0,1},{1,0},{2,3},{3,2},{4,5},{5,4},{6,7},{7,6},{8,9},{9,8},{10,11... | collective-permute-start | bytes 884744 | tf_op jit(solution)/shard_map/ppermute | solution.py:514
  47.9 1.9 %collective-permute-start.10 = (f32[8,512]{1,0:T(8,128)S(1)}, f32[8,512]{1,0:T(8,128)S(1)}, u32[]{:S(2)}, u32[]{:S(2)}) collective-permute-start(f32[8,512]{1,0:T(8,128)S(1)} %first_pass.1.own_ref), channel_id=1, source_target_pairs={{0,1},{1,0},{2,3},{3,2},{4,5},{5,4},{6,7},{7,6},{8,9},{9,8},{10,11... | collective-permute-start | bytes 49160 | tf_op jit(solution)/shard_map/ppermute | solution.py:514
  49.8 5.6 %collective-permute-start.13 = (f32[8,512]{1,0:T(8,128)S(1)}, f32[8,512]{1,0:T(8,128)S(1)}, u32[]{:S(2)}, u32[]{:S(2)}) collective-permute-start(f32[8,512]{1,0:T(8,128)S(1)} %core_join.1.refs_0_), channel_id=1, source_target_pairs={{0,6},{1,7},{2,4},{3,5},{4,2},{5,3},{6,0},{7,1},{8,14},{9,15},{10,... | collective-permute-start | bytes 49160 | tf_op jit(solution)/shard_map/ppermute | solution.py:514
  52.6 4.7 %collective-permute-start.12 = (f32[8,512]{1,0:T(8,128)S(1)}, f32[8,512]{1,0:T(8,128)S(1)}, u32[]{:S(2)}, u32[]{:S(2)}) collective-permute-start(f32[8,512]{1,0:T(8,128)S(1)} %core_join.1.refs_0_), channel_id=1, source_target_pairs={{0,4},{1,5},{2,6},{3,7},{4,0},{5,1},{6,2},{7,3},{8,12},{9,13},{10,... | collective-permute-start | bytes 49160 | tf_op jit(solution)/shard_map/ppermute | solution.py:514
  55.4 3.7 %collective-permute-start.11 = (f32[8,512]{1,0:T(8,128)S(1)}, f32[8,512]{1,0:T(8,128)S(1)}, u32[]{:S(2)}, u32[]{:S(2)}) collective-permute-start(f32[8,512]{1,0:T(8,128)S(1)} %core_join.1.refs_0_), channel_id=1, source_target_pairs={{0,2},{1,3},{2,0},{3,1},{4,6},{5,7},{6,4},{7,5},{8,10},{9,11},{10,... | collective-permute-start | bytes 49160 | tf_op jit(solution)/shard_map/ppermute | solution.py:514
  59.4 4.7 %collective-permute-start.16 = (f32[8,512]{1,0:T(8,128)S(1)}, f32[8,512]{1,0:T(8,128)S(1)}, u32[]{:S(2)}, u32[]{:S(2)}) collective-permute-start(f32[8,512]{1,0:T(8,128)S(1)} %get-tuple-element.64.refs_0_), channel_id=1, source_target_pairs={{0,24},{8,16},{16,8},{24,0},{1,25},{9,17},{17,9},{25,1},{2,26},{10... | collective-permute-start | bytes 49160 | tf_op jit(solution)/shard_map/ppermute | solution.py:517
  61.8 3.7 %collective-permute-start.15 = (f32[8,512]{1,0:T(8,128)S(1)}, f32[8,512]{1,0:T(8,128)S(1)}, u32[]{:S(2)}, u32[]{:S(2)}) collective-permute-start(f32[8,512]{1,0:T(8,128)S(1)} %get-tuple-element.64.refs_0_), channel_id=1, source_target_pairs={{0,16},{8,24},{16,0},{24,8},{1,17},{9,25},{17,1},{25,9},{2,18},{10... | collective-permute-start | bytes 49160 | tf_op jit(solution)/shard_map/ppermute | solution.py:517
  62.4 3.7 %collective-permute-start.14 = (f32[8,512]{1,0:T(8,128)S(1)}, f32[8,512]{1,0:T(8,128)S(1)}, u32[]{:S(2)}, u32[]{:S(2)}) collective-permute-start(f32[8,512]{1,0:T(8,128)S(1)} %get-tuple-element.64.refs_0_), channel_id=1, source_target_pairs={{0,8},{8,0},{16,24},{24,16},{1,9},{9,1},{17,25},{25,17},{2,10},{10... | collective-permute-start | bytes 49160 | tf_op jit(solution)/shard_map/ppermute | solution.py:517
  80.0 17.8 %collective-permute-start.17 = (bf16[64,2048]{1,0:T(8,128)(2,1)S(1)}, bf16[64,2048]{1,0:T(8,128)(2,1)S(1)}, u32[]{:S(2)}, u32[]{:S(2)}) collective-permute-start(bf16[64,2048]{1,0:T(8,128)(2,1)S(1)} %get-tuple-element.70), channel_id=1, source_target_pairs={{0,8},{8,0},{16,24},{24,16},{1,9},{9,1},{17,25},{25,17},{2,10},{10... | collective-permute-start | bytes 786440 | tf_op jit(solution)/shard_map/ppermute | solution.py:517
  80.6 17.2 %collective-permute-start.18 = (bf16[64,2048]{1,0:T(8,128)(2,1)S(1)}, bf16[64,2048]{1,0:T(8,128)(2,1)S(1)}, u32[]{:S(2)}, u32[]{:S(2)}) collective-permute-start(bf16[64,2048]{1,0:T(8,128)(2,1)S(1)} %get-tuple-element.71), channel_id=1, source_target_pairs={{0,16},{8,24},{16,0},{24,8},{1,17},{9,25},{17,1},{25,9},{2,18},{10... | collective-permute-start | bytes 786440 | tf_op jit(solution)/shard_map/ppermute | solution.py:517
  82.1 15.7 %collective-permute-start.19 = (bf16[64,2048]{1,0:T(8,128)(2,1)S(1)}, bf16[64,2048]{1,0:T(8,128)(2,1)S(1)}, u32[]{:S(2)}, u32[]{:S(2)}) collective-permute-start(bf16[64,2048]{1,0:T(8,128)(2,1)S(1)} %get-tuple-element.72), channel_id=1, source_target_pairs={{0,24},{8,16},{16,8},{24,0},{1,25},{9,17},{17,9},{25,1},{2,26},{10... | collective-permute-start | bytes 786440 | tf_op jit(solution)/shard_map/ppermute | solution.py:517
  83.6 36.7 %slice-start = ((s8[16777216]{0:T(1024)(128)(4,1)}), s8[4194304]{0:T(1024)(128)(4,1)S(1)}, s32[]{:S(2)}) async-start(s8[16777216]{0:T(1024)(128)(4,1)} %bitcast.6), calls=%async_computation | async-start | bytes 8388608
  83.6 36.7 %slice-start.1 = ((s8[16777216]{0:T(1024)(128)(4,1)}), s8[4194304]{0:T(1024)(128)(4,1)S(1)}, s32[]{:S(2)}) async-start(s8[16777216]{0:T(1024)(128)(4,1)} %bitcast.6), calls=%async_computation.1 | async-start | bytes 8388608
  83.6 36.7 %slice-start.2 = ((s8[16777216]{0:T(1024)(128)(4,1)}), s8[4194304]{0:T(1024)(128)(4,1)S(1)}, s32[]{:S(2)}) async-start(s8[16777216]{0:T(1024)(128)(4,1)} %bitcast.6), calls=%async_computation.2 | async-start | bytes 8388608
  83.6 36.7 %slice-start.3 = ((s8[16777216]{0:T(1024)(128)(4,1)}), s8[4194304]{0:T(1024)(128)(4,1)S(1)}, s32[]{:S(2)}) async-start(s8[16777216]{0:T(1024)(128)(4,1)} %bitcast.6), calls=%async_computation.3 | async-start | bytes 8388608
  83.6 36.7 %copy-start.1 = (f32[64,16384]{1,0:T(8,128)S(1)}, f32[64,16384]{1,0:T(8,128)}, u32[]{:S(2)}) copy-start(f32[64,16384]{1,0:T(8,128)} %refs_6_.3) | copy-start | bytes 12582916
  97.9 2.0 %collective-permute-start.20 = (bf16[1024,256]{1,0:T(8,128)(2,1)S(1)}, bf16[1024,256]{1,0:T(8,128)(2,1)S(1)}, u32[]{:S(2)}, u32[]{:S(2)}) collective-permute-start(bf16[1024,256]{1,0:T(8,128)(2,1)S(1)} %get-tuple-element.73), channel_id=1, source_target_pairs={{0,1},{1,0},{2,3},{3,2},{4,5},{5,4},{6,7},{7,6},{8,9},{9,8},{10,11... | collective-permute-start | bytes 1572872 | tf_op jit(solution)/shard_map/ppermute | solution.py:514
  98.0 1.9 %collective-permute-start.21 = (f32[8,128]{1,0:T(8,128)S(1)}, f32[8,128]{1,0:T(8,128)S(1)}, u32[]{:S(2)}, u32[]{:S(2)}) collective-permute-start(f32[8,128]{1,0:T(8,128)S(1)} %sub.3.loss_ref), channel_id=1, source_target_pairs={{0,1},{1,0},{2,3},{3,2},{4,5},{5,4},{6,7},{7,6},{8,9},{9,8},{10,11... | collective-permute-start | bytes 12296 | tf_op jit(solution)/shard_map/ppermute | solution.py:514
  100.0 6.8 %collective-permute-start.22 = (bf16[272,256]{1,0:T(8,128)(2,1)S(1)}, bf16[272,256]{1,0:T(8,128)(2,1)S(1)}, u32[]{:S(2)}, u32[]{:S(2)}) collective-permute-start(bf16[272,256]{1,0:T(8,128)(2,1)S(1)} %get-tuple-element.78), channel_id=1, source_target_pairs={{0,2},{1,3},{2,0},{3,1},{4,6},{5,7},{6,4},{7,5},{8,10},{9,11},{10,... | collective-permute-start | bytes 417800 | tf_op jit(solution)/shard_map/ppermute | solution.py:514
  100.1 18.8 %collective-permute-start.28 = (bf16[64,2048]{1,0:T(8,128)(2,1)S(1)}, bf16[64,2048]{1,0:T(8,128)(2,1)S(1)}, u32[]{:S(2)}, u32[]{:S(2)}) collective-permute-start(bf16[64,2048]{1,0:T(8,128)(2,1)S(1)} %get-tuple-element.90), channel_id=1, source_target_pairs={{0,8},{8,0},{16,24},{24,16},{1,9},{9,1},{17,25},{25,17},{2,10},{10... | collective-permute-start | bytes 786440 | tf_op jit(solution)/shard_map/ppermute | solution.py:517
  100.7 27.9 %collective-permute-start.29 = (bf16[64,2048]{1,0:T(8,128)(2,1)S(1)}, bf16[64,2048]{1,0:T(8,128)(2,1)S(1)}, u32[]{:S(2)}, u32[]{:S(2)}) collective-permute-start(bf16[64,2048]{1,0:T(8,128)(2,1)S(1)} %get-tuple-element.91), channel_id=1, source_target_pairs={{0,16},{8,24},{16,0},{24,8},{1,17},{9,25},{17,1},{25,9},{2,18},{10... | collective-permute-start | bytes 786440 | tf_op jit(solution)/shard_map/ppermute | solution.py:517
  102.2 26.4 %collective-permute-start.30 = (bf16[64,2048]{1,0:T(8,128)(2,1)S(1)}, bf16[64,2048]{1,0:T(8,128)(2,1)S(1)}, u32[]{:S(2)}, u32[]{:S(2)}) collective-permute-start(bf16[64,2048]{1,0:T(8,128)(2,1)S(1)} %get-tuple-element.92), channel_id=1, source_target_pairs={{0,24},{8,16},{16,8},{24,0},{1,25},{9,17},{17,9},{25,1},{2,26},{10... | collective-permute-start | bytes 786440 | tf_op jit(solution)/shard_map/ppermute | solution.py:517
  103.6 13.0 %collective-permute-start.23 = (bf16[272,256]{1,0:T(8,128)(2,1)S(1)}, bf16[272,256]{1,0:T(8,128)(2,1)S(1)}, u32[]{:S(2)}, u32[]{:S(2)}) collective-permute-start(bf16[272,256]{1,0:T(8,128)(2,1)S(1)} %get-tuple-element.79), channel_id=1, source_target_pairs={{0,4},{1,5},{2,6},{3,7},{4,0},{5,1},{6,2},{7,3},{8,12},{9,13},{10,... | collective-permute-start | bytes 417800 | tf_op jit(solution)/shard_map/ppermute | solution.py:514
  106.8 9.8 %collective-permute-start.24 = (bf16[272,256]{1,0:T(8,128)(2,1)S(1)}, bf16[272,256]{1,0:T(8,128)(2,1)S(1)}, u32[]{:S(2)}, u32[]{:S(2)}) collective-permute-start(bf16[272,256]{1,0:T(8,128)(2,1)S(1)} %get-tuple-element.80), channel_id=1, source_target_pairs={{0,6},{1,7},{2,4},{3,5},{4,2},{5,3},{6,0},{7,1},{8,14},{9,15},{10,... | collective-permute-start | bytes 417800 | tf_op jit(solution)/shard_map/ppermute | solution.py:514
  116.7 18.1 %collective-permute-start.25 = (bf16[80,256]{1,0:T(8,128)(2,1)S(1)}, bf16[80,256]{1,0:T(8,128)(2,1)S(1)}, u32[]{:S(2)}, u32[]{:S(2)}) collective-permute-start(bf16[80,256]{1,0:T(8,128)(2,1)S(1)} %get-tuple-element.85), channel_id=1, source_target_pairs={{0,8},{8,0},{16,24},{24,16},{1,9},{9,1},{17,25},{25,17},{2,10},{10... | collective-permute-start | bytes 122888 | tf_op jit(solution)/shard_map/ppermute | solution.py:517
  117.3 17.4 %collective-permute-start.26 = (bf16[80,256]{1,0:T(8,128)(2,1)S(1)}, bf16[80,256]{1,0:T(8,128)(2,1)S(1)}, u32[]{:S(2)}, u32[]{:S(2)}) collective-permute-start(bf16[80,256]{1,0:T(8,128)(2,1)S(1)} %get-tuple-element.86), channel_id=1, source_target_pairs={{0,16},{8,24},{16,0},{24,8},{1,17},{9,25},{17,1},{25,9},{2,18},{10... | collective-permute-start | bytes 122888 | tf_op jit(solution)/shard_map/ppermute | solution.py:517
  118.9 15.9 %collective-permute-start.27 = (bf16[80,256]{1,0:T(8,128)(2,1)S(1)}, bf16[80,256]{1,0:T(8,128)(2,1)S(1)}, u32[]{:S(2)}, u32[]{:S(2)}) collective-permute-start(bf16[80,256]{1,0:T(8,128)(2,1)S(1)} %get-tuple-element.87), channel_id=1, source_target_pairs={{0,24},{8,16},{16,8},{24,0},{1,25},{9,17},{17,9},{25,1},{2,26},{10... | collective-permute-start | bytes 122888 | tf_op jit(solution)/shard_map/ppermute | solution.py:517
  120.3 2.2 %copy-start.2 = (f32[64,16384]{1,0:T(8,128)S(1)}, f32[64,16384]{1,0:T(8,128)}, u32[]{:S(2)}) copy-start(f32[64,16384]{1,0:T(8,128)} %refs_7_.3) | copy-start | bytes 12582916

commit v3 on v2

--- a/solution.py
+++ b/solution.py
@@ -21,6 +21,8 @@
 
 log2_e = 1.4426950408889634
 ln_2 = 0.6931471805599453
+least = 2.0**-60
+most = 2.0**120
 scale_s = log2_e / student_temp
 scale_t = log2_e / teacher_temp
 
@@ -82,81 +84,108 @@
             jax.ShapeDtypeStruct((count, width), f32),
             jax.ShapeDtypeStruct((count, 128), f32),
         ],
-        compiler_params=params(8),
+        compiler_params=params(56),
         cost_estimate=cost(0, 1 << 20),
         name="pick_rows",
     )(rows, image, student, teacher)
 
 
+def round_kernel(s_ref, t_ref, out_s, out_t):
+    out_s[...] = s_ref[...].astype(bf16)
+    out_t[...] = t_ref[...].astype(bf16)
+
+
+def round_protos(student, teacher):
+    width, cols = student.shape
+    tile = min(cols, 2048)
+    column = pl.BlockSpec((width, tile), lambda j: (0, j))
+    return pl.pallas_call(
+        round_kernel,
+        grid=(cols // tile,),
+        in_specs=[column] * 2,
+        out_specs=[column] * 2,
+        out_shape=[jax.ShapeDtypeStruct((width, cols), bf16)] * 2,
+        compiler_params=params(24),
+        cost_estimate=cost(0, 12 * width * cols),
+        name="round_protos",
+    )(student, teacher)
+
+
 def first_kernel(own_ref, other_ref, ws_ref, wt_ref, centre_ref, out_ref, us, ut, ms, ss, mt, st, *, count):
-    step = pl.program_id(0)
     pack = 2 * count + PAD
     rows = us.shape[0]
     half = rows // 2
     cols = ws_ref.shape[1]
-
-    @pl.when(step == 0)
-    def _():
-        for c, ref in enumerate((own_ref, other_ref)):
-            for z in range(half // count):
-                at = c * half + z * count
-                us[at : at + count, :] = ref[z * pack : z * pack + count, :]
-                ut[at : at + count, :] = ref[z * pack + count : z * pack + 2 * count, :]
-        for m, s in ((ms, ss), (mt, st)):
-            m[...] = jnp.full_like(m, -jnp.inf)
-            s[...] = jnp.zeros_like(s)
-
-    def update(parts, m_ref, s_ref, at):
+    for c, ref in enumerate((own_ref, other_ref)):
+        for z in range(half // count):
+            at = c * half + z * count
+            us[at : at + count, :] = ref[z * pack : z * pack + count, :]
+            ut[at : at + count, :] = ref[z * pack + count : z * pack + 2 * count, :]
+
+    block = min(rows, 512)
+    tile = min(cols, 1024)
+    unroll = 2 if cols % (2 * tile) == 0 else 1
+
+    def sweep(update):
+        @pl.loop(0, cols // (tile * unroll))
+        def _(j):
+            for u in range(unroll):
+                span = pl.ds(pl.multiple_of((j * unroll + u) * tile, tile), tile)
+                ws = ws_ref[:, span]
+                wt = wt_ref[:, span]
+                shift = centre_ref[:, span] * scale_t
+                for r in range(rows // block):
+                    at = slice(r * block, (r + 1) * block)
+                    zs = jnp.dot(us[at, :], ws, preferred_element_type=f32)
+                    update([zs[:, i : i + 128] * scale_s for i in range(0, tile, 128)], ms, ss, at)
+                    zt = jnp.dot(ut[at, :], wt, preferred_element_type=f32)
+                    update([zt[:, i : i + 128] * scale_t - shift[:, i : i + 128] for i in range(0, tile, 128)], mt, st, at)
+
+    def plain(parts, m_ref, s_ref, at):
+        s_ref[at, :] += functools.reduce(jnp.add, [jnp.exp2(part) for part in parts])
+
+    def running(parts, m_ref, s_ref, at):
         old = m_ref[at, :]
         new = functools.reduce(jnp.maximum, parts, old)
         total = functools.reduce(jnp.add, [jnp.exp2(part - new) for part in parts])
         s_ref[at, :] = s_ref[at, :] * jnp.exp2(old - new) + total
         m_ref[at, :] = new
 
-    block = min(rows, 512)
-    tile = min(cols, 1024)
-    for t in range(cols // tile):
-        span = slice(t * tile, (t + 1) * tile)
-        ws = ws_ref[:, span].astype(bf16)
-        wt = wt_ref[:, span].astype(bf16)
-        shift = centre_ref[:, span] * scale_t
-        for r in range(rows // block):
-            at = slice(r * block, (r + 1) * block)
-            zs = jnp.dot(us[at, :], ws, preferred_element_type=f32)
-            update([zs[:, i : i + 128] * scale_s for i in range(0, tile, 128)], ms, ss, at)
-            zt = jnp.dot(ut[at, :], wt, preferred_element_type=f32)
-            update([zt[:, i : i + 128] * scale_t - shift[:, i : i + 128] for i in range(0, tile, 128)], mt, st, at)
-
-    @pl.when(step == pl.num_programs(0) - 1)
+    for m, s in ((ms, ss), (mt, st)):
+        m[...] = jnp.zeros_like(m)
+        s[...] = jnp.zeros_like(s)
+    sweep(plain)
+    far = jnp.zeros((rows, 1), f32)
+    for s in (ss, st):
+        total = jnp.sum(s[...], axis=1, keepdims=True)
+        far = jnp.maximum(far, jnp.where((total > least) & (total < most), 0.0, 1.0))
+
+    @pl.when(jnp.max(far) > 0.5)
     def _():
-        out_ref[...] = jnp.zeros_like(out_ref)
-        for k, (m, s) in enumerate(((ms, ss), (mt, st))):
-            lanes = m[...]
-            peak = jnp.max(lanes, axis=1, keepdims=True)
-            total = jnp.sum(s[...] * jnp.exp2(lanes - peak), axis=1, keepdims=True)
-            lse = jnp.broadcast_to(peak + jnp.log2(total), lanes.shape)
-            out_ref[k : k + 1, :] = jnp.transpose(lse)[0:1, :]
+        for m, s in ((ms, ss), (mt, st)):
+            m[...] = jnp.full_like(m, -jnp.inf)
+            s[...] = jnp.zeros_like(s)
+        sweep(running)
+
+    out_ref[...] = jnp.zeros_like(out_ref)
+    for k, (m, s) in enumerate(((ms, ss), (mt, st))):
+        lanes = m[...]
+        peak = jnp.max(lanes, axis=1, keepdims=True)
+        total = jnp.sum(s[...] * jnp.exp2(lanes - peak), axis=1, keepdims=True)
+        lse = jnp.broadcast_to(peak + jnp.log2(total), lanes.shape)
+        out_ref[k : k + 1, :] = jnp.transpose(lse)[0:1, :]
 
 
 def first_pass(own, other, ws, wt, centre, count):
     width, cols = ws.shape
     rows = 2 * own.shape[0] // (2 * count + PAD) * count
-    tile = min(cols, 2048)
     return pl.pallas_call(
         functools.partial(first_kernel, count=count),
-        grid=(cols // tile,),
-        in_specs=[
-            whole(own.shape),
-            whole(other.shape),
-            pl.BlockSpec((width, tile), lambda j: (0, j)),
-            pl.BlockSpec((width, tile), lambda j: (0, j)),
-            pl.BlockSpec((1, tile), lambda j: (0, j)),
-        ],
-        out_specs=whole((8, rows)),
+        in_specs=[pl.BlockSpec(memory_space=pltpu.VMEM)] * 5,
         out_shape=jax.ShapeDtypeStruct((8, rows), f32),
         scratch_shapes=[pltpu.VMEM((rows, width), bf16)] * 2 + [pltpu.VMEM((rows, 128), f32)] * 4,
-        compiler_params=params(24),
-        cost_estimate=cost(4 * rows * width * cols, 8 * width * cols),
+        compiler_params=params(10),
+        cost_estimate=cost(4 * rows * width * cols, 4 * width * cols),
         name="first_pass",
     )(own, other, ws, wt, centre)
 
@@ -235,117 +264,107 @@
     )(slab, *packs)
 
 
-def second_kernel(place_ref, us, ut, flipped, ws_ref, wt_ref, centre_ref, *refs, groups, first, last, count):
-    stats = refs[:groups]
-    refs = refs[groups:]
-    if first:
-        carry_ref = seed_ref = None
-    else:
-        carry_ref, seed_ref = refs[:2]
-        refs = refs[2:]
+def second_kernel(us, ut, flipped, ws_ref, wt_ref, centre_ref, *refs, groups, index, chunk, last, count):
+    stats, refs = refs[:groups], refs[groups:]
+    if index:
+        (carry_ref, seed_ref), refs = refs[:2], refs[2:]
     grads, refs = refs[:groups], refs[groups:]
     if last:
         keep_ref, send_ref, loss_ref, total, loss_sum, shift_s, shift_t = refs
     else:
         total, loss_ref, loss_sum, shift_s, shift_t = refs
-    step = pl.program_id(0)
     rows, width = us.shape
     group_rows = rows // groups
-    tile = ws_ref.shape[1]
-
-    @pl.when(step == 0)
-    def _():
-        total[...] = jnp.zeros_like(total) if first else carry_ref[...]
-        loss_sum[...] = jnp.zeros_like(loss_sum)
+    slab = width // groups
+    total[...] = carry_ref[...] if index else jnp.zeros_like(total)
+    loss_sum[...] = jnp.zeros_like(loss_sum)
+    for g in range(groups):
+        at = slice(g * group_rows, (g + 1) * group_rows)
+        for k, shift in enumerate((shift_s, shift_t)):
+            shift[at, :] = jnp.transpose(jnp.broadcast_to(stats[g][k : k + 1, :], (128, group_rows)))
+
+    tile = min(chunk, 512)
+    block = min(group_rows, 256)
+    places = [slice(r * block, (r + 1) * block) for r in range(rows // block)]
+
+    @pl.loop(0, chunk // tile)
+    def _(j):
+        span = pl.ds(pl.multiple_of(index * chunk + j * tile, tile), tile)
+        ws = ws_ref[:, span]
+        wt = wt_ref[:, span]
+        centre = centre_ref[:, span] * scale_t
+
+        def products(at):
+            return (
+                jnp.dot(us[at, :], ws, preferred_element_type=f32),
+                jnp.dot(ut[at, :], wt, preferred_element_type=f32),
+            )
+
+        ready = products(places[0])
+        grad = None
+        for r, at in enumerate(places):
+            zs, zt = ready
+            if r + 1 < len(places):
+                ready = products(places[r + 1])
+            down_s, down_t = shift_s[at, :], shift_t[at, :]
+            parts = []
+            loss = None
+            for i in range(0, tile, 128):
+                zsi = zs[:, i : i + 128]
+                ps = jnp.exp2(zsi * scale_s - down_s)
+                pt = jnp.exp2(zt[:, i : i + 128] * scale_t - centre[:, i : i + 128] - down_t)
+                cross = pt * zsi
+                loss = cross if loss is None else loss + cross
+                parts.append((ps - pt).astype(bf16))
+            loss_sum[...] += jnp.sum(loss.reshape(block // 8, 8, 128), axis=0)
+            logit = jnp.concatenate(parts, axis=1)
+            total[at, :] += lax.dot_general(logit, ws, (((1,), (1,)), ((), ())), preferred_element_type=f32)
+            part = jnp.dot(flipped[:, at], logit, preferred_element_type=f32)
+            grad = part if grad is None else grad + part
+        out = pl.ds(pl.multiple_of(j * tile, tile), tile)
+        for k in range(groups):
+            grads[k][:, out] = grad[k * slab : (k + 1) * slab, :].astype(bf16)
+
+    done = jnp.sum(jnp.sum(loss_sum[...], axis=1, keepdims=True), axis=0, keepdims=True)
+    loss = jnp.broadcast_to(done, loss_ref.shape)
+    loss_ref[...] = loss + seed_ref[...] if index else loss
+    if last:
+        depth = group_rows // (2 * count)
         for g in range(groups):
-            at = slice(g * group_rows, (g + 1) * group_rows)
-            for k, shift in enumerate((shift_s, shift_t)):
-                line = jnp.broadcast_to(stats[g][k : k + 1, :], (128, group_rows))
-                shift[at, :] = jnp.transpose(line)
-
-    ws = ws_ref[...].astype(bf16)
-    wt = wt_ref[...].astype(bf16)
-    centre = centre_ref[...] * scale_t
-    block = min(group_rows, 512)
-    grad = None
-    for r in range(rows // block):
-        at = slice(r * block, (r + 1) * block)
-        zs = jnp.dot(us[at, :], ws, preferred_element_type=f32)
-        zt = jnp.dot(ut[at, :], wt, preferred_element_type=f32)
-        as_, at_ = shift_s[at, :], shift_t[at, :]
-        parts = []
-        loss = None
-        for i in range(0, tile, 128):
-            zsi = zs[:, i : i + 128]
-            ps = jnp.exp2(zsi * scale_s - as_)
-            pt = jnp.exp2(zt[:, i : i + 128] * scale_t - centre[:, i : i + 128] - at_)
-            cross = pt * zsi
-            loss = cross if loss is None else loss + cross
-            parts.append((ps - pt).astype(bf16))
-        loss_sum[...] += jnp.sum(loss.reshape(block // 8, 8, 128), axis=0)
-        logit = jnp.concatenate(parts, axis=1)
-        total[at, :] += lax.dot_general(logit, ws, (((1,), (1,)), ((), ())), preferred_element_type=f32)
-        part = jnp.dot(flipped[:, at], logit, preferred_element_type=f32)
-        grad = part if grad is None else grad + part
-    slab = width // groups
-    for k in range(groups):
-        grads[k][...] = grad[k * slab : (k + 1) * slab, :].astype(bf16)
-
-    @pl.when(step == pl.num_programs(0) - 1)
-    def _():
-        done = jnp.sum(jnp.sum(loss_sum[...], axis=1, keepdims=True), axis=0, keepdims=True)
-        loss = jnp.broadcast_to(done, loss_ref.shape)
-        if not first:
-            loss += seed_ref[...]
-        loss_ref[...] = loss
-        if last:
-            zs_count = group_rows // (2 * count)
-            for g in range(groups):
-                for c, ref in enumerate((keep_ref, send_ref)):
-                    for z in range(zs_count):
-                        src = g * group_rows + (c * zs_count + z) * count
-                        dst = (z * groups + g) * count
-                        ref[dst : dst + count, :] = total[src : src + count, :].astype(ref.dtype)
-
-
-def second_pass(place, us, ut, flipped, ws, wt, centre, stats, carry, index, chunks, share, count):
+            for c, ref in enumerate((keep_ref, send_ref)):
+                for z in range(depth):
+                    src = g * group_rows + (c * depth + z) * count
+                    dst = (z * groups + g) * count
+                    ref[dst : dst + count, :] = total[src : src + count, :].astype(ref.dtype)
+
+
+def second_pass(us, ut, flipped, ws, wt, centre, stats, carry, index, chunks, count):
     rows, width = us.shape
     groups = len(stats)
     slab = width // groups
-    chunk = share // chunks
-    tile = min(chunk, 512)
-    steps = chunk // tile
-    first, last = index == 0, index == chunks - 1
-    column = lambda j, place_ref: (0, place_ref[0] * (share // tile) + index * steps + j)
-    in_specs = [whole(us.shape), whole(ut.shape), whole(flipped.shape)]
-    in_specs += [pl.BlockSpec((width, tile), column)] * 2 + [pl.BlockSpec((1, tile), column)]
-    in_specs += [whole(stats[0].shape)] * groups
+    chunk = ws.shape[1] // chunks
+    last = index == chunks - 1
     args = [us, ut, flipped, ws, wt, centre, *stats]
-    if not first:
-        in_specs += [whole(carry[0].shape), whole(carry[1].shape)]
+    if index:
         args += list(carry)
-    out_specs = [pl.BlockSpec((slab, tile), lambda j, place_ref: (0, j))] * groups
     out_shape = [jax.ShapeDtypeStruct((slab, chunk), bf16)] * groups
     scratch = [pltpu.VMEM((8, 128), f32)] + [pltpu.VMEM((rows, 128), f32)] * 2
     if last:
-        out_specs += [whole((rows // 2, width))] * 2
         out_shape += [jax.ShapeDtypeStruct((rows // 2, width), f32), jax.ShapeDtypeStruct((rows // 2, width), bf16)]
         scratch = [pltpu.VMEM((rows, width), f32)] + scratch
     else:
-        out_specs += [whole((rows, width))]
         out_shape += [jax.ShapeDtypeStruct((rows, width), f32)]
-    out_specs += [whole((8, 128))]
     out_shape += [jax.ShapeDtypeStruct((8, 128), f32)]
-    return pl.pallas_call(
-        functools.partial(second_kernel, groups=groups, first=first, last=last, count=count),
-        grid_spec=pltpu.PrefetchScalarGridSpec(
-            num_scalar_prefetch=1, grid=(steps,), in_specs=in_specs, out_specs=out_specs, scratch_shapes=scratch
-        ),
+    held = 2 * rows * 128 * 4 + rows * width * 4
+    return pl.pallas_call(
+        functools.partial(second_kernel, groups=groups, index=index, chunk=chunk, last=last, count=count),
+        in_specs=[pl.BlockSpec(memory_space=pltpu.VMEM)] * len(args),
         out_shape=out_shape,
-        compiler_params=params(32),
+        scratch_shapes=scratch,
+        compiler_params=params((held >> 20) + 8),
         cost_estimate=cost(8 * rows * width * chunk, 8 * width * chunk),
         name="second_pass",
-    )(place, *args)
+    )(*args)
 
 
 def pieces(value):
@@ -517,18 +536,14 @@
         return lax.ppermute(x, "dp", xor_pairs(groups, k))
 
     pack, raw, inv = pick_rows(masked_rows, patch_image, student_patch[0], teacher_patch[0])
-    own = jnp.concatenate([pack] + [proto_swap(pack, k) for k in range(2, protos, 2)], axis=0)
+    near = [proto_swap(pack, k) for k in range(2, protos, 2)]
+    ws, wt = round_protos(student_proto, teacher_proto)
+    near, ws, wt = lax.optimization_barrier((near, ws, wt))
+    own = jnp.concatenate([pack] + near, axis=0)
     other = proto_swap(own, 1)
     far = [dp_swap(own, k) for k in range(1, groups)]
 
-    stats = first_pass(own, other, student_proto, teacher_proto, centre, count)
-    stats, *far = lax.optimization_barrier((stats, *far))
-    far_other = [proto_swap(x, 1) for x in far]
-    packs = [own, other]
-    for pair in zip(far, far_other):
-        packs += list(pair)
-    us, ut, flipped = lay_rows(place, packs, count)
-
+    stats = first_pass(own, other, ws, wt, centre, count)
     stats = pl.pallas_call(
         core_join_kernel,
         out_shape=jax.ShapeDtypeStruct(stats.shape, f32),
@@ -536,6 +551,14 @@
         cost_estimate=cost(0, 1 << 20),
         name="core_join",
     )(stats, proto_swap(stats, 1))
+    stats, ws, wt, *far = lax.optimization_barrier((stats, ws, wt, *far))
+    far_other = [proto_swap(x, 1) for x in far]
+    packs = [own, other]
+    for pair in zip(far, far_other):
+        packs += list(pair)
+    us, ut, flipped = lay_rows(place, packs, count)
+
+    own_ws, own_wt, own_centre = [lax.dynamic_slice_in_dim(x, place[0] * share, share, 1) for x in (ws, wt, centre)]
     stats, loss_own = pl.pallas_call(
         functools.partial(final_join_kernel, count=count, images=images, ratio=ratio),
         out_shape=[jax.ShapeDtypeStruct(stats.shape, f32), jax.ShapeDtypeStruct((8, 128), f32)],
@@ -548,19 +571,27 @@
     carry = None
     sent = []
     for index in range(CHUNKS):
-        out = second_pass(
-            place, us, ut, flipped, student_proto, teacher_proto, centre, all_stats, carry, index, CHUNKS, share, count
-        )
+        out = second_pass(us, ut, flipped, own_ws, own_wt, own_centre, all_stats, carry, index, CHUNKS, count)
         grads, carry = out[:groups], out[groups:]
         sent.append([grads[0]] + [dp_swap(grads[k], k) for k in range(1, groups)])
     keep, send, cross = carry
     send, sent[:-1] = lax.optimization_barrier((send, sent[:-1]))
     loss = loss_own - cross
 
-    zs_count = protos // 2
-    out = core_sum(keep, proto_swap(send, 1), loss, proto_swap(loss, 1), zs_count)
-    out = axis_sum(out[0], out[-1], [proto_swap(out[k], 2 * k) for k in range(1, zs_count)], groups)
+    depth = protos // 2
+    out = core_sum(keep, proto_swap(send, 1), loss, proto_swap(loss, 1), depth)
+    got = [proto_swap(out[k], 2 * k) for k in range(1, depth)]
+    done = None
+    for index in range(CHUNKS - 1):
+        done = optimizer(
+            place, sent[index], student_proto, teacher_proto, first_moment, second_moment, done, index, CHUNKS, share
+        )
+    got, done = lax.optimization_barrier((got, done))
+    out = axis_sum(out[0], out[-1], got, groups)
     got = [dp_swap(out[k], k) for k in range(1, groups)]
+    done = optimizer(
+        place, sent[-1], student_proto, teacher_proto, first_moment, second_moment, done, CHUNKS - 1, CHUNKS, share
+    )
     row_grad, total = pl.pallas_call(
         functools.partial(row_kernel, sources=len(got), rows_total=rows_total),
         out_shape=[jax.ShapeDtypeStruct((count, width), f32), jax.ShapeDtypeStruct((8, 128), f32)],
@@ -568,12 +599,6 @@
         cost_estimate=cost(0, 1 << 20),
         name="row_grad",
     )(out[0], out[-1], raw, inv, *got)
-
-    done = None
-    for index in range(CHUNKS):
-        done = optimizer(
-            place, sent[index], student_proto, teacher_proto, first_moment, second_moment, done, index, CHUNKS, share
-        )
     new_student, new_first, new_second, new_teacher = done
     return (row_grad[None], new_student, new_first, new_second, new_teacher, total[0, 0])
 

time: 137 us -> 126 us (0.920)
  starting transfers between devices: 32.9 us -> 48.5 us
  waiting for transfers between devices: 25.9 us -> 10.3 us
  local copies, waits for them, and re-layouts: 12.3 us -> 3.3 us
  Pallas kernels: 64.1 us -> 62.6 us
    ppermute x16, starting transfers between devices: 15.2 us -> 30.9 us  [proto_swap(): return lax.ppermute(x, 'proto', xor_pairs(protos, k))]
    ppermute x16, waiting for transfers between devices: 23.1 us -> 8.95 us  [proto_swap(): return lax.ppermute(x, 'proto', xor_pairs(protos, k))]
    unnamed x29 -> x27, local copies, waits for them, and re-layouts: 11.8 us -> 0.07 us
    pallas_call x3 -> x4, Pallas kernels: 49.8 us -> 46.8 us  [the longest x2 23.4 us: second_pass(): pl.pallas_call(functools.partial(second_kernel, groups=groups, index=inde...]
    dynamic_slice x0 -> x1, local copies, waits for them, and re-layouts: none -> 2.71 us  [local(): lax.dynamic_slice_in_dim(x, place[0] * share, share, 1)]
    pallas_call x1, Pallas kernels: 0.29 us -> 1.84 us  [pick_rows(): pl.pallas_call(pick_kernel, out_shape=[jax.ShapeDtypeStruct((2 * count +...]
    ppermute x15, waiting for transfers between devices: 2.74 us -> 1.37 us  [dp_swap(): return lax.ppermute(x, 'dp', xor_pairs(groups, k))]
  transfers between devices with their start and end apart: 31 -> 31, of which waited for: 11 -> 9; matrix products, arithmetic and copies ran while one was open for 0% -> 2% of each run, Pallas kernels for 36% -> 38%
where the time goes in v3:
time: 126 us
  Pallas kernels  62.6 us (50%)
  starting transfers between devices  48.5 us (38%)
  waiting for transfers between devices  10.3 us (8%)
  local copies, waits for them, and re-layouts  3.3 us (3%)
    ppermute x16, starting transfers between devices, proto_swap(): return lax.ppermute(x, 'proto', xor_pairs(protos, k))  30.9 us
    pallas_call x2, Pallas kernels, second_pass(): pl.pallas_call(functools.partial(second_kernel, groups=groups, index=inde...  23.4 us
    ppermute x15, starting transfers between devices, dp_swap(): return lax.ppermute(x, 'dp', xor_pairs(groups, k))  17.6 us
    pallas_call x2, Pallas kernels, optimizer(): pl.pallas_call(functools.partial(step_kernel, groups=groups), grid_spec=p...  12.3 us
    pallas_call x1, Pallas kernels, round_protos(): pl.pallas_call(round_kernel, grid=(cols // tile,), in_specs=[column] * 2,...  12.2 us
    pallas_call x1, Pallas kernels, first_pass(): pl.pallas_call(functools.partial(first_kernel, count=count), in_specs=[pl...  11.2 us
    ppermute x16, waiting for transfers between devices, proto_swap(): return lax.ppermute(x, 'proto', xor_pairs(protos, k))  8.95 us
    dynamic_slice x1, local copies, waits for them, and re-layouts, local(): lax.dynamic_slice_in_dim(x, place[0] * share, share, 1)  2.71 us
  transfers between devices with their start and end apart: 31, of which 9 were waited for; matrix products, arithmetic and copies ran while one was open for 2% of the time, Pallas kernels for 38%

profile of v3, /device:TPU:0, one launch (start us, length us, event | category | flops | bytes accessed | tf_op | source)
XLA Modules:
  0.0 125.7 jit_solution(2450865477952695691)
XLA Ops:
  0.6 1.8 %pick_rows.1 = (bf16[144,256]{1,0:T(8,128)(2,1)}, f32[64,256]{1,0:T(8,128)}, f32[64,128]{1,0:T(8,128)}) custom-call(s32[1,64]{1,0:T(1,128)} %rows_ref.1, s32[1,128]{1,0:T(1,128)} %image_ref.1, bf16[128,256]{1,0:T(8,128)(2,1)} %bitcast.12, bf16[128,256]{1,0:T(8,128)(2,1)} %bitcast.13), custom_call_target="tpu_custom_call" | custom-call | bytes 1048576 | tf_op jit(solution)/shard_map/pick_rows/pallas_call | solution.py:80
  2.5 5.0 %collective-permute-start.2 = (bf16[144,256]{1,0:T(8,128)(2,1)}, bf16[144,256]{1,0:T(8,128)(2,1)S(1)}, u32[]{:S(2)}, u32[]{:S(2)}) collective-permute-start(bf16[144,256]{1,0:T(8,128)(2,1)} %get-tuple-element.72), channel_id=1, source_target_pairs={{0,6},{1,7},{2,4},{3,5},{4,2},{5,3},{6,0},{7,1},{8,14},{9,15},{10,... | collective-permute-start | bytes 221192 | tf_op jit(solution)/shard_map/ppermute | solution.py:533
  7.5 0.0 collective-permute-start.1
  7.5 0.6 collective-permute-start
  8.2 12.2 %round_protos.1 = (bf16[256,16384]{1,0:T(8,128)(2,1)S(1)}, bf16[256,16384]{1,0:T(8,128)(2,1)S(1)}) custom-call(f32[256,16384]{1,0:T(8,128)} %refs_4_.3, f32[256,16384]{1,0:T(8,128)} %refs_5_.3), custom_call_target="tpu_custom_call" | custom-call | bytes 50331648 | tf_op jit(solution)/shard_map/round_protos/pallas_call | solution.py:102
  20.4 0.0 collective-permute-done.2
  20.4 0.0 collective-permute-done.1
  20.4 0.0 collective-permute-done
  20.5 0.1 collective-permute-start.3
  20.6 2.7 %collective-permute-start.7 = (bf16[576,256]{1,0:T(8,128)(2,1)S(1)}, bf16[576,256]{1,0:T(8,128)(2,1)S(1)}, u32[]{:S(2)}, u32[]{:S(2)}) collective-permute-start(bf16[576,256]{1,0:T(8,128)(2,1)S(1)} %constant_dynamic-update-slice_fusion.own_ref.refs_0_.refs_4_), channel_id=1, source_target_pairs={{0,24},{8,16},{16,8},{24,0},{1,25},{9,17},{17,9},{25,1},{2,26},{10... | collective-permute-start | bytes 884744 | tf_op jit(solution)/shard_map/ppermute | solution.py:536
  23.2 0.5 collective-permute-start.6
  23.7 0.4 collective-permute-start.5
  24.1 11.2 %first_pass.1.own_ref = f32[8,512]{1,0:T(8,128)S(1)} custom-call(bf16[576,256]{1,0:T(8,128)(2,1)S(1)} %constant_dynamic-update-slice_fusion.own_ref.refs_0_.refs_4_, bf16[576,256]{1,0:T(8,128)(2,1)S(1)} %collective-permute-done.3.other_ref.refs_1_.refs_5_, bf16[256,16384]{1,0:T(8,128)(2,1)S(1)} %get-tuple-element.86.ws_ref, ...), custom_call_target="tpu_custom_call" | custom-call | flops 8589934592 | bytes 16777216 | tf_op jit(solution)/shard_map/first_pass/pallas_call | solution.py:182
  35.3 0.1 collective-permute-start.4
  35.4 1.2 collective-permute-done.4.other_ref
  36.6 0.0 collective-permute-done.7.refs_6_
  36.6 0.6 collective-permute-done.6.refs_4_
  37.2 0.2 collective-permute-done.5.refs_2_
  37.5 3.6 %collective-permute-start.13 = (f32[8,512]{1,0:T(8,128)S(1)}, f32[8,512]{1,0:T(8,128)S(1)}, u32[]{:S(2)}, u32[]{:S(2)}) collective-permute-start(f32[8,512]{1,0:T(8,128)S(1)} %core_join.1.refs_0_), channel_id=1, source_target_pairs={{0,6},{1,7},{2,4},{3,5},{4,2},{5,3},{6,0},{7,1},{8,14},{9,15},{10,... | collective-permute-start | bytes 49160 | tf_op jit(solution)/shard_map/ppermute | solution.py:533
  41.1 16.5 %collective-permute-start.12 = (f32[8,512]{1,0:T(8,128)S(1)}, f32[8,512]{1,0:T(8,128)S(1)}, u32[]{:S(2)}, u32[]{:S(2)}) collective-permute-start(f32[8,512]{1,0:T(8,128)S(1)} %core_join.1.refs_0_), channel_id=1, source_target_pairs={{0,4},{1,5},{2,6},{3,7},{4,0},{5,1},{6,2},{7,3},{8,12},{9,13},{10,... | collective-permute-start | bytes 49160 | tf_op jit(solution)/shard_map/ppermute | solution.py:533
  57.6 0.0 collective-permute-start.11
  57.6 0.0 collective-permute-done.13.refs_3_
  57.6 0.5 collective-permute-start.10
  58.1 1.5 %collective-permute-done.12.refs_2_ = f32[8,512]{1,0:T(8,128)S(1)} collective-permute-done((f32[8,512]{1,0:T(8,128)S(1)}, f32[8,512]{1,0:T(8,128)S(1)}, u32[]{:S(2)}, u32[]{:S(2)}) %collective-permute-start.12) | collective-permute-done | bytes 16416 | tf_op jit(solution)/shard_map/ppermute | solution.py:533
  59.7 1.7 %collective-permute-done.11.refs_1_ = f32[8,512]{1,0:T(8,128)S(1)} collective-permute-done((f32[8,512]{1,0:T(8,128)S(1)}, f32[8,512]{1,0:T(8,128)S(1)}, u32[]{:S(2)}, u32[]{:S(2)}) %collective-permute-start.11) | collective-permute-done | bytes 16416 | tf_op jit(solution)/shard_map/ppermute | solution.py:533
  61.3 0.2 final_join.1
  61.6 0.0 collective-permute-start.16
  61.6 3.5 %collective-permute-start.15 = (f32[8,512]{1,0:T(8,128)S(1)}, f32[8,512]{1,0:T(8,128)S(1)}, u32[]{:S(2)}, u32[]{:S(2)}) collective-permute-start(f32[8,512]{1,0:T(8,128)S(1)} %get-tuple-element.89.refs_0_), channel_id=1, source_target_pairs={{0,16},{8,24},{16,0},{24,8},{1,17},{9,25},{17,1},{25,9},{2,18},{10... | collective-permute-start | bytes 49160 | tf_op jit(solution)/shard_map/ppermute | solution.py:536
  65.1 2.7 %constant_dynamic-slice_fusion = (bf16[256,4096]{1,0:T(8,128)(2,1)S(1)}, bf16[256,4096]{1,0:T(8,128)(2,1)S(1)}) fusion(bf16[256,16384]{1,0:T(8,128)(2,1)} %copy-done.3, s32[]{:T(128)S(6)} %select_n.2, bf16[256,16384]{1,0:T(8,128)(2,1)} %copy-done.2), kind=kLoop, calls=%fused_computation.4 | loop fusion | bytes 8388612 | tf_op jit(solution)/shard_map/dynamic_slice | solution.py:561
  67.8 0.0 collective-permute-done.9.refs_5_
  67.8 0.5 lay_rows.1
  68.3 0.0 collective-permute-done.15.refs_2_
  68.4 0.5 collective-permute-done.14.refs_1_
  68.8 11.8 %second_pass.2 = (bf16[64,2048]{1,0:T(8,128)(2,1)S(1)}, bf16[64,2048]{1,0:T(8,128)(2,1)S(1)}, bf16[64,2048]{1,0:T(8,128)(2,1)S(1)}, bf16[64,2048]{1,0:T(8,128)(2...) custom-call(bf16[2048,256]{1,0:T(8,128)(2,1)S(1)} %get-tuple-element.83.us, ...), custom_call_target="tpu_custom_call" | custom-call | flops 8589934592 | bytes 4194304 | tf_op jit(solution)/shard_map/second_pass/pallas_call | solution.py:359
  80.6 1.6 %collective-permute-start.17 = (bf16[64,2048]{1,0:T(8,128)(2,1)S(1)}, bf16[64,2048]{1,0:T(8,128)(2,1)S(1)}, u32[]{:S(2)}, u32[]{:S(2)}) collective-permute-start(bf16[64,2048]{1,0:T(8,128)(2,1)S(1)} %get-tuple-element.95), channel_id=1, source_target_pairs={{0,8},{8,0},{16,24},{24,16},{1,9},{9,1},{17,25},{25,17},{2,10},{10... | collective-permute-start | bytes 786440 | tf_op jit(solution)/shard_map/ppermute | solution.py:536
  82.2 0.0 collective-permute-start.18
  82.2 2.0 %collective-permute-start.19 = (bf16[64,2048]{1,0:T(8,128)(2,1)S(1)}, bf16[64,2048]{1,0:T(8,128)(2,1)S(1)}, u32[]{:S(2)}, u32[]{:S(2)}) collective-permute-start(bf16[64,2048]{1,0:T(8,128)(2,1)S(1)} %get-tuple-element.97), channel_id=1, source_target_pairs={{0,24},{8,16},{16,8},{24,0},{1,25},{9,17},{17,9},{25,1},{2,26},{10... | collective-permute-start | bytes 786440 | tf_op jit(solution)/shard_map/ppermute | solution.py:536
  84.1 0.0 copy-start
  84.1 0.0 copy-start.1
  84.2 11.6 %second_pass.3 = (bf16[64,2048]{1,0:T(8,128)(2,1)S(1)}, bf16[64,2048]{1,0:T(8,128)(2,1)S(1)}, bf16[64,2048]{1,0:T(8,128)(2,1)S(1)}, bf16[64,2048]{1,0:T(8,128)(2...) custom-call(bf16[2048,256]{1,0:T(8,128)(2,1)S(1)} %get-tuple-element.83.us, ...), custom_call_target="tpu_custom_call" | custom-call | flops 8589934592 | bytes 4194304 | tf_op jit(solution)/shard_map/second_pass/pallas_call | solution.py:359
  95.8 0.0 collective-permute-done.18.refs_2_
  95.8 0.0 collective-permute-done.19.refs_3_
  95.8 0.1 collective-permute-start.20
  95.9 0.5 collective-permute-start.21
  96.4 1.4 %collective-permute-done.21.other_ref = f32[8,128]{1,0:T(8,128)S(1)} collective-permute-done((f32[8,128]{1,0:T(8,128)S(1)}, f32[8,128]{1,0:T(8,128)S(1)}, u32[]{:S(2)}, u32[]{:S(2)}) %collective-permute-start.21) | collective-permute-done | bytes 4128 | tf_op jit(solution)/shard_map/ppermute | solution.py:533
  97.8 0.1 core_sum.1
  97.9 0.7 collective-permute-start.22
  98.7 1.0 collective-permute-start.28
  99.7 1.5 %collective-permute-start.29 = (bf16[64,2048]{1,0:T(8,128)(2,1)S(1)}, bf16[64,2048]{1,0:T(8,128)(2,1)S(1)}, u32[]{:S(2)}, u32[]{:S(2)}) collective-permute-start(bf16[64,2048]{1,0:T(8,128)(2,1)S(1)} %get-tuple-element.127), channel_id=1, source_target_pairs={{0,16},{8,24},{16,0},{24,8},{1,17},{9,25},{17,1},{25,9},{2,18},{10... | collective-permute-start | bytes 786440 | tf_op jit(solution)/shard_map/ppermute | solution.py:536
  101.2 1.0 collective-permute-start.30
  102.2 0.9 collective-permute-start.23
  103.1 0.6 collective-permute-done.22.refs_0_
  103.7 2.2 %collective-permute-start.24 = (bf16[272,256]{1,0:T(8,128)(2,1)S(1)}, bf16[272,256]{1,0:T(8,128)(2,1)S(1)}, u32[]{:S(2)}, u32[]{:S(2)}) collective-permute-start(bf16[272,256]{1,0:T(8,128)(2,1)S(1)} %get-tuple-element.105), channel_id=1, source_target_pairs={{0,6},{1,7},{2,4},{3,5},{4,2},{5,3},{6,0},{7,1},{8,14},{9,15},{10,... | collective-permute-start | bytes 417800 | tf_op jit(solution)/shard_map/ppermute | solution.py:533
  105.9 6.2 %optimizer.2 = (f32[64,16384]{1,0:T(8,128)}, f32[64,16384]{1,0:T(8,128)}, f32[64,16384]{1,0:T(8,128)}, f32[64,16384]{1,0:T(8,128)}) custom-call(s32[1]{0:T(128)} %bitcast.slab_ref.place_ref, bf16[64,2048]{1,0:T(8,128)(2,1)S(1)} %get-tuple-element.106.refs_0_, bf16[64,2048]{1,0:T(8,128)(2,1)S(1)} %collective-permute-done.17.refs_1_, ...), custom_call_target="tpu_custom_call" | custom-call | flops 10485760 | bytes 17825792 | tf_op jit(solution)/shard_map/optimizer/pallas_call | solution.py:496
  112.1 2.5 %collective-permute-done.23.refs_1_ = bf16[272,256]{1,0:T(8,128)(2,1)S(1)} collective-permute-done((bf16[272,256]{1,0:T(8,128)(2,1)S(1)}, bf16[272,256]{1,0:T(8,128)(2,1)S(1)}, u32[]{:S(2)}, u32[]{:S(2)}) %collective-permute-start.23) | collective-permute-done | bytes 139296 | tf_op jit(solution)/shard_map/ppermute | solution.py:533
  114.6 0.1 axis_sum.1
  114.7 1.6 %collective-permute-start.25 = (bf16[80,256]{1,0:T(8,128)(2,1)S(1)}, bf16[80,256]{1,0:T(8,128)(2,1)S(1)}, u32[]{:S(2)}, u32[]{:S(2)}) collective-permute-start(bf16[80,256]{1,0:T(8,128)(2,1)S(1)} %get-tuple-element.121), channel_id=1, source_target_pairs={{0,8},{8,0},{16,24},{24,16},{1,9},{9,1},{17,25},{25,17},{2,10},{10... | collective-permute-start | bytes 122888 | tf_op jit(solution)/shard_map/ppermute | solution.py:536
  116.3 0.3 collective-permute-start.26
  116.6 0.0 collective-permute-done.28.refs_1_
  116.6 1.7 %collective-permute-start.27 = (bf16[80,256]{1,0:T(8,128)(2,1)S(1)}, bf16[80,256]{1,0:T(8,128)(2,1)S(1)}, u32[]{:S(2)}, u32[]{:S(2)}) collective-permute-start(bf16[80,256]{1,0:T(8,128)(2,1)S(1)} %get-tuple-element.123), channel_id=1, source_target_pairs={{0,24},{8,16},{16,8},{24,0},{1,25},{9,17},{17,9},{25,1},{2,26},{10... | collective-permute-start | bytes 122888 | tf_op jit(solution)/shard_map/ppermute | solution.py:536
  118.2 6.2 %optimizer.3 = (f32[64,16384]{1,0:T(8,128)}, f32[64,16384]{1,0:T(8,128)}, f32[64,16384]{1,0:T(8,128)}, f32[64,16384]{1,0:T(8,128)}) custom-call(s32[1]{0:T(128)} %bitcast.slab_ref.place_ref, bf16[64,2048]{1,0:T(8,128)(2,1)S(1)} %get-tuple-element.125.refs_0_, ...), custom_call_target="tpu_custom_call", output_to_operand_aliasing={{0}: (9, {}), {1}: (10, {}), {2}: (11, {}), {3}: (12, {})} | custom-call | flops 10485760 | bytes 17825792 | tf_op jit(solution)/shard_map/optimizer/pallas_call | solution.py:496
  124.4 0.0 collective-permute-done.27.refs_2_
  124.4 0.8 row_grad.1
  125.2 0.5 slice.3
  (44 shorter events, 0.1 us)
Async XLA Ops:
  2.5 17.9 %copy-start.7 = (bf16[144,256]{1,0:T(8,128)(2,1)S(1)}, bf16[144,256]{1,0:T(8,128)(2,1)}, u32[]{:S(2)}) copy-start(bf16[144,256]{1,0:T(8,128)(2,1)} %get-tuple-element.72) | copy-start | bytes 221188
  2.5 21.6 %copy-start.6 = (f32[16384]{0:T(1024)S(1)}, f32[16384]{0:T(1024)}, u32[]{:S(2)}) copy-start(f32[16384]{0:T(1024)} %param.17) | copy-start | bytes 196612
  2.5 17.9 %collective-permute-start.2 = (bf16[144,256]{1,0:T(8,128)(2,1)}, bf16[144,256]{1,0:T(8,128)(2,1)S(1)}, u32[]{:S(2)}, u32[]{:S(2)}) collective-permute-start(bf16[144,256]{1,0:T(8,128)(2,1)} %get-tuple-element.72), channel_id=1, source_target_pairs={{0,6},{1,7},{2,4},{3,5},{4,2},{5,3},{6,0},{7,1},{8,14},{9,15},{10,... | collective-permute-start | bytes 221192 | tf_op jit(solution)/shard_map/ppermute | solution.py:533
  7.5 12.9 %collective-permute-start.1 = (bf16[144,256]{1,0:T(8,128)(2,1)}, bf16[144,256]{1,0:T(8,128)(2,1)S(1)}, u32[]{:S(2)}, u32[]{:S(2)}) collective-permute-start(bf16[144,256]{1,0:T(8,128)(2,1)} %get-tuple-element.72), channel_id=1, source_target_pairs={{0,4},{1,5},{2,6},{3,7},{4,0},{5,1},{6,2},{7,3},{8,12},{9,13},{10,... | collective-permute-start | bytes 221192 | tf_op jit(solution)/shard_map/ppermute | solution.py:533
  7.5 12.9 %collective-permute-start = (bf16[144,256]{1,0:T(8,128)(2,1)}, bf16[144,256]{1,0:T(8,128)(2,1)S(1)}, u32[]{:S(2)}, u32[]{:S(2)}) collective-permute-start(bf16[144,256]{1,0:T(8,128)(2,1)} %get-tuple-element.72), channel_id=1, source_target_pairs={{0,2},{1,3},{2,0},{3,1},{4,6},{5,7},{6,4},{7,5},{8,10},{9,11},{10,... | collective-permute-start | bytes 221192 | tf_op jit(solution)/shard_map/ppermute | solution.py:533
  20.4 14.9 %copy-start.2 = (bf16[256,16384]{1,0:T(8,128)(2,1)}, bf16[256,16384]{1,0:T(8,128)(2,1)S(1)}, u32[]{:S(2)}) copy-start(bf16[256,16384]{1,0:T(8,128)(2,1)S(1)} %get-tuple-element.86.ws_ref) | copy-start | bytes 25165828
  20.4 14.9 %copy-start.3 = (bf16[256,16384]{1,0:T(8,128)(2,1)}, bf16[256,16384]{1,0:T(8,128)(2,1)S(1)}, u32[]{:S(2)}) copy-start(bf16[256,16384]{1,0:T(8,128)(2,1)S(1)} %get-tuple-element.87.wt_ref) | copy-start | bytes 25165828
  20.5 3.6 %collective-permute-start.3 = (bf16[576,256]{1,0:T(8,128)(2,1)S(1)}, bf16[576,256]{1,0:T(8,128)(2,1)S(1)}, u32[]{:S(2)}, u32[]{:S(2)}) collective-permute-start(bf16[576,256]{1,0:T(8,128)(2,1)S(1)} %constant_dynamic-update-slice_fusion.own_ref.refs_0_.refs_4_), channel_id=1, source_target_pairs={{0,1},{1,0},{2,3},{3,2},{4,5},{5,4},{6,7},{7,6},{8,9},{9,8},{10,11... | collective-permute-start | bytes 884744 | tf_op jit(solution)/shard_map/ppermute | solution.py:533
  20.6 16.0 %collective-permute-start.7 = (bf16[576,256]{1,0:T(8,128)(2,1)S(1)}, bf16[576,256]{1,0:T(8,128)(2,1)S(1)}, u32[]{:S(2)}, u32[]{:S(2)}) collective-permute-start(bf16[576,256]{1,0:T(8,128)(2,1)S(1)} %constant_dynamic-update-slice_fusion.own_ref.refs_0_.refs_4_), channel_id=1, source_target_pairs={{0,24},{8,16},{16,8},{24,0},{1,25},{9,17},{17,9},{25,1},{2,26},{10... | collective-permute-start | bytes 884744 | tf_op jit(solution)/shard_map/ppermute | solution.py:536
  23.2 14.0 %collective-permute-start.6 = (bf16[576,256]{1,0:T(8,128)(2,1)S(1)}, bf16[576,256]{1,0:T(8,128)(2,1)S(1)}, u32[]{:S(2)}, u32[]{:S(2)}) collective-permute-start(bf16[576,256]{1,0:T(8,128)(2,1)S(1)} %constant_dynamic-update-slice_fusion.own_ref.refs_0_.refs_4_), channel_id=1, source_target_pairs={{0,16},{8,24},{16,0},{24,8},{1,17},{9,25},{17,1},{25,9},{2,18},{10... | collective-permute-start | bytes 884744 | tf_op jit(solution)/shard_map/ppermute | solution.py:536
  23.7 13.7 %collective-permute-start.5 = (bf16[576,256]{1,0:T(8,128)(2,1)S(1)}, bf16[576,256]{1,0:T(8,128)(2,1)S(1)}, u32[]{:S(2)}, u32[]{:S(2)}) collective-permute-start(bf16[576,256]{1,0:T(8,128)(2,1)S(1)} %constant_dynamic-update-slice_fusion.own_ref.refs_0_.refs_4_), channel_id=1, source_target_pairs={{0,8},{8,0},{16,24},{24,16},{1,9},{9,1},{17,25},{25,17},{2,10},{10... | collective-permute-start | bytes 884744 | tf_op jit(solution)/shard_map/ppermute | solution.py:536
  35.3 1.3 collective-permute-start.4
  37.5 27.7 %collective-permute-start.8 = (bf16[576,256]{1,0:T(8,128)(2,1)S(1)}, bf16[576,256]{1,0:T(8,128)(2,1)S(1)}, u32[]{:S(2)}, u32[]{:S(2)}) collective-permute-start(bf16[576,256]{1,0:T(8,128)(2,1)S(1)} %collective-permute-done.5.refs_2_), channel_id=1, source_target_pairs={{0,1},{1,0},{2,3},{3,2},{4,5},{5,4},{6,7},{7,6},{8,9},{9,8},{10,11... | collective-permute-start | bytes 884744 | tf_op jit(solution)/shard_map/ppermute | solution.py:533
  37.5 20.2 %collective-permute-start.13 = (f32[8,512]{1,0:T(8,128)S(1)}, f32[8,512]{1,0:T(8,128)S(1)}, u32[]{:S(2)}, u32[]{:S(2)}) collective-permute-start(f32[8,512]{1,0:T(8,128)S(1)} %core_join.1.refs_0_), channel_id=1, source_target_pairs={{0,6},{1,7},{2,4},{3,5},{4,2},{5,3},{6,0},{7,1},{8,14},{9,15},{10,... | collective-permute-start | bytes 49160 | tf_op jit(solution)/shard_map/ppermute | solution.py:533
  41.1 18.6 %collective-permute-start.12 = (f32[8,512]{1,0:T(8,128)S(1)}, f32[8,512]{1,0:T(8,128)S(1)}, u32[]{:S(2)}, u32[]{:S(2)}) collective-permute-start(f32[8,512]{1,0:T(8,128)S(1)} %core_join.1.refs_0_), channel_id=1, source_target_pairs={{0,4},{1,5},{2,6},{3,7},{4,0},{5,1},{6,2},{7,3},{8,12},{9,13},{10,... | collective-permute-start | bytes 49160 | tf_op jit(solution)/shard_map/ppermute | solution.py:533
  57.6 3.7 %collective-permute-start.11 = (f32[8,512]{1,0:T(8,128)S(1)}, f32[8,512]{1,0:T(8,128)S(1)}, u32[]{:S(2)}, u32[]{:S(2)}) collective-permute-start(f32[8,512]{1,0:T(8,128)S(1)} %core_join.1.refs_0_), channel_id=1, source_target_pairs={{0,2},{1,3},{2,0},{3,1},{4,6},{5,7},{6,4},{7,5},{8,10},{9,11},{10,... | collective-permute-start | bytes 49160 | tf_op jit(solution)/shard_map/ppermute | solution.py:533
  57.6 10.2 %collective-permute-start.9 = (bf16[576,256]{1,0:T(8,128)(2,1)S(1)}, bf16[576,256]{1,0:T(8,128)(2,1)S(1)}, u32[]{:S(2)}, u32[]{:S(2)}) collective-permute-start(bf16[576,256]{1,0:T(8,128)(2,1)S(1)} %collective-permute-done.6.refs_4_), channel_id=1, source_target_pairs={{0,1},{1,0},{2,3},{3,2},{4,5},{5,4},{6,7},{7,6},{8,9},{9,8},{10,11... | collective-permute-start | bytes 884744 | tf_op jit(solution)/shard_map/ppermute | solution.py:533
  57.6 10.2 %collective-permute-start.10 = (bf16[576,256]{1,0:T(8,128)(2,1)S(1)}, bf16[576,256]{1,0:T(8,128)(2,1)S(1)}, u32[]{:S(2)}, u32[]{:S(2)}) collective-permute-start(bf16[576,256]{1,0:T(8,128)(2,1)S(1)} %collective-permute-done.7.refs_6_), channel_id=1, source_target_pairs={{0,1},{1,0},{2,3},{3,2},{4,5},{5,4},{6,7},{7,6},{8,9},{9,8},{10,11... | collective-permute-start | bytes 884744 | tf_op jit(solution)/shard_map/ppermute | solution.py:533
  61.6 6.8 %collective-permute-start.16 = (f32[8,512]{1,0:T(8,128)S(1)}, f32[8,512]{1,0:T(8,128)S(1)}, u32[]{:S(2)}, u32[]{:S(2)}) collective-permute-start(f32[8,512]{1,0:T(8,128)S(1)} %get-tuple-element.89.refs_0_), channel_id=1, source_target_pairs={{0,24},{8,16},{16,8},{24,0},{1,25},{9,17},{17,9},{25,1},{2,26},{10... | collective-permute-start | bytes 49160 | tf_op jit(solution)/shard_map/ppermute | solution.py:536
  61.6 6.7 %collective-permute-start.15 = (f32[8,512]{1,0:T(8,128)S(1)}, f32[8,512]{1,0:T(8,128)S(1)}, u32[]{:S(2)}, u32[]{:S(2)}) collective-permute-start(f32[8,512]{1,0:T(8,128)S(1)} %get-tuple-element.89.refs_0_), channel_id=1, source_target_pairs={{0,16},{8,24},{16,0},{24,8},{1,17},{9,25},{17,1},{25,9},{2,18},{10... | collective-permute-start | bytes 49160 | tf_op jit(solution)/shard_map/ppermute | solution.py:536
  65.1 3.7 %collective-permute-start.14 = (f32[8,512]{1,0:T(8,128)S(1)}, f32[8,512]{1,0:T(8,128)S(1)}, u32[]{:S(2)}, u32[]{:S(2)}) collective-permute-start(f32[8,512]{1,0:T(8,128)S(1)} %get-tuple-element.89.refs_0_), channel_id=1, source_target_pairs={{0,8},{8,0},{16,24},{24,16},{1,9},{9,1},{17,25},{25,17},{2,10},{10... | collective-permute-start | bytes 49160 | tf_op jit(solution)/shard_map/ppermute | solution.py:536
  80.6 15.2 %collective-permute-start.17 = (bf16[64,2048]{1,0:T(8,128)(2,1)S(1)}, bf16[64,2048]{1,0:T(8,128)(2,1)S(1)}, u32[]{:S(2)}, u32[]{:S(2)}) collective-permute-start(bf16[64,2048]{1,0:T(8,128)(2,1)S(1)} %get-tuple-element.95), channel_id=1, source_target_pairs={{0,8},{8,0},{16,24},{24,16},{1,9},{9,1},{17,25},{25,17},{2,10},{10... | collective-permute-start | bytes 786440 | tf_op jit(solution)/shard_map/ppermute | solution.py:536
  82.2 13.6 %collective-permute-start.18 = (bf16[64,2048]{1,0:T(8,128)(2,1)S(1)}, bf16[64,2048]{1,0:T(8,128)(2,1)S(1)}, u32[]{:S(2)}, u32[]{:S(2)}) collective-permute-start(bf16[64,2048]{1,0:T(8,128)(2,1)S(1)} %get-tuple-element.96), channel_id=1, source_target_pairs={{0,16},{8,24},{16,0},{24,8},{1,17},{9,25},{17,1},{25,9},{2,18},{10... | collective-permute-start | bytes 786440 | tf_op jit(solution)/shard_map/ppermute | solution.py:536
  82.2 13.6 %collective-permute-start.19 = (bf16[64,2048]{1,0:T(8,128)(2,1)S(1)}, bf16[64,2048]{1,0:T(8,128)(2,1)S(1)}, u32[]{:S(2)}, u32[]{:S(2)}) collective-permute-start(bf16[64,2048]{1,0:T(8,128)(2,1)S(1)} %get-tuple-element.97), channel_id=1, source_target_pairs={{0,24},{8,16},{16,8},{24,0},{1,25},{9,17},{17,9},{25,1},{2,26},{10... | collective-permute-start | bytes 786440 | tf_op jit(solution)/shard_map/ppermute | solution.py:536
  84.1 21.8 %slice-start = ((s8[16777216]{0:T(1024)(128)(4,1)}), s8[4194304]{0:T(1024)(128)(4,1)S(1)}, s32[]{:S(2)}) async-start(s8[16777216]{0:T(1024)(128)(4,1)} %bitcast.7), calls=%async_computation | async-start | bytes 8388608
  84.1 21.8 %slice-start.1 = ((s8[16777216]{0:T(1024)(128)(4,1)}), s8[4194304]{0:T(1024)(128)(4,1)S(1)}, s32[]{:S(2)}) async-start(s8[16777216]{0:T(1024)(128)(4,1)} %bitcast.7), calls=%async_computation.1 | async-start | bytes 8388608
  84.1 21.8 %slice-start.2 = ((s8[16777216]{0:T(1024)(128)(4,1)}), s8[4194304]{0:T(1024)(128)(4,1)S(1)}, s32[]{:S(2)}) async-start(s8[16777216]{0:T(1024)(128)(4,1)} %bitcast.7), calls=%async_computation.2 | async-start | bytes 8388608
  84.1 21.8 %slice-start.3 = ((s8[16777216]{0:T(1024)(128)(4,1)}), s8[4194304]{0:T(1024)(128)(4,1)S(1)}, s32[]{:S(2)}) async-start(s8[16777216]{0:T(1024)(128)(4,1)} %bitcast.7), calls=%async_computation.3 | async-start | bytes 8388608
  84.1 21.8 %copy-start = (f32[64,16384]{1,0:T(8,128)S(1)}, f32[64,16384]{1,0:T(8,128)}, u32[]{:S(2)}) copy-start(f32[64,16384]{1,0:T(8,128)} %refs_6_.3) | copy-start | bytes 12582916
  84.1 21.8 %copy-start.1 = (f32[64,16384]{1,0:T(8,128)S(1)}, f32[64,16384]{1,0:T(8,128)}, u32[]{:S(2)}) copy-start(f32[64,16384]{1,0:T(8,128)} %refs_7_.3) | copy-start | bytes 12582916
  95.8 2.0 %collective-permute-start.20 = (bf16[1024,256]{1,0:T(8,128)(2,1)S(1)}, bf16[1024,256]{1,0:T(8,128)(2,1)S(1)}, u32[]{:S(2)}, u32[]{:S(2)}) collective-permute-start(bf16[1024,256]{1,0:T(8,128)(2,1)S(1)} %get-tuple-element.98), channel_id=1, source_target_pairs={{0,1},{1,0},{2,3},{3,2},{4,5},{5,4},{6,7},{7,6},{8,9},{9,8},{10,11... | collective-permute-start | bytes 1572872 | tf_op jit(solution)/shard_map/ppermute | solution.py:533
  95.9 1.9 %collective-permute-start.21 = (f32[8,128]{1,0:T(8,128)S(1)}, f32[8,128]{1,0:T(8,128)S(1)}, u32[]{:S(2)}, u32[]{:S(2)}) collective-permute-start(f32[8,128]{1,0:T(8,128)S(1)} %sub.3.loss_ref), channel_id=1, source_target_pairs={{0,1},{1,0},{2,3},{3,2},{4,5},{5,4},{6,7},{7,6},{8,9},{9,8},{10,11... | collective-permute-start | bytes 12296 | tf_op jit(solution)/shard_map/ppermute | solution.py:533
  97.9 5.8 %collective-permute-start.22 = (bf16[272,256]{1,0:T(8,128)(2,1)S(1)}, bf16[272,256]{1,0:T(8,128)(2,1)S(1)}, u32[]{:S(2)}, u32[]{:S(2)}) collective-permute-start(bf16[272,256]{1,0:T(8,128)(2,1)S(1)} %get-tuple-element.103), channel_id=1, source_target_pairs={{0,2},{1,3},{2,0},{3,1},{4,6},{5,7},{6,4},{7,5},{8,10},{9,11},{10,... | collective-permute-start | bytes 417800 | tf_op jit(solution)/shard_map/ppermute | solution.py:533
  98.7 17.9 %collective-permute-start.28 = (bf16[64,2048]{1,0:T(8,128)(2,1)S(1)}, bf16[64,2048]{1,0:T(8,128)(2,1)S(1)}, u32[]{:S(2)}, u32[]{:S(2)}) collective-permute-start(bf16[64,2048]{1,0:T(8,128)(2,1)S(1)} %get-tuple-element.126), channel_id=1, source_target_pairs={{0,8},{8,0},{16,24},{24,16},{1,9},{9,1},{17,25},{25,17},{2,10},{10... | collective-permute-start | bytes 786440 | tf_op jit(solution)/shard_map/ppermute | solution.py:536
  99.7 18.5 %collective-permute-start.29 = (bf16[64,2048]{1,0:T(8,128)(2,1)S(1)}, bf16[64,2048]{1,0:T(8,128)(2,1)S(1)}, u32[]{:S(2)}, u32[]{:S(2)}) collective-permute-start(bf16[64,2048]{1,0:T(8,128)(2,1)S(1)} %get-tuple-element.127), channel_id=1, source_target_pairs={{0,16},{8,24},{16,0},{24,8},{1,17},{9,25},{17,1},{25,9},{2,18},{10... | collective-permute-start | bytes 786440 | tf_op jit(solution)/shard_map/ppermute | solution.py:536
  101.2 17.0 %collective-permute-start.30 = (bf16[64,2048]{1,0:T(8,128)(2,1)S(1)}, bf16[64,2048]{1,0:T(8,128)(2,1)S(1)}, u32[]{:S(2)}, u32[]{:S(2)}) collective-permute-start(bf16[64,2048]{1,0:T(8,128)(2,1)S(1)} %get-tuple-element.128), channel_id=1, source_target_pairs={{0,24},{8,16},{16,8},{24,0},{1,25},{9,17},{17,9},{25,1},{2,26},{10... | collective-permute-start | bytes 786440 | tf_op jit(solution)/shard_map/ppermute | solution.py:536
  102.2 12.4 %collective-permute-start.23 = (bf16[272,256]{1,0:T(8,128)(2,1)S(1)}, bf16[272,256]{1,0:T(8,128)(2,1)S(1)}, u32[]{:S(2)}, u32[]{:S(2)}) collective-permute-start(bf16[272,256]{1,0:T(8,128)(2,1)S(1)} %get-tuple-element.104), channel_id=1, source_target_pairs={{0,4},{1,5},{2,6},{3,7},{4,0},{5,1},{6,2},{7,3},{8,12},{9,13},{10,... | collective-permute-start | bytes 417800 | tf_op jit(solution)/shard_map/ppermute | solution.py:533
  103.7 10.9 %collective-permute-start.24 = (bf16[272,256]{1,0:T(8,128)(2,1)S(1)}, bf16[272,256]{1,0:T(8,128)(2,1)S(1)}, u32[]{:S(2)}, u32[]{:S(2)}) collective-permute-start(bf16[272,256]{1,0:T(8,128)(2,1)S(1)} %get-tuple-element.105), channel_id=1, source_target_pairs={{0,6},{1,7},{2,4},{3,5},{4,2},{5,3},{6,0},{7,1},{8,14},{9,15},{10,... | collective-permute-start | bytes 417800 | tf_op jit(solution)/shard_map/ppermute | solution.py:533
  114.7 9.7 %collective-permute-start.25 = (bf16[80,256]{1,0:T(8,128)(2,1)S(1)}, bf16[80,256]{1,0:T(8,128)(2,1)S(1)}, u32[]{:S(2)}, u32[]{:S(2)}) collective-permute-start(bf16[80,256]{1,0:T(8,128)(2,1)S(1)} %get-tuple-element.121), channel_id=1, source_target_pairs={{0,8},{8,0},{16,24},{24,16},{1,9},{9,1},{17,25},{25,17},{2,10},{10... | collective-permute-start | bytes 122888 | tf_op jit(solution)/shard_map/ppermute | solution.py:536
  116.3 8.1 %collective-permute-start.26 = (bf16[80,256]{1,0:T(8,128)(2,1)S(1)}, bf16[80,256]{1,0:T(8,128)(2,1)S(1)}, u32[]{:S(2)}, u32[]{:S(2)}) collective-permute-start(bf16[80,256]{1,0:T(8,128)(2,1)S(1)} %get-tuple-element.122), channel_id=1, source_target_pairs={{0,16},{8,24},{16,0},{24,8},{1,17},{9,25},{17,1},{25,9},{2,18},{10... | collective-permute-start | bytes 122888 | tf_op jit(solution)/shard_map/ppermute | solution.py:536
  116.6 7.8 %collective-permute-start.27 = (bf16[80,256]{1,0:T(8,128)(2,1)S(1)}, bf16[80,256]{1,0:T(8,128)(2,1)S(1)}, u32[]{:S(2)}, u32[]{:S(2)}) collective-permute-start(bf16[80,256]{1,0:T(8,128)(2,1)S(1)} %get-tuple-element.123), channel_id=1, source_target_pairs={{0,24},{8,16},{16,8},{24,0},{1,25},{9,17},{17,9},{25,1},{2,26},{10... | collective-permute-start | bytes 122888 | tf_op jit(solution)/shard_map/ppermute | solution.py:536
  118.2 6.2 %copy-start.4 = (f32[64,256]{1,0:T(8,128)S(1)}, f32[64,256]{1,0:T(8,128)}, u32[]{:S(2)}) copy-start(f32[64,256]{1,0:T(8,128)} %get-tuple-element.119.raw_ref) | copy-start | bytes 196612
  118.2 6.2 %copy-start.5 = (f32[64,128]{1,0:T(8,128)S(1)}, f32[64,128]{1,0:T(8,128)}, u32[]{:S(2)}) copy-start(f32[64,128]{1,0:T(8,128)} %get-tuple-element.120.inv_ref) | copy-start | bytes 98308

commit v4 on v3

--- a/solution.py
+++ b/solution.py
@@ -40,8 +40,8 @@
     return pl.CostEstimate(flops=flops, bytes_accessed=moved, transcendentals=0)
 
 
-def whole(shape):
-    return pl.BlockSpec(shape, lambda *_: (0,) * len(shape))
+def in_hbm(x):
+    return pltpu.with_memory_space_constraint(x, pltpu.HBM)
 
 
 def xor_pairs(size, k):
@@ -84,31 +84,53 @@
             jax.ShapeDtypeStruct((count, width), f32),
             jax.ShapeDtypeStruct((count, 128), f32),
         ],
-        compiler_params=params(56),
+        compiler_params=params(2),
         cost_estimate=cost(0, 1 << 20),
         name="pick_rows",
-    )(rows, image, student, teacher)
-
-
-def round_kernel(s_ref, t_ref, out_s, out_t):
-    out_s[...] = s_ref[...].astype(bf16)
-    out_t[...] = t_ref[...].astype(bf16)
-
-
-def round_protos(student, teacher):
+    )(*map(in_hbm, (rows, image, student, teacher)))
+
+
+def round_kernel(place_ref, s_hbm, t_hbm, ws, wt, slab_s, slab_t, buffer, sem, *, tile, depth, groups):
+    width, cols = s_hbm.shape
+    slab = width // groups
+    steps = cols // tile
+    start = pl.multiple_of(place_ref[0] * slab, slab)
+
+    def copies(j):
+        k = j % depth
+        span = pl.ds(j * tile, tile)
+        return [pltpu.make_async_copy(hbm.at[:, span], buffer.at[i, k], sem.at[i, k]) for i, hbm in enumerate((s_hbm, t_hbm))]
+
+    for j in range(depth - 1):
+        for copy in copies(j):
+            copy.start()
+    for j in range(steps):
+        if j + depth - 1 < steps:
+            for copy in copies(j + depth - 1):
+                copy.start()
+        span = slice(j * tile, (j + 1) * tile)
+        for i, (copy, out, rows) in enumerate(zip(copies(j), (ws, wt), (slab_s, slab_t))):
+            copy.wait()
+            out[:, span] = buffer[i, j % depth].astype(bf16)
+            rows[:, span] = buffer[i, j % depth, pl.ds(start, slab), :]
+
+
+def round_protos(place, student, teacher, groups):
     width, cols = student.shape
-    tile = min(cols, 2048)
-    column = pl.BlockSpec((width, tile), lambda j: (0, j))
-    return pl.pallas_call(
-        round_kernel,
-        grid=(cols // tile,),
-        in_specs=[column] * 2,
-        out_specs=[column] * 2,
-        out_shape=[jax.ShapeDtypeStruct((width, cols), bf16)] * 2,
-        compiler_params=params(24),
+    tile = min(cols, 1024)
+    depth = 4
+    vmem = pl.BlockSpec(memory_space=pltpu.VMEM)
+    return pl.pallas_call(
+        functools.partial(round_kernel, tile=tile, depth=depth, groups=groups),
+        in_specs=[pl.BlockSpec(memory_space=pltpu.SMEM)] + [pl.BlockSpec(memory_space=pltpu.HBM)] * 2,
+        out_specs=[vmem] * 4,
+        out_shape=[jax.ShapeDtypeStruct((width, cols), bf16)] * 2
+        + [jax.ShapeDtypeStruct((width // groups, cols), f32)] * 2,
+        scratch_shapes=[pltpu.VMEM((2, depth, width, tile), f32), pltpu.SemaphoreType.DMA((2, depth))],
+        compiler_params=params(10),
         cost_estimate=cost(0, 12 * width * cols),
         name="round_protos",
-    )(student, teacher)
+    )(place, in_hbm(student), in_hbm(teacher))
 
 
 def first_kernel(own_ref, other_ref, ws_ref, wt_ref, centre_ref, out_ref, us, ut, ms, ss, mt, st, *, count):
@@ -184,7 +206,7 @@
         in_specs=[pl.BlockSpec(memory_space=pltpu.VMEM)] * 5,
         out_shape=jax.ShapeDtypeStruct((8, rows), f32),
         scratch_shapes=[pltpu.VMEM((rows, width), bf16)] * 2 + [pltpu.VMEM((rows, 128), f32)] * 4,
-        compiler_params=params(10),
+        compiler_params=params((rows * (2 * width + 2048) >> 20) + 5),
         cost_estimate=cost(4 * rows * width * cols, 4 * width * cols),
         name="first_pass",
     )(own, other, ws, wt, centre)
@@ -229,45 +251,72 @@
     loss_ref[...] = jnp.broadcast_to(own, loss_ref.shape)
 
 
-def lay_kernel(slab_ref, *refs, count, groups):
-    packs, us, ut, flipped, turned = refs[: 2 * groups], refs[-4], refs[-3], refs[-2], refs[-1]
+def lay_kernel(place_ref, *refs, count, groups):
+    packs, (s_hbm, t_hbm), refs = refs[: 2 * groups], refs[2 * groups : 2 * groups + 2], refs[2 * groups + 2 :]
+    us, ut, flipped, own_s, own_t, turned, sem = refs
+    share = own_s.shape[1]
+    span = pl.ds(pl.multiple_of(place_ref[0] * share, share), share)
+    copies = [
+        pltpu.make_async_copy(hbm.at[:, span], own, sem.at[i]) for i, (hbm, own) in enumerate(((s_hbm, own_s), (t_hbm, own_t)))
+    ]
+    for copy in copies:
+        copy.start()
     pack = 2 * count + PAD
-    zs = packs[0].shape[0] // pack
     at = 0
-    for g in range(groups):
-        for c in range(2):
-            ref = packs[2 * g + c]
-            for z in range(zs):
-                us[at : at + count, :] = ref[z * pack : z * pack + count, :]
-                ut[at : at + count, :] = ref[z * pack + count : z * pack + 2 * count, :]
-                at += count
+    for ref in packs:
+        for z in range(ref.shape[0] // pack):
+            us[at : at + count, :] = ref[z * pack : z * pack + count, :]
+            ut[at : at + count, :] = ref[z * pack + count : z * pack + 2 * count, :]
+            at += count
     width = us.shape[1]
     turned[...] = jnp.transpose(us[...])
     slab = width // groups
     for k in range(groups):
-        start = pl.multiple_of((slab_ref[0] ^ k) * slab, slab)
+        start = pl.multiple_of((place_ref[0] ^ k) * slab, slab)
         flipped[k * slab : (k + 1) * slab, :] = turned[pl.ds(start, slab), :]
-
-
-def lay_rows(slab, packs, count):
+    for copy in copies:
+        copy.wait()
+
+
+def lay_rows(place, packs, ws, wt, count):
     groups = len(packs) // 2
-    width = packs[0].shape[1]
+    width, cols = ws.shape
     rows = 2 * groups * (packs[0].shape[0] // (2 * count + PAD)) * count
+    vmem = pl.BlockSpec(memory_space=pltpu.VMEM)
+    hbm = pl.BlockSpec(memory_space=pltpu.HBM)
     return pl.pallas_call(
         functools.partial(lay_kernel, count=count, groups=groups),
-        in_specs=[pl.BlockSpec(memory_space=pltpu.SMEM)] + [pl.BlockSpec(memory_space=pltpu.VMEM)] * len(packs),
-        out_shape=[jax.ShapeDtypeStruct((rows, width), bf16)] * 2 + [jax.ShapeDtypeStruct((width, rows), bf16)],
-        scratch_shapes=[pltpu.VMEM((width, rows), bf16)],
-        compiler_params=params(16),
+        in_specs=[pl.BlockSpec(memory_space=pltpu.SMEM)] + [vmem] * len(packs) + [hbm] * 2,
+        out_shape=[jax.ShapeDtypeStruct((rows, width), bf16)] * 2
+        + [jax.ShapeDtypeStruct((width, rows), bf16)]
+        + [jax.ShapeDtypeStruct((width, cols // groups), bf16)] * 2,
+        out_specs=[vmem] * 5,
+        scratch_shapes=[pltpu.VMEM((width, rows), bf16), pltpu.SemaphoreType.DMA((2,))],
+        compiler_params=params((width * rows * 2 >> 20) + 2),
         cost_estimate=cost(0, 4 << 20),
         name="lay_rows",
-    )(slab, *packs)
+    )(place, *packs, in_hbm(ws), in_hbm(wt))
+
+
+def pieces(value):
+    rows = lax.broadcasted_iota(jnp.int32, (PAD, 256), 0)
+    out = jnp.zeros((PAD, 256), f32)
+    for k in range(3):
+        piece = value.astype(bf16).astype(f32)
+        out = jnp.where(rows == k, piece, out)
+        value = value - piece
+    return out.astype(bf16)
+
+
+def joined(block):
+    return jnp.sum(block[:, 0:1].astype(f32), axis=0, keepdims=True)
 
 
 def second_kernel(us, ut, flipped, ws_ref, wt_ref, centre_ref, *refs, groups, index, chunk, last, count):
     stats, refs = refs[:groups], refs[groups:]
+    seed_ref, refs = refs[0], refs[1:]
     if index:
-        (carry_ref, seed_ref), refs = refs[:2], refs[2:]
+        carry_ref, refs = refs[0], refs[1:]
     grads, refs = refs[:groups], refs[groups:]
     if last:
         keep_ref, send_ref, loss_ref, total, loss_sum, shift_s, shift_t = refs
@@ -276,6 +325,9 @@
     rows, width = us.shape
     group_rows = rows // groups
     slab = width // groups
+    tile = min(chunk, 512)
+    steps = chunk // tile
+
     total[...] = carry_ref[...] if index else jnp.zeros_like(total)
     loss_sum[...] = jnp.zeros_like(loss_sum)
     for g in range(groups):
@@ -283,11 +335,10 @@
         for k, shift in enumerate((shift_s, shift_t)):
             shift[at, :] = jnp.transpose(jnp.broadcast_to(stats[g][k : k + 1, :], (128, group_rows)))
 
-    tile = min(chunk, 512)
     block = min(group_rows, 256)
     places = [slice(r * block, (r + 1) * block) for r in range(rows // block)]
 
-    @pl.loop(0, chunk // tile)
+    @pl.loop(0, steps)
     def _(j):
         span = pl.ds(pl.multiple_of(index * chunk + j * tile, tile), tile)
         ws = ws_ref[:, span]
@@ -326,9 +377,10 @@
             grads[k][:, out] = grad[k * slab : (k + 1) * slab, :].astype(bf16)
 
     done = jnp.sum(jnp.sum(loss_sum[...], axis=1, keepdims=True), axis=0, keepdims=True)
-    loss = jnp.broadcast_to(done, loss_ref.shape)
-    loss_ref[...] = loss + seed_ref[...] if index else loss
+    loss = seed_ref[0:1, 0:1] - done
+    loss_ref[...] = jnp.broadcast_to(loss, loss_ref.shape)
     if last:
+        send_ref[rows // 2 :, :] = pieces(loss)
         depth = group_rows // (2 * count)
         for g in range(groups):
             for c, ref in enumerate((keep_ref, send_ref)):
@@ -342,48 +394,32 @@
     rows, width = us.shape
     groups = len(stats)
     slab = width // groups
-    chunk = ws.shape[1] // chunks
+    chunk = centre.shape[1] // chunks
     last = index == chunks - 1
-    args = [us, ut, flipped, ws, wt, centre, *stats]
-    if index:
-        args += list(carry)
+    args = [us, ut, flipped, ws, wt, centre, *stats, *carry]
     out_shape = [jax.ShapeDtypeStruct((slab, chunk), bf16)] * groups
     scratch = [pltpu.VMEM((8, 128), f32)] + [pltpu.VMEM((rows, 128), f32)] * 2
     if last:
-        out_shape += [jax.ShapeDtypeStruct((rows // 2, width), f32), jax.ShapeDtypeStruct((rows // 2, width), bf16)]
+        out_shape += [jax.ShapeDtypeStruct((rows // 2, width), f32), jax.ShapeDtypeStruct((rows // 2 + PAD, width), bf16)]
         scratch = [pltpu.VMEM((rows, width), f32)] + scratch
     else:
         out_shape += [jax.ShapeDtypeStruct((rows, width), f32)]
     out_shape += [jax.ShapeDtypeStruct((8, 128), f32)]
-    held = 2 * rows * 128 * 4 + rows * width * 4
+    held = 2 * rows * 128 * 4 + 2 * rows * width * 4
     return pl.pallas_call(
         functools.partial(second_kernel, groups=groups, index=index, chunk=chunk, last=last, count=count),
         in_specs=[pl.BlockSpec(memory_space=pltpu.VMEM)] * len(args),
         out_shape=out_shape,
         scratch_shapes=scratch,
-        compiler_params=params((held >> 20) + 8),
+        compiler_params=params((held >> 20) + 4),
         cost_estimate=cost(8 * rows * width * chunk, 8 * width * chunk),
         name="second_pass",
     )(*args)
 
 
-def pieces(value):
-    rows = lax.broadcasted_iota(jnp.int32, (PAD, 256), 0)
-    out = jnp.zeros((PAD, 256), f32)
-    for k in range(3):
-        piece = value.astype(bf16).astype(f32)
-        out = jnp.where(rows == k, piece, out)
-        value = value - piece
-    return out.astype(bf16)
-
-
-def joined(block):
-    return jnp.sum(block[:, 0:1].astype(f32), axis=0, keepdims=True)
-
-
-def core_sum_kernel(keep_ref, got_ref, loss_ref, other_ref, *outs, blocks):
+def core_sum_kernel(keep_ref, got_ref, loss_ref, *outs, blocks):
     size = keep_ref.shape[0] // blocks
-    loss = loss_ref[0:1, 0:1] + other_ref[0:1, 0:1]
+    loss = loss_ref[0:1, 0:1] + joined(got_ref[keep_ref.shape[0] :, :])
     for k in range(blocks):
         at = slice(k * size, (k + 1) * size)
         outs[k][0:size, :] = (keep_ref[at, :] + got_ref[at, :].astype(f32)).astype(outs[k].dtype)
@@ -392,7 +428,7 @@
     outs[-1][...] = jnp.broadcast_to(loss, outs[-1].shape)
 
 
-def core_sum(keep, got, loss, other, blocks):
+def core_sum(keep, got, loss, blocks):
     rows, width = keep.shape
     size = rows // blocks
     return pl.pallas_call(
@@ -400,10 +436,10 @@
         out_shape=[jax.ShapeDtypeStruct((size, width), f32)]
         + [jax.ShapeDtypeStruct((size + PAD, width), bf16)] * (blocks - 1)
         + [jax.ShapeDtypeStruct((8, 128), f32)],
-        compiler_params=params(8),
+        compiler_params=params(3),
         cost_estimate=cost(0, 1 << 20),
         name="core_sum",
-    )(keep, got, loss, other)
+    )(keep, got, loss)
 
 
 def axis_sum_kernel(keep_ref, loss_ref, *refs, blocks, sources):
@@ -432,7 +468,7 @@
         out_shape=[jax.ShapeDtypeStruct((size, width), f32)]
         + [jax.ShapeDtypeStruct((size + PAD, width), bf16)] * (blocks - 1)
         + [jax.ShapeDtypeStruct((8, 128), f32)],
-        compiler_params=params(8),
+        compiler_params=params(3),
         cost_estimate=cost(0, 1 << 20),
         name="axis_sum",
     )(keep, loss, *got)
@@ -449,61 +485,55 @@
     raw = raw_ref[...]
     inv = inv_ref[:, 0:1]
     out_ref[...] = inv * grad - inv * inv * inv * raw * jnp.sum(raw * grad, axis=-1, keepdims=True)
-    total_ref[...] = jnp.broadcast_to(loss / rows_total, total_ref.shape)
-
-
-def step_kernel(place_ref, *refs, groups):
+    total_ref[0, 0] = jnp.sum(loss) / rows_total
+
+
+def step_kernel(place_ref, *refs, groups, index, chunk, share):
     grads = refs[:groups]
     student_ref, teacher_ref, first_ref, second_ref = refs[groups : groups + 4]
-    out_student, out_first, out_second, out_teacher = refs[-4:]
-    source = pl.program_id(0)
+    outs, stage, sem = refs[-6:-2], refs[-2], refs[-1]
+    copies = []
     for k in range(groups):
-
-        @pl.when(source == k)
-        def _(k=k):
-            grad = grads[k][...].astype(f32)
-            first = beta_one * first_ref[...] + (1.0 - beta_one) * grad
-            second = beta_two * second_ref[...] + (1.0 - beta_two) * grad * grad
-            step = first / fix_one / (jnp.sqrt(second / fix_two) + 1e-08)
-            student = student_ref[...]
-            student = student - learn_rate * (step + decay_rate * student)
-            out_student[...] = student
-            out_first[...] = first
-            out_second[...] = second
-            out_teacher[...] = teacher_keep * teacher_ref[...] + (1.0 - teacher_keep) * student
+        span = pl.ds(pl.multiple_of((place_ref[0] ^ k) * share + index * chunk, chunk), chunk)
+        grad = grads[k][...].astype(f32)
+        first = beta_one * first_ref[:, span] + (1.0 - beta_one) * grad
+        second = beta_two * second_ref[:, span] + (1.0 - beta_two) * grad * grad
+        step = first / fix_one / (jnp.sqrt(second / fix_two) + 1e-08)
+        student = student_ref[:, span]
+        student = student - learn_rate * (step + decay_rate * student)
+        teacher = teacher_keep * teacher_ref[:, span] + (1.0 - teacher_keep) * student
+        for i, value in enumerate((student, first, second, teacher)):
+            stage[k, i] = value
+            copies.append(pltpu.make_async_copy(stage.at[k, i], outs[i].at[:, span], sem.at[k, i]))
+            copies[-1].start()
+    for copy in copies:
+        copy.wait()
 
 
 def optimizer(place, grads, student, teacher, first, second, done, index, chunks, share):
     groups = len(grads)
     slab, total = first.shape
     chunk = share // chunks
-    tile = min(chunk, 2048)
-    steps = chunk // tile
-    column = lambda k, j, place_ref: (place_ref[0] ^ k) * (share // tile) + index * steps + j
-    sliced = pl.BlockSpec((slab, tile), lambda k, j, place_ref: (place_ref[0], column(k, j, place_ref)))
-    local = pl.BlockSpec((slab, tile), lambda k, j, place_ref: (0, column(k, j, place_ref)))
-    grad_specs = [
-        pl.BlockSpec((slab, tile), lambda k, j, place_ref, g=g: (0, jnp.where(k == g, j, jnp.where(k < g, 0, steps - 1))))
-        for g in range(groups)
-    ]
-    in_specs = grad_specs + [sliced, sliced, local, local]
-    args = [*grads, student, teacher, first, second]
+    vmem = pl.BlockSpec(memory_space=pltpu.VMEM)
+    hbm = pl.BlockSpec(memory_space=pltpu.HBM)
+    in_specs = [pl.BlockSpec(memory_space=pltpu.SMEM)] + [vmem] * (groups + 4)
+    args = [place, *grads, student, teacher, first, second]
     aliases = {}
     if done is not None:
-        aliases = {1 + len(args) + i: i for i in range(4)}
-        in_specs += [pl.BlockSpec(memory_space=pl.ANY)] * 4
+        aliases = {len(args) + i: i for i in range(4)}
+        in_specs += [hbm] * 4
         args += list(done)
     return pl.pallas_call(
-        functools.partial(step_kernel, groups=groups),
-        grid_spec=pltpu.PrefetchScalarGridSpec(
-            num_scalar_prefetch=1, grid=(groups, steps), in_specs=in_specs, out_specs=[local] * 4
-        ),
+        functools.partial(step_kernel, groups=groups, index=index, chunk=chunk, share=share),
+        in_specs=in_specs,
+        out_specs=[hbm] * 4,
         out_shape=[jax.ShapeDtypeStruct((slab, total), f32)] * 4,
+        scratch_shapes=[pltpu.VMEM((groups, 4, slab, chunk), f32), pltpu.SemaphoreType.DMA((groups, 4))],
         input_output_aliases=aliases,
-        compiler_params=params(16),
-        cost_estimate=cost(20 * slab * groups * chunk, 34 * slab * groups * chunk),
+        compiler_params=params(11),
+        cost_estimate=cost(20 * slab * groups * chunk, 16 * slab * groups * chunk),
         name="optimizer",
-    )(place, *args)
+    )(*args)
 
 
 def local(
@@ -537,7 +567,7 @@
 
     pack, raw, inv = pick_rows(masked_rows, patch_image, student_patch[0], teacher_patch[0])
     near = [proto_swap(pack, k) for k in range(2, protos, 2)]
-    ws, wt = round_protos(student_proto, teacher_proto)
+    ws, wt, slab_s, slab_t = round_protos(place, student_proto, teacher_proto, groups)
     near, ws, wt = lax.optimization_barrier((near, ws, wt))
     own = jnp.concatenate([pack] + near, axis=0)
     other = proto_swap(own, 1)
@@ -547,60 +577,63 @@
     stats = pl.pallas_call(
         core_join_kernel,
         out_shape=jax.ShapeDtypeStruct(stats.shape, f32),
-        compiler_params=params(8),
+        compiler_params=params(3),
         cost_estimate=cost(0, 1 << 20),
         name="core_join",
     )(stats, proto_swap(stats, 1))
-    stats, ws, wt, *far = lax.optimization_barrier((stats, ws, wt, *far))
+    stats, *far = lax.optimization_barrier((stats, *far))
     far_other = [proto_swap(x, 1) for x in far]
     packs = [own, other]
     for pair in zip(far, far_other):
         packs += list(pair)
-    us, ut, flipped = lay_rows(place, packs, count)
-
-    own_ws, own_wt, own_centre = [lax.dynamic_slice_in_dim(x, place[0] * share, share, 1) for x in (ws, wt, centre)]
+    us, ut, flipped, own_ws, own_wt = lay_rows(place, packs, ws, wt, count)
+
+    own_centre = lax.dynamic_slice_in_dim(centre, place[0] * share, share, 1)
+    near = [proto_swap(stats, k) for k in range(2, protos, 2)]
     stats, loss_own = pl.pallas_call(
         functools.partial(final_join_kernel, count=count, images=images, ratio=ratio),
         out_shape=[jax.ShapeDtypeStruct(stats.shape, f32), jax.ShapeDtypeStruct((8, 128), f32)],
-        compiler_params=params(8),
+        compiler_params=params(3),
         cost_estimate=cost(0, 1 << 20),
         name="final_join",
-    )(stats, *[proto_swap(stats, k) for k in range(2, protos, 2)], own, other)
+    )(stats, *near, own, other)
     all_stats = [stats] + [dp_swap(stats, k) for k in range(1, groups)]
 
-    carry = None
+    carry = [loss_own]
     sent = []
     for index in range(CHUNKS):
         out = second_pass(us, ut, flipped, own_ws, own_wt, own_centre, all_stats, carry, index, CHUNKS, count)
-        grads, carry = out[:groups], out[groups:]
-        sent.append([grads[0]] + [dp_swap(grads[k], k) for k in range(1, groups)])
-    keep, send, cross = carry
-    send, sent[:-1] = lax.optimization_barrier((send, sent[:-1]))
-    loss = loss_own - cross
-
+        grads, carry = out[:groups], out[: groups - 1 : -1]
+        if index + 1 < CHUNKS:
+            sent.append([grads[0]] + [dp_swap(grads[k], k) for k in range(1, groups)])
+    loss, send, keep = carry
+    send, sent = lax.optimization_barrier((send, sent))
     depth = protos // 2
-    out = core_sum(keep, proto_swap(send, 1), loss, proto_swap(loss, 1), depth)
+    out = core_sum(keep, proto_swap(send, 1), loss, depth)
     got = [proto_swap(out[k], 2 * k) for k in range(1, depth)]
+    sent.append([grads[0]] + [dp_swap(grads[k], k) for k in range(1, groups)])
     done = None
     for index in range(CHUNKS - 1):
         done = optimizer(
-            place, sent[index], student_proto, teacher_proto, first_moment, second_moment, done, index, CHUNKS, share
+            place, sent[index], slab_s, slab_t, first_moment, second_moment, done, index, CHUNKS, share
         )
     got, done = lax.optimization_barrier((got, done))
     out = axis_sum(out[0], out[-1], got, groups)
     got = [dp_swap(out[k], k) for k in range(1, groups)]
     done = optimizer(
-        place, sent[-1], student_proto, teacher_proto, first_moment, second_moment, done, CHUNKS - 1, CHUNKS, share
+        place, sent[-1], slab_s, slab_t, first_moment, second_moment, done, CHUNKS - 1, CHUNKS, share
     )
+    got, done = lax.optimization_barrier((got, done))
     row_grad, total = pl.pallas_call(
         functools.partial(row_kernel, sources=len(got), rows_total=rows_total),
-        out_shape=[jax.ShapeDtypeStruct((count, width), f32), jax.ShapeDtypeStruct((8, 128), f32)],
-        compiler_params=params(8),
+        out_shape=[jax.ShapeDtypeStruct((count, width), f32), jax.ShapeDtypeStruct((1, 1), f32)],
+        out_specs=[pl.BlockSpec(memory_space=pltpu.VMEM), pl.BlockSpec(memory_space=pltpu.SMEM)],
+        compiler_params=params(3),
         cost_estimate=cost(0, 1 << 20),
         name="row_grad",
     )(out[0], out[-1], raw, inv, *got)
     new_student, new_first, new_second, new_teacher = done
-    return (row_grad[None], new_student, new_first, new_second, new_teacher, total[0, 0])
+    return (row_grad[None], new_student, new_first, new_second, new_teacher, total.reshape(()))
 
 
 def solution(mesh):

time: 126 us -> 124 us (0.984)
  Pallas kernels: 62.6 us -> 58 us
  starting transfers between devices: 48.5 us -> 52.6 us
  local copies, waits for them, and re-layouts: 3.3 us -> 0.08 us
  waiting for transfers between devices: 10.3 us -> 11.7 us
    pallas_call x3, Pallas kernels: 24.5 us -> 19 us  [the longest x1 11 us: round_protos(): pl.pallas_call(functools.partial(round_kernel, tile=tile, depth=depth, gr...]
    dynamic_slice x1 -> x0, local copies, waits for them, and re-layouts: 2.71 us -> none  [local(): lax.dynamic_slice_in_dim(x, place[0] * share, share, 1)]
    ppermute x16 -> x15, starting transfers between devices: 30.9 us -> 33 us  [proto_swap(): return lax.ppermute(x, 'proto', xor_pairs(protos, k))]
    ppermute x15, starting transfers between devices: 17.6 us -> 19.7 us  [dp_swap(): return lax.ppermute(x, 'dp', xor_pairs(groups, k))]
    pallas_call x1, Pallas kernels: 0.48 us -> 2.47 us  [lay_rows(): pl.pallas_call(functools.partial(lay_kernel, count=count, groups=groups),...]
    ppermute x16 -> x15, waiting for transfers between devices: 8.95 us -> 10.8 us  [proto_swap(): return lax.ppermute(x, 'proto', xor_pairs(protos, k))]
  transfers between devices with their start and end apart: 31 -> 30, of which waited for: 9 -> 8; matrix products, arithmetic and copies ran while one was open for 2% -> 0% of each run, Pallas kernels for 38% -> 36%
where the time goes in v4:
time: 124 us
  Pallas kernels  58 us (47%)
  starting transfers between devices  52.6 us (42%)
  waiting for transfers between devices  11.7 us (9%)
    ppermute x15, starting transfers between devices, proto_swap(): return lax.ppermute(x, 'proto', xor_pairs(protos, k))  33 us
    pallas_call x2, Pallas kernels, second_pass(): pl.pallas_call(functools.partial(second_kernel, groups=groups, index=inde...  22.7 us
    ppermute x15, starting transfers between devices, dp_swap(): return lax.ppermute(x, 'dp', xor_pairs(groups, k))  19.7 us
    pallas_call x1, Pallas kernels, first_pass(): pl.pallas_call(functools.partial(first_kernel, count=count), in_specs=[pl...  11.5 us
    pallas_call x1, Pallas kernels, round_protos(): pl.pallas_call(functools.partial(round_kernel, tile=tile, depth=depth, gr...  11 us
    ppermute x15, waiting for transfers between devices, proto_swap(): return lax.ppermute(x, 'proto', xor_pairs(protos, k))  10.8 us
    pallas_call x2, Pallas kernels, optimizer(): pl.pallas_call(functools.partial(step_kernel, groups=groups, index=index,...  7.97 us
  transfers between devices with their start and end apart: 30, of which 8 were waited for; matrix products, arithmetic and copies ran while one was open for 0% of the time, Pallas kernels for 36%

profile of v4, /device:TPU:0, one launch (start us, length us, event | category | flops | bytes accessed | tf_op | source)
XLA Modules:
  0.0 123.6 jit_solution(15966250184590507892)
XLA Ops:
  0.6 1.2 pick_rows.1
  1.8 5.1 %collective-permute-start.2 = (bf16[144,256]{1,0:T(8,128)(2,1)S(1)}, bf16[144,256]{1,0:T(8,128)(2,1)S(1)}, u32[]{:S(2)}, u32[]{:S(2)}) collective-permute-start(bf16[144,256]{1,0:T(8,128)(2,1)S(1)} %get-tuple-element.81), channel_id=1, source_target_pairs={{0,6},{1,7},{2,4},{3,5},{4,2},{5,3},{6,0},{7,1},{8,14},{9,15},{10,... | collective-permute-start | bytes 221192 | tf_op jit(solution)/shard_map/ppermute | solution.py:563
  6.9 0.0 collective-permute-start.1
  7.0 0.6 collective-permute-start
  7.6 11.0 %round_protos.1 = (bf16[256,16384]{1,0:T(8,128)(2,1)S(1)}, bf16[256,16384]{1,0:T(8,128)(2,1)S(1)}, f32[64,16384]{1,0:T(8,128)S(1)}, f32[64,16384]{1,0:T(8,128)S(1)}) custom-call(s32[1]{0:T(128)} %bitcast.place_ref, f32[256,16384]{1,0:T(8,128)} %s_hbm.1, f32[256,16384]{1,0:T(8,128)} %t_hbm.1), custom_call_target="tpu_custom_call" | custom-call | bytes 50331648 | tf_op jit(solution)/shard_map/round_protos/pallas_call | solution.py:123
  18.6 0.0 copy-start.2
  18.6 0.0 copy-start.4
  18.7 0.0 collective-permute-done.2
  18.7 0.0 collective-permute-done.1
  18.8 0.1 collective-permute-start.3
  18.8 2.7 %collective-permute-start.7 = (bf16[576,256]{1,0:T(8,128)(2,1)S(1)}, bf16[576,256]{1,0:T(8,128)(2,1)S(1)}, u32[]{:S(2)}, u32[]{:S(2)}) collective-permute-start(bf16[576,256]{1,0:T(8,128)(2,1)S(1)} %constant_dynamic-update-slice_fusion.own_ref.refs_0_.refs_4_), channel_id=1, source_target_pairs={{0,24},{8,16},{16,8},{24,0},{1,25},{9,17},{17,9},{25,1},{2,26},{10... | collective-permute-start | bytes 884744 | tf_op jit(solution)/shard_map/ppermute | solution.py:566
  21.5 0.5 collective-permute-start.6
  22.0 0.4 collective-permute-start.5
  22.4 0.0 collective-permute-done.3.other_ref.refs_1_.refs_5_
  22.4 11.5 %first_pass.1.own_ref = f32[8,512]{1,0:T(8,128)S(1)} custom-call(bf16[576,256]{1,0:T(8,128)(2,1)S(1)} %constant_dynamic-update-slice_fusion.own_ref.refs_0_.refs_4_, bf16[576,256]{1,0:T(8,128)(2,1)S(1)} %collective-permute-done.3.other_ref.refs_1_.refs_5_, bf16[256,16384]{1,0:T(8,128)(2,1)S(1)} %get-tuple-element.87.ws_ref.refs_8_, ...), custom_call_target="tpu_custom_call" | custom-call | flops 8589934592 | bytes 16777216 | tf_op jit(solution)/shard_map/first_pass/pallas_call | solution.py:204
  33.9 0.0 copy-done.6
  33.9 0.1 collective-permute-start.4
  34.0 1.2 collective-permute-done.4.other_ref
  35.2 0.2 collective-permute-done.6.refs_4_
  35.5 0.2 collective-permute-done.5.refs_2_
  35.7 0.0 collective-permute-start.8
  35.7 0.5 collective-permute-start.9
  36.2 0.0 collective-permute-start.10
  36.2 3.6 %collective-permute-start.13 = (f32[8,512]{1,0:T(8,128)S(1)}, f32[8,512]{1,0:T(8,128)S(1)}, u32[]{:S(2)}, u32[]{:S(2)}) collective-permute-start(f32[8,512]{1,0:T(8,128)S(1)} %core_join.1.refs_0_), channel_id=1, source_target_pairs={{0,6},{1,7},{2,4},{3,5},{4,2},{5,3},{6,0},{7,1},{8,14},{9,15},{10,... | collective-permute-start | bytes 49160 | tf_op jit(solution)/shard_map/ppermute | solution.py:563
  39.8 17.2 %collective-permute-start.12 = (f32[8,512]{1,0:T(8,128)S(1)}, f32[8,512]{1,0:T(8,128)S(1)}, u32[]{:S(2)}, u32[]{:S(2)}) collective-permute-start(f32[8,512]{1,0:T(8,128)S(1)} %core_join.1.refs_0_), channel_id=1, source_target_pairs={{0,4},{1,5},{2,6},{3,7},{4,0},{5,1},{6,2},{7,3},{8,12},{9,13},{10,... | collective-permute-start | bytes 49160 | tf_op jit(solution)/shard_map/ppermute | solution.py:563
  57.0 2.3 %collective-permute-start.11 = (f32[8,512]{1,0:T(8,128)S(1)}, f32[8,512]{1,0:T(8,128)S(1)}, u32[]{:S(2)}, u32[]{:S(2)}) collective-permute-start(f32[8,512]{1,0:T(8,128)S(1)} %core_join.1.refs_0_), channel_id=1, source_target_pairs={{0,2},{1,3},{2,0},{3,1},{4,6},{5,7},{6,4},{7,5},{8,10},{9,11},{10,... | collective-permute-start | bytes 49160 | tf_op jit(solution)/shard_map/ppermute | solution.py:563
  59.3 1.7 %collective-permute-done.11.refs_1_ = f32[8,512]{1,0:T(8,128)S(1)} collective-permute-done((f32[8,512]{1,0:T(8,128)S(1)}, f32[8,512]{1,0:T(8,128)S(1)}, u32[]{:S(2)}, u32[]{:S(2)}) %collective-permute-start.11) | collective-permute-done | bytes 16416 | tf_op jit(solution)/shard_map/ppermute | solution.py:563
  61.0 0.2 final_join.1
  61.2 0.0 collective-permute-start.16
  61.3 4.1 %collective-permute-start.15 = (f32[8,512]{1,0:T(8,128)S(1)}, f32[8,512]{1,0:T(8,128)S(1)}, u32[]{:S(2)}, u32[]{:S(2)}) collective-permute-start(f32[8,512]{1,0:T(8,128)S(1)} %get-tuple-element.98.refs_0_), channel_id=1, source_target_pairs={{0,16},{8,24},{16,0},{24,8},{1,17},{9,25},{17,1},{25,9},{2,18},{10... | collective-permute-start | bytes 49160 | tf_op jit(solution)/shard_map/ppermute | solution.py:566
  65.4 0.0 collective-permute-done.8.refs_3_
  65.4 1.4 %collective-permute-start.14 = (f32[8,512]{1,0:T(8,128)S(1)}, f32[8,512]{1,0:T(8,128)S(1)}, u32[]{:S(2)}, u32[]{:S(2)}) collective-permute-start(f32[8,512]{1,0:T(8,128)S(1)} %get-tuple-element.98.refs_0_), channel_id=1, source_target_pairs={{0,8},{8,0},{16,24},{24,16},{1,9},{9,1},{17,25},{25,17},{2,10},{10... | collective-permute-start | bytes 49160 | tf_op jit(solution)/shard_map/ppermute | solution.py:566
  66.8 2.5 %lay_rows.1 = (bf16[2048,256]{1,0:T(8,128)(2,1)S(1)}, bf16[2048,256]{1,0:T(8,128)(2,1)S(1)}, bf16[256,2048]{1,0:T(8,128)(2,1)S(1)}, bf16[256,4096]{1,0:T(8,128)(2,1)S(1)}, bf16[256,4096]{1,0:T(8,128)(2,1)S(1)}) custom-call(s32[1]{0:T(128)} %bitcast.place_ref, bf16[576,256]{1,0:T(8,128)(2,1)S(1)} %constant_dynamic-update-slice_fusion.own_ref.refs_0_.refs_4_, ...), custom_call_target="tpu_custom_call" | custom-call | bytes 4194304 | tf_op jit(solution)/shard_map/lay_rows/pallas_call | solution.py:287
  69.3 0.0 collective-permute-done.16.refs_3_
  69.3 0.0 collective-permute-done.15.refs_2_
  69.3 11.2 %second_pass.2 = (bf16[64,2048]{1,0:T(8,128)(2,1)S(1)}, bf16[64,2048]{1,0:T(8,128)(2,1)S(1)}, bf16[64,2048]{1,0:T(8,128)(2,1)S(1)}, bf16[64,2048]{1,0:T(8,128)(2...) custom-call(bf16[2048,256]{1,0:T(8,128)(2,1)S(1)} %get-tuple-element.92.us, ...), custom_call_target="tpu_custom_call" | custom-call | flops 8589934592 | bytes 4194304 | tf_op jit(solution)/shard_map/second_pass/pallas_call | solution.py:409
  80.5 1.3 %collective-permute-start.17 = (bf16[64,2048]{1,0:T(8,128)(2,1)S(1)}, bf16[64,2048]{1,0:T(8,128)(2,1)S(1)}, u32[]{:S(2)}, u32[]{:S(2)}) collective-permute-start(bf16[64,2048]{1,0:T(8,128)(2,1)S(1)} %get-tuple-element.105), channel_id=1, source_target_pairs={{0,8},{8,0},{16,24},{24,16},{1,9},{9,1},{17,25},{25,17},{2,10},{10... | collective-permute-start | bytes 786440 | tf_op jit(solution)/shard_map/ppermute | solution.py:566
  81.8 2.0 %collective-permute-start.18 = (bf16[64,2048]{1,0:T(8,128)(2,1)S(1)}, bf16[64,2048]{1,0:T(8,128)(2,1)S(1)}, u32[]{:S(2)}, u32[]{:S(2)}) collective-permute-start(bf16[64,2048]{1,0:T(8,128)(2,1)S(1)} %get-tuple-element.106), channel_id=1, source_target_pairs={{0,16},{8,24},{16,0},{24,8},{1,17},{9,25},{17,1},{25,9},{2,18},{10... | collective-permute-start | bytes 786440 | tf_op jit(solution)/shard_map/ppermute | solution.py:566
  83.8 0.3 collective-permute-start.19
  84.1 11.4 %second_pass.3 = (bf16[64,2048]{1,0:T(8,128)(2,1)S(1)}, bf16[64,2048]{1,0:T(8,128)(2,1)S(1)}, bf16[64,2048]{1,0:T(8,128)(2,1)S(1)}, bf16[64,2048]{1,0:T(8,128)(2...) custom-call(bf16[2048,256]{1,0:T(8,128)(2,1)S(1)} %get-tuple-element.92.us, ...), custom_call_target="tpu_custom_call" | custom-call | flops 8589934592 | bytes 4194304 | tf_op jit(solution)/shard_map/second_pass/pallas_call | solution.py:409
  95.6 0.0 collective-permute-done.17.refs_1_
  95.6 0.0 collective-permute-done.19.refs_3_
  95.6 0.1 collective-permute-start.20
  95.7 1.9 %collective-permute-done.20.got_ref = bf16[1040,256]{1,0:T(8,128)(2,1)S(1)} collective-permute-done((bf16[1040,256]{1,0:T(8,128)(2,1)S(1)}, bf16[1040,256]{1,0:T(8,128)(2,1)S(1)}, u32[]{:S(2)}, u32[]{:S(2)}) %collective-permute-start.20) | collective-permute-done | bytes 532512 | tf_op jit(solution)/shard_map/ppermute | solution.py:563
  97.6 0.1 core_sum.1
  97.7 1.2 %collective-permute-start.21 = (bf16[272,256]{1,0:T(8,128)(2,1)S(1)}, bf16[272,256]{1,0:T(8,128)(2,1)S(1)}, u32[]{:S(2)}, u32[]{:S(2)}) collective-permute-start(bf16[272,256]{1,0:T(8,128)(2,1)S(1)} %get-tuple-element.112), channel_id=1, source_target_pairs={{0,2},{1,3},{2,0},{3,1},{4,6},{5,7},{6,4},{7,5},{8,10},{9,11},{10,... | collective-permute-start | bytes 417800 | tf_op jit(solution)/shard_map/ppermute | solution.py:563
  99.0 0.8 collective-permute-start.27
  99.8 1.3 %collective-permute-start.28 = (bf16[64,2048]{1,0:T(8,128)(2,1)S(1)}, bf16[64,2048]{1,0:T(8,128)(2,1)S(1)}, u32[]{:S(2)}, u32[]{:S(2)}) collective-permute-start(bf16[64,2048]{1,0:T(8,128)(2,1)S(1)} %get-tuple-element.137), channel_id=1, source_target_pairs={{0,16},{8,24},{16,0},{24,8},{1,17},{9,25},{17,1},{25,9},{2,18},{10... | collective-permute-start | bytes 786440 | tf_op jit(solution)/shard_map/ppermute | solution.py:566
  101.1 1.4 %collective-permute-start.29 = (bf16[64,2048]{1,0:T(8,128)(2,1)S(1)}, bf16[64,2048]{1,0:T(8,128)(2,1)S(1)}, u32[]{:S(2)}, u32[]{:S(2)}) collective-permute-start(bf16[64,2048]{1,0:T(8,128)(2,1)S(1)} %get-tuple-element.138), channel_id=1, source_target_pairs={{0,24},{8,16},{16,8},{24,0},{1,25},{9,17},{17,9},{25,1},{2,26},{10... | collective-permute-start | bytes 786440 | tf_op jit(solution)/shard_map/ppermute | solution.py:566
  102.4 0.0 collective-permute-start.22
  102.4 1.0 collective-permute-done.21.refs_0_
  103.5 2.2 %collective-permute-start.23 = (bf16[272,256]{1,0:T(8,128)(2,1)S(1)}, bf16[272,256]{1,0:T(8,128)(2,1)S(1)}, u32[]{:S(2)}, u32[]{:S(2)}) collective-permute-start(bf16[272,256]{1,0:T(8,128)(2,1)S(1)} %get-tuple-element.114), channel_id=1, source_target_pairs={{0,6},{1,7},{2,4},{3,5},{4,2},{5,3},{6,0},{7,1},{8,14},{9,15},{10,... | collective-permute-start | bytes 417800 | tf_op jit(solution)/shard_map/ppermute | solution.py:563
  105.7 4.0 %optimizer.2 = (f32[64,16384]{1,0:T(8,128)}, f32[64,16384]{1,0:T(8,128)}, f32[64,16384]{1,0:T(8,128)}, f32[64,16384]{1,0:T(8,128)}) custom-call(s32[1]{0:T(128)} %bitcast.place_ref, bf16[64,2048]{1,0:T(8,128)(2,1)S(1)} %get-tuple-element.115.refs_0_, bf16[64,2048]{1,0:T(8,128)(2,1)S(1)} %collective-permute-done.17.refs_1_, ...), custom_call_target="tpu_custom_call" | custom-call | flops 10485760 | bytes 8388608 | tf_op jit(solution)/shard_map/optimizer/pallas_call | solution.py:526
  109.7 5.0 %collective-permute-done.22.refs_1_ = bf16[272,256]{1,0:T(8,128)(2,1)S(1)} collective-permute-done((bf16[272,256]{1,0:T(8,128)(2,1)S(1)}, bf16[272,256]{1,0:T(8,128)(2,1)S(1)}, u32[]{:S(2)}, u32[]{:S(2)}) %collective-permute-start.22) | collective-permute-done | bytes 139296 | tf_op jit(solution)/shard_map/ppermute | solution.py:563
  114.6 0.0 collective-permute-done.23.refs_2_
  114.6 0.1 axis_sum.1
  114.7 1.3 %collective-permute-start.24 = (bf16[80,256]{1,0:T(8,128)(2,1)S(1)}, bf16[80,256]{1,0:T(8,128)(2,1)S(1)}, u32[]{:S(2)}, u32[]{:S(2)}) collective-permute-start(bf16[80,256]{1,0:T(8,128)(2,1)S(1)} %get-tuple-element.132), channel_id=1, source_target_pairs={{0,8},{8,0},{16,24},{24,16},{1,9},{9,1},{17,25},{25,17},{2,10},{10... | collective-permute-start | bytes 122888 | tf_op jit(solution)/shard_map/ppermute | solution.py:566
  116.0 1.7 %collective-permute-start.25 = (bf16[80,256]{1,0:T(8,128)(2,1)S(1)}, bf16[80,256]{1,0:T(8,128)(2,1)S(1)}, u32[]{:S(2)}, u32[]{:S(2)}) collective-permute-start(bf16[80,256]{1,0:T(8,128)(2,1)S(1)} %get-tuple-element.133), channel_id=1, source_target_pairs={{0,16},{8,24},{16,0},{24,8},{1,17},{9,25},{17,1},{25,9},{2,18},{10... | collective-permute-start | bytes 122888 | tf_op jit(solution)/shard_map/ppermute | solution.py:566
  117.7 0.0 collective-permute-done.27.refs_1_
  117.7 0.5 collective-permute-start.26
  118.3 0.0 collective-permute-done.28.refs_2_
  118.3 4.0 %optimizer.3 = (f32[64,16384]{1,0:T(8,128)}, f32[64,16384]{1,0:T(8,128)}, f32[64,16384]{1,0:T(8,128)}, f32[64,16384]{1,0:T(8,128)}) custom-call(s32[1]{0:T(128)} %bitcast.place_ref, bf16[64,2048]{1,0:T(8,128)(2,1)S(1)} %get-tuple-element.135.refs_0_, ...), custom_call_target="tpu_custom_call", output_to_operand_aliasing={{0}: (9, {}), {1}: (10, {}), {2}: (11, {}), {3}: (12, {})} | custom-call | flops 10485760 | bytes 8388608 | tf_op jit(solution)/shard_map/optimizer/pallas_call | solution.py:526
  122.3 0.3 collective-permute-done.26.refs_2_
  122.6 0.8 row_grad.1
  (32 shorter events, 0.1 us)
Async XLA Ops:
  1.8 16.8 %collective-permute-start.2 = (bf16[144,256]{1,0:T(8,128)(2,1)S(1)}, bf16[144,256]{1,0:T(8,128)(2,1)S(1)}, u32[]{:S(2)}, u32[]{:S(2)}) collective-permute-start(bf16[144,256]{1,0:T(8,128)(2,1)S(1)} %get-tuple-element.81), channel_id=1, source_target_pairs={{0,6},{1,7},{2,4},{3,5},{4,2},{5,3},{6,0},{7,1},{8,14},{9,15},{10,... | collective-permute-start | bytes 221192 | tf_op jit(solution)/shard_map/ppermute | solution.py:563
  6.9 11.7 %collective-permute-start.1 = (bf16[144,256]{1,0:T(8,128)(2,1)S(1)}, bf16[144,256]{1,0:T(8,128)(2,1)S(1)}, u32[]{:S(2)}, u32[]{:S(2)}) collective-permute-start(bf16[144,256]{1,0:T(8,128)(2,1)S(1)} %get-tuple-element.81), channel_id=1, source_target_pairs={{0,4},{1,5},{2,6},{3,7},{4,0},{5,1},{6,2},{7,3},{8,12},{9,13},{10,... | collective-permute-start | bytes 221192 | tf_op jit(solution)/shard_map/ppermute | solution.py:563
  7.0 11.7 %collective-permute-start = (bf16[144,256]{1,0:T(8,128)(2,1)S(1)}, bf16[144,256]{1,0:T(8,128)(2,1)S(1)}, u32[]{:S(2)}, u32[]{:S(2)}) collective-permute-start(bf16[144,256]{1,0:T(8,128)(2,1)S(1)} %get-tuple-element.81), channel_id=1, source_target_pairs={{0,2},{1,3},{2,0},{3,1},{4,6},{5,7},{6,4},{7,5},{8,10},{9,11},{10,... | collective-permute-start | bytes 221192 | tf_op jit(solution)/shard_map/ppermute | solution.py:563
  7.6 14.8 %copy-start.8 = (f32[16384]{0:T(1024)S(1)}, f32[16384]{0:T(1024)}, u32[]{:S(2)}) copy-start(f32[16384]{0:T(1024)} %param.17) | copy-start | bytes 196612
  18.6 15.3 %copy-start.2 = (f32[64,16384]{1,0:T(8,128)}, f32[64,16384]{1,0:T(8,128)S(1)}, u32[]{:S(2)}) copy-start(f32[64,16384]{1,0:T(8,128)S(1)} %get-tuple-element.119.refs_4_) | copy-start | bytes 12582916
  18.6 15.3 %copy-start.4 = (f32[64,16384]{1,0:T(8,128)}, f32[64,16384]{1,0:T(8,128)S(1)}, u32[]{:S(2)}) copy-start(f32[64,16384]{1,0:T(8,128)S(1)} %get-tuple-element.120.refs_5_) | copy-start | bytes 12582916
  18.6 15.3 %copy-start.6 = (bf16[256,16384]{1,0:T(8,128)(2,1)}, bf16[256,16384]{1,0:T(8,128)(2,1)S(1)}, u32[]{:S(2)}) copy-start(bf16[256,16384]{1,0:T(8,128)(2,1)S(1)} %get-tuple-element.87.ws_ref.refs_8_) | copy-start | bytes 25165828
  18.6 15.3 %copy-start.7 = (bf16[256,16384]{1,0:T(8,128)(2,1)}, bf16[256,16384]{1,0:T(8,128)(2,1)S(1)}, u32[]{:S(2)}) copy-start(bf16[256,16384]{1,0:T(8,128)(2,1)S(1)} %get-tuple-element.88.wt_ref.refs_9_) | copy-start | bytes 25165828
  18.8 3.6 %collective-permute-start.3 = (bf16[576,256]{1,0:T(8,128)(2,1)S(1)}, bf16[576,256]{1,0:T(8,128)(2,1)S(1)}, u32[]{:S(2)}, u32[]{:S(2)}) collective-permute-start(bf16[576,256]{1,0:T(8,128)(2,1)S(1)} %constant_dynamic-update-slice_fusion.own_ref.refs_0_.refs_4_), channel_id=1, source_target_pairs={{0,1},{1,0},{2,3},{3,2},{4,5},{5,4},{6,7},{7,6},{8,9},{9,8},{10,11... | collective-permute-start | bytes 884744 | tf_op jit(solution)/shard_map/ppermute | solution.py:563
  18.8 16.4 %collective-permute-start.7 = (bf16[576,256]{1,0:T(8,128)(2,1)S(1)}, bf16[576,256]{1,0:T(8,128)(2,1)S(1)}, u32[]{:S(2)}, u32[]{:S(2)}) collective-permute-start(bf16[576,256]{1,0:T(8,128)(2,1)S(1)} %constant_dynamic-update-slice_fusion.own_ref.refs_0_.refs_4_), channel_id=1, source_target_pairs={{0,24},{8,16},{16,8},{24,0},{1,25},{9,17},{17,9},{25,1},{2,26},{10... | collective-permute-start | bytes 884744 | tf_op jit(solution)/shard_map/ppermute | solution.py:566
  21.5 14.0 %collective-permute-start.6 = (bf16[576,256]{1,0:T(8,128)(2,1)S(1)}, bf16[576,256]{1,0:T(8,128)(2,1)S(1)}, u32[]{:S(2)}, u32[]{:S(2)}) collective-permute-start(bf16[576,256]{1,0:T(8,128)(2,1)S(1)} %constant_dynamic-update-slice_fusion.own_ref.refs_0_.refs_4_), channel_id=1, source_target_pairs={{0,16},{8,24},{16,0},{24,8},{1,17},{9,25},{17,1},{25,9},{2,18},{10... | collective-permute-start | bytes 884744 | tf_op jit(solution)/shard_map/ppermute | solution.py:566
  22.0 13.7 %collective-permute-start.5 = (bf16[576,256]{1,0:T(8,128)(2,1)S(1)}, bf16[576,256]{1,0:T(8,128)(2,1)S(1)}, u32[]{:S(2)}, u32[]{:S(2)}) collective-permute-start(bf16[576,256]{1,0:T(8,128)(2,1)S(1)} %constant_dynamic-update-slice_fusion.own_ref.refs_0_.refs_4_), channel_id=1, source_target_pairs={{0,8},{8,0},{16,24},{24,16},{1,9},{9,1},{17,25},{25,17},{2,10},{10... | collective-permute-start | bytes 884744 | tf_op jit(solution)/shard_map/ppermute | solution.py:566
  33.9 1.2 %collective-permute-start.4 = (f32[8,512]{1,0:T(8,128)S(1)}, f32[8,512]{1,0:T(8,128)S(1)}, u32[]{:S(2)}, u32[]{:S(2)}) collective-permute-start(f32[8,512]{1,0:T(8,128)S(1)} %first_pass.1.own_ref), channel_id=1, source_target_pairs={{0,1},{1,0},{2,3},{3,2},{4,5},{5,4},{6,7},{7,6},{8,9},{9,8},{10,11... | collective-permute-start | bytes 49160 | tf_op jit(solution)/shard_map/ppermute | solution.py:563
  35.7 29.7 %collective-permute-start.8 = (bf16[576,256]{1,0:T(8,128)(2,1)S(1)}, bf16[576,256]{1,0:T(8,128)(2,1)S(1)}, u32[]{:S(2)}, u32[]{:S(2)}) collective-permute-start(bf16[576,256]{1,0:T(8,128)(2,1)S(1)} %collective-permute-done.5.refs_2_), channel_id=1, source_target_pairs={{0,1},{1,0},{2,3},{3,2},{4,5},{5,4},{6,7},{7,6},{8,9},{9,8},{10,11... | collective-permute-start | bytes 884744 | tf_op jit(solution)/shard_map/ppermute | solution.py:563
  35.7 31.1 %collective-permute-start.9 = (bf16[576,256]{1,0:T(8,128)(2,1)S(1)}, bf16[576,256]{1,0:T(8,128)(2,1)S(1)}, u32[]{:S(2)}, u32[]{:S(2)}) collective-permute-start(bf16[576,256]{1,0:T(8,128)(2,1)S(1)} %collective-permute-done.6.refs_4_), channel_id=1, source_target_pairs={{0,1},{1,0},{2,3},{3,2},{4,5},{5,4},{6,7},{7,6},{8,9},{9,8},{10,11... | collective-permute-start | bytes 884744 | tf_op jit(solution)/shard_map/ppermute | solution.py:563
  36.2 30.6 %collective-permute-start.10 = (bf16[576,256]{1,0:T(8,128)(2,1)S(1)}, bf16[576,256]{1,0:T(8,128)(2,1)S(1)}, u32[]{:S(2)}, u32[]{:S(2)}) collective-permute-start(bf16[576,256]{1,0:T(8,128)(2,1)S(1)} %collective-permute-done.7.refs_6_), channel_id=1, source_target_pairs={{0,1},{1,0},{2,3},{3,2},{4,5},{5,4},{6,7},{7,6},{8,9},{9,8},{10,11... | collective-permute-start | bytes 884744 | tf_op jit(solution)/shard_map/ppermute | solution.py:563
  36.2 20.8 %collective-permute-start.13 = (f32[8,512]{1,0:T(8,128)S(1)}, f32[8,512]{1,0:T(8,128)S(1)}, u32[]{:S(2)}, u32[]{:S(2)}) collective-permute-start(f32[8,512]{1,0:T(8,128)S(1)} %core_join.1.refs_0_), channel_id=1, source_target_pairs={{0,6},{1,7},{2,4},{3,5},{4,2},{5,3},{6,0},{7,1},{8,14},{9,15},{10,... | collective-permute-start | bytes 49160 | tf_op jit(solution)/shard_map/ppermute | solution.py:563
  39.8 19.5 %collective-permute-start.12 = (f32[8,512]{1,0:T(8,128)S(1)}, f32[8,512]{1,0:T(8,128)S(1)}, u32[]{:S(2)}, u32[]{:S(2)}) collective-permute-start(f32[8,512]{1,0:T(8,128)S(1)} %core_join.1.refs_0_), channel_id=1, source_target_pairs={{0,4},{1,5},{2,6},{3,7},{4,0},{5,1},{6,2},{7,3},{8,12},{9,13},{10,... | collective-permute-start | bytes 49160 | tf_op jit(solution)/shard_map/ppermute | solution.py:563
  57.0 4.0 %collective-permute-start.11 = (f32[8,512]{1,0:T(8,128)S(1)}, f32[8,512]{1,0:T(8,128)S(1)}, u32[]{:S(2)}, u32[]{:S(2)}) collective-permute-start(f32[8,512]{1,0:T(8,128)S(1)} %core_join.1.refs_0_), channel_id=1, source_target_pairs={{0,2},{1,3},{2,0},{3,1},{4,6},{5,7},{6,4},{7,5},{8,10},{9,11},{10,... | collective-permute-start | bytes 49160 | tf_op jit(solution)/shard_map/ppermute | solution.py:563
  61.2 8.0 %collective-permute-start.16 = (f32[8,512]{1,0:T(8,128)S(1)}, f32[8,512]{1,0:T(8,128)S(1)}, u32[]{:S(2)}, u32[]{:S(2)}) collective-permute-start(f32[8,512]{1,0:T(8,128)S(1)} %get-tuple-element.98.refs_0_), channel_id=1, source_target_pairs={{0,24},{8,16},{16,8},{24,0},{1,25},{9,17},{17,9},{25,1},{2,26},{10... | collective-permute-start | bytes 49160 | tf_op jit(solution)/shard_map/ppermute | solution.py:566
  61.3 8.0 %collective-permute-start.15 = (f32[8,512]{1,0:T(8,128)S(1)}, f32[8,512]{1,0:T(8,128)S(1)}, u32[]{:S(2)}, u32[]{:S(2)}) collective-permute-start(f32[8,512]{1,0:T(8,128)S(1)} %get-tuple-element.98.refs_0_), channel_id=1, source_target_pairs={{0,16},{8,24},{16,0},{24,8},{1,17},{9,25},{17,1},{25,9},{2,18},{10... | collective-permute-start | bytes 49160 | tf_op jit(solution)/shard_map/ppermute | solution.py:566
  65.4 3.9 %collective-permute-start.14 = (f32[8,512]{1,0:T(8,128)S(1)}, f32[8,512]{1,0:T(8,128)S(1)}, u32[]{:S(2)}, u32[]{:S(2)}) collective-permute-start(f32[8,512]{1,0:T(8,128)S(1)} %get-tuple-element.98.refs_0_), channel_id=1, source_target_pairs={{0,8},{8,0},{16,24},{24,16},{1,9},{9,1},{17,25},{25,17},{2,10},{10... | collective-permute-start | bytes 49160 | tf_op jit(solution)/shard_map/ppermute | solution.py:566
  80.5 15.0 %collective-permute-start.17 = (bf16[64,2048]{1,0:T(8,128)(2,1)S(1)}, bf16[64,2048]{1,0:T(8,128)(2,1)S(1)}, u32[]{:S(2)}, u32[]{:S(2)}) collective-permute-start(bf16[64,2048]{1,0:T(8,128)(2,1)S(1)} %get-tuple-element.105), channel_id=1, source_target_pairs={{0,8},{8,0},{16,24},{24,16},{1,9},{9,1},{17,25},{25,17},{2,10},{10... | collective-permute-start | bytes 786440 | tf_op jit(solution)/shard_map/ppermute | solution.py:566
  81.8 13.8 %collective-permute-start.18 = (bf16[64,2048]{1,0:T(8,128)(2,1)S(1)}, bf16[64,2048]{1,0:T(8,128)(2,1)S(1)}, u32[]{:S(2)}, u32[]{:S(2)}) collective-permute-start(bf16[64,2048]{1,0:T(8,128)(2,1)S(1)} %get-tuple-element.106), channel_id=1, source_target_pairs={{0,16},{8,24},{16,0},{24,8},{1,17},{9,25},{17,1},{25,9},{2,18},{10... | collective-permute-start | bytes 786440 | tf_op jit(solution)/shard_map/ppermute | solution.py:566
  83.8 11.7 %collective-permute-start.19 = (bf16[64,2048]{1,0:T(8,128)(2,1)S(1)}, bf16[64,2048]{1,0:T(8,128)(2,1)S(1)}, u32[]{:S(2)}, u32[]{:S(2)}) collective-permute-start(bf16[64,2048]{1,0:T(8,128)(2,1)S(1)} %get-tuple-element.107), channel_id=1, source_target_pairs={{0,24},{8,16},{16,8},{24,0},{1,25},{9,17},{17,9},{25,1},{2,26},{10... | collective-permute-start | bytes 786440 | tf_op jit(solution)/shard_map/ppermute | solution.py:566
  84.1 21.6 %copy-start = (f32[64,16384]{1,0:T(8,128)S(1)}, f32[64,16384]{1,0:T(8,128)}, u32[]{:S(2)}) copy-start(f32[64,16384]{1,0:T(8,128)} %refs_6_.3) | copy-start | bytes 12582916
  84.1 21.6 %copy-start.1 = (f32[64,16384]{1,0:T(8,128)S(1)}, f32[64,16384]{1,0:T(8,128)}, u32[]{:S(2)}) copy-start(f32[64,16384]{1,0:T(8,128)} %refs_7_.3) | copy-start | bytes 12582916
  84.1 21.6 %copy-start.3 = (f32[64,16384]{1,0:T(8,128)S(1)}, f32[64,16384]{1,0:T(8,128)}, u32[]{:S(2)}) copy-start(f32[64,16384]{1,0:T(8,128)} %copy-done.2) | copy-start | bytes 12582916
  84.1 21.6 %copy-start.5 = (f32[64,16384]{1,0:T(8,128)S(1)}, f32[64,16384]{1,0:T(8,128)}, u32[]{:S(2)}) copy-start(f32[64,16384]{1,0:T(8,128)} %copy-done.4) | copy-start | bytes 12582916
  95.6 2.0 %collective-permute-start.20 = (bf16[1040,256]{1,0:T(8,128)(2,1)S(1)}, bf16[1040,256]{1,0:T(8,128)(2,1)S(1)}, u32[]{:S(2)}, u32[]{:S(2)}) collective-permute-start(bf16[1040,256]{1,0:T(8,128)(2,1)S(1)} %get-tuple-element.108), channel_id=1, source_target_pairs={{0,1},{1,0},{2,3},{3,2},{4,5},{5,4},{6,7},{7,6},{8,9},{9,8},{10,11... | collective-permute-start | bytes 1597448 | tf_op jit(solution)/shard_map/ppermute | solution.py:563
  97.7 5.8 %collective-permute-start.21 = (bf16[272,256]{1,0:T(8,128)(2,1)S(1)}, bf16[272,256]{1,0:T(8,128)(2,1)S(1)}, u32[]{:S(2)}, u32[]{:S(2)}) collective-permute-start(bf16[272,256]{1,0:T(8,128)(2,1)S(1)} %get-tuple-element.112), channel_id=1, source_target_pairs={{0,2},{1,3},{2,0},{3,1},{4,6},{5,7},{6,4},{7,5},{8,10},{9,11},{10,... | collective-permute-start | bytes 417800 | tf_op jit(solution)/shard_map/ppermute | solution.py:563
  99.0 18.8 %collective-permute-start.27 = (bf16[64,2048]{1,0:T(8,128)(2,1)S(1)}, bf16[64,2048]{1,0:T(8,128)(2,1)S(1)}, u32[]{:S(2)}, u32[]{:S(2)}) collective-permute-start(bf16[64,2048]{1,0:T(8,128)(2,1)S(1)} %get-tuple-element.136), channel_id=1, source_target_pairs={{0,8},{8,0},{16,24},{24,16},{1,9},{9,1},{17,25},{25,17},{2,10},{10... | collective-permute-start | bytes 786440 | tf_op jit(solution)/shard_map/ppermute | solution.py:566
  99.8 18.5 %collective-permute-start.28 = (bf16[64,2048]{1,0:T(8,128)(2,1)S(1)}, bf16[64,2048]{1,0:T(8,128)(2,1)S(1)}, u32[]{:S(2)}, u32[]{:S(2)}) collective-permute-start(bf16[64,2048]{1,0:T(8,128)(2,1)S(1)} %get-tuple-element.137), channel_id=1, source_target_pairs={{0,16},{8,24},{16,0},{24,8},{1,17},{9,25},{17,1},{25,9},{2,18},{10... | collective-permute-start | bytes 786440 | tf_op jit(solution)/shard_map/ppermute | solution.py:566
  101.1 17.2 %collective-permute-start.29 = (bf16[64,2048]{1,0:T(8,128)(2,1)S(1)}, bf16[64,2048]{1,0:T(8,128)(2,1)S(1)}, u32[]{:S(2)}, u32[]{:S(2)}) collective-permute-start(bf16[64,2048]{1,0:T(8,128)(2,1)S(1)} %get-tuple-element.138), channel_id=1, source_target_pairs={{0,24},{8,16},{16,8},{24,0},{1,25},{9,17},{17,9},{25,1},{2,26},{10... | collective-permute-start | bytes 786440 | tf_op jit(solution)/shard_map/ppermute | solution.py:566
  102.4 12.2 %collective-permute-start.22 = (bf16[272,256]{1,0:T(8,128)(2,1)S(1)}, bf16[272,256]{1,0:T(8,128)(2,1)S(1)}, u32[]{:S(2)}, u32[]{:S(2)}) collective-permute-start(bf16[272,256]{1,0:T(8,128)(2,1)S(1)} %get-tuple-element.113), channel_id=1, source_target_pairs={{0,4},{1,5},{2,6},{3,7},{4,0},{5,1},{6,2},{7,3},{8,12},{9,13},{10,... | collective-permute-start | bytes 417800 | tf_op jit(solution)/shard_map/ppermute | solution.py:563
  103.5 11.1 %collective-permute-start.23 = (bf16[272,256]{1,0:T(8,128)(2,1)S(1)}, bf16[272,256]{1,0:T(8,128)(2,1)S(1)}, u32[]{:S(2)}, u32[]{:S(2)}) collective-permute-start(bf16[272,256]{1,0:T(8,128)(2,1)S(1)} %get-tuple-element.114), channel_id=1, source_target_pairs={{0,6},{1,7},{2,4},{3,5},{4,2},{5,3},{6,0},{7,1},{8,14},{9,15},{10,... | collective-permute-start | bytes 417800 | tf_op jit(solution)/shard_map/ppermute | solution.py:563
  114.7 7.6 %collective-permute-start.24 = (bf16[80,256]{1,0:T(8,128)(2,1)S(1)}, bf16[80,256]{1,0:T(8,128)(2,1)S(1)}, u32[]{:S(2)}, u32[]{:S(2)}) collective-permute-start(bf16[80,256]{1,0:T(8,128)(2,1)S(1)} %get-tuple-element.132), channel_id=1, source_target_pairs={{0,8},{8,0},{16,24},{24,16},{1,9},{9,1},{17,25},{25,17},{2,10},{10... | collective-permute-start | bytes 122888 | tf_op jit(solution)/shard_map/ppermute | solution.py:566
  116.0 6.3 %collective-permute-start.25 = (bf16[80,256]{1,0:T(8,128)(2,1)S(1)}, bf16[80,256]{1,0:T(8,128)(2,1)S(1)}, u32[]{:S(2)}, u32[]{:S(2)}) collective-permute-start(bf16[80,256]{1,0:T(8,128)(2,1)S(1)} %get-tuple-element.133), channel_id=1, source_target_pairs={{0,16},{8,24},{16,0},{24,8},{1,17},{9,25},{17,1},{25,9},{2,18},{10... | collective-permute-start | bytes 122888 | tf_op jit(solution)/shard_map/ppermute | solution.py:566
  117.7 4.9 %collective-permute-start.26 = (bf16[80,256]{1,0:T(8,128)(2,1)S(1)}, bf16[80,256]{1,0:T(8,128)(2,1)S(1)}, u32[]{:S(2)}, u32[]{:S(2)}) collective-permute-start(bf16[80,256]{1,0:T(8,128)(2,1)S(1)} %get-tuple-element.134), channel_id=1, source_target_pairs={{0,24},{8,16},{16,8},{24,0},{1,25},{9,17},{17,9},{25,1},{2,26},{10... | collective-permute-start | bytes 122888 | tf_op jit(solution)/shard_map/ppermute | solution.py:566

commit v5 on v4

--- a/solution.py
+++ b/solution.py
@@ -90,54 +90,58 @@
     )(*map(in_hbm, (rows, image, student, teacher)))
 
 
-def round_kernel(place_ref, s_hbm, t_hbm, ws, wt, slab_s, slab_t, buffer, sem, *, tile, depth, groups):
-    width, cols = s_hbm.shape
-    slab = width // groups
-    steps = cols // tile
-    start = pl.multiple_of(place_ref[0] * slab, slab)
+def round_kernel(s_hbm, t_hbm, ws, wt, buffer, sem, *, tile, depth):
+    steps = ws.shape[1] // tile
 
     def copies(j):
         k = j % depth
         span = pl.ds(j * tile, tile)
         return [pltpu.make_async_copy(hbm.at[:, span], buffer.at[i, k], sem.at[i, k]) for i, hbm in enumerate((s_hbm, t_hbm))]
 
-    for j in range(depth - 1):
+    for j in range(min(depth - 1, steps)):
         for copy in copies(j):
             copy.start()
     for j in range(steps):
         if j + depth - 1 < steps:
             for copy in copies(j + depth - 1):
                 copy.start()
-        span = slice(j * tile, (j + 1) * tile)
-        for i, (copy, out, rows) in enumerate(zip(copies(j), (ws, wt), (slab_s, slab_t))):
+        for i, (copy, out) in enumerate(zip(copies(j), (ws, wt))):
             copy.wait()
-            out[:, span] = buffer[i, j % depth].astype(bf16)
-            rows[:, span] = buffer[i, j % depth, pl.ds(start, slab), :]
-
-
-def round_protos(place, student, teacher, groups):
+            out[:, j * tile : (j + 1) * tile] = buffer[i, j % depth].astype(bf16)
+
+
+def round_protos(student, teacher):
     width, cols = student.shape
-    tile = min(cols, 1024)
+    half = cols // 2
+    tile = min(half, 1024)
     depth = 4
-    vmem = pl.BlockSpec(memory_space=pltpu.VMEM)
     return pl.pallas_call(
-        functools.partial(round_kernel, tile=tile, depth=depth, groups=groups),
-        in_specs=[pl.BlockSpec(memory_space=pltpu.SMEM)] + [pl.BlockSpec(memory_space=pltpu.HBM)] * 2,
-        out_specs=[vmem] * 4,
-        out_shape=[jax.ShapeDtypeStruct((width, cols), bf16)] * 2
-        + [jax.ShapeDtypeStruct((width // groups, cols), f32)] * 2,
+        functools.partial(round_kernel, tile=tile, depth=depth),
+        in_specs=[pl.BlockSpec(memory_space=pltpu.HBM)] * 2,
+        out_specs=[pl.BlockSpec(memory_space=pltpu.VMEM)] * 2,
+        out_shape=[jax.ShapeDtypeStruct((width, half), bf16)] * 2,
         scratch_shapes=[pltpu.VMEM((2, depth, width, tile), f32), pltpu.SemaphoreType.DMA((2, depth))],
         compiler_params=params(10),
-        cost_estimate=cost(0, 12 * width * cols),
+        cost_estimate=cost(0, 12 * width * half),
         name="round_protos",
-    )(place, in_hbm(student), in_hbm(teacher))
-
-
-def first_kernel(own_ref, other_ref, ws_ref, wt_ref, centre_ref, out_ref, us, ut, ms, ss, mt, st, *, count):
+    )(in_hbm(student), in_hbm(teacher))
+
+
+def first_kernel(
+    own_ref, other_ref, ws_ref, wt_ref, centre_ref, s_hbm, t_hbm, out_ref, us, ut, ms, ss, mt, st, rest, sem, *, count
+):
     pack = 2 * count + PAD
     rows = us.shape[0]
     half = rows // 2
     cols = ws_ref.shape[1]
+    tile = min(cols, 1024)
+    unroll = 2 if cols % (2 * tile) == 0 else 1
+    copies = []
+    for j in range(cols // tile):
+        for i, hbm in enumerate((s_hbm, t_hbm)):
+            span = slice(j * tile, (j + 1) * tile)
+            copies.append(pltpu.make_async_copy(hbm.at[:, pl.ds(cols + j * tile, tile)], rest.at[i, :, span], sem.at[i, j]))
+            copies[-1].start()
     for c, ref in enumerate((own_ref, other_ref)):
         for z in range(half // count):
             at = c * half + z * count
@@ -145,17 +149,21 @@
             ut[at : at + count, :] = ref[z * pack + count : z * pack + 2 * count, :]
 
     block = min(rows, 512)
-    tile = min(cols, 1024)
-    unroll = 2 if cols % (2 * tile) == 0 else 1
-
-    def sweep(update):
+
+    def sweep(update, second):
         @pl.loop(0, cols // (tile * unroll))
         def _(j):
             for u in range(unroll):
                 span = pl.ds(pl.multiple_of((j * unroll + u) * tile, tile), tile)
-                ws = ws_ref[:, span]
-                wt = wt_ref[:, span]
-                shift = centre_ref[:, span] * scale_t
+                if second:
+                    ws = rest[0, :, span].astype(bf16)
+                    wt = rest[1, :, span].astype(bf16)
+                    place = pl.ds(pl.multiple_of(cols + (j * unroll + u) * tile, tile), tile)
+                else:
+                    ws = ws_ref[:, span]
+                    wt = wt_ref[:, span]
+                    place = span
+                shift = centre_ref[:, place] * scale_t
                 for r in range(rows // block):
                     at = slice(r * block, (r + 1) * block)
                     zs = jnp.dot(us[at, :], ws, preferred_element_type=f32)
@@ -176,7 +184,10 @@
     for m, s in ((ms, ss), (mt, st)):
         m[...] = jnp.zeros_like(m)
         s[...] = jnp.zeros_like(s)
-    sweep(plain)
+    sweep(plain, False)
+    for copy in copies:
+        copy.wait()
+    sweep(plain, True)
     far = jnp.zeros((rows, 1), f32)
     for s in (ss, st):
         total = jnp.sum(s[...], axis=1, keepdims=True)
@@ -187,7 +198,8 @@
         for m, s in ((ms, ss), (mt, st)):
             m[...] = jnp.full_like(m, -jnp.inf)
             s[...] = jnp.zeros_like(s)
-        sweep(running)
+        sweep(running, False)
+        sweep(running, True)
 
     out_ref[...] = jnp.zeros_like(out_ref)
     for k, (m, s) in enumerate(((ms, ss), (mt, st))):
@@ -198,18 +210,21 @@
         out_ref[k : k + 1, :] = jnp.transpose(lse)[0:1, :]
 
 
-def first_pass(own, other, ws, wt, centre, count):
+def first_pass(own, other, ws, wt, centre, student, teacher, count):
     width, cols = ws.shape
+    tile = min(cols, 1024)
     rows = 2 * own.shape[0] // (2 * count + PAD) * count
     return pl.pallas_call(
         functools.partial(first_kernel, count=count),
-        in_specs=[pl.BlockSpec(memory_space=pltpu.VMEM)] * 5,
+        in_specs=[pl.BlockSpec(memory_space=pltpu.VMEM)] * 5 + [pl.BlockSpec(memory_space=pltpu.HBM)] * 2,
         out_shape=jax.ShapeDtypeStruct((8, rows), f32),
-        scratch_shapes=[pltpu.VMEM((rows, width), bf16)] * 2 + [pltpu.VMEM((rows, 128), f32)] * 4,
-        compiler_params=params((rows * (2 * width + 2048) >> 20) + 5),
-        cost_estimate=cost(4 * rows * width * cols, 4 * width * cols),
+        scratch_shapes=[pltpu.VMEM((rows, width), bf16)] * 2
+        + [pltpu.VMEM((rows, 128), f32)] * 4
+        + [pltpu.VMEM((2, width, cols), f32), pltpu.SemaphoreType.DMA((2, cols // tile))],
+        compiler_params=params((rows * (2 * width + 2048) + 8 * width * cols >> 20) + 7),
+        cost_estimate=cost(8 * rows * width * cols, 12 * width * cols),
         name="first_pass",
-    )(own, other, ws, wt, centre)
+    )(own, other, ws, wt, centre, in_hbm(student), in_hbm(teacher))
 
 
 def join(parts):
@@ -253,14 +268,17 @@
 
 def lay_kernel(place_ref, *refs, count, groups):
     packs, (s_hbm, t_hbm), refs = refs[: 2 * groups], refs[2 * groups : 2 * groups + 2], refs[2 * groups + 2 :]
-    us, ut, flipped, own_s, own_t, turned, sem = refs
+    us, ut, flipped, own_s, own_t, turned, buffer, sem = refs
     share = own_s.shape[1]
-    span = pl.ds(pl.multiple_of(place_ref[0] * share, share), share)
-    copies = [
-        pltpu.make_async_copy(hbm.at[:, span], own, sem.at[i]) for i, (hbm, own) in enumerate(((s_hbm, own_s), (t_hbm, own_t)))
-    ]
-    for copy in copies:
-        copy.start()
+    tile = share // sem.shape[1]
+    copies = []
+    for j in range(share // tile):
+        span = pl.ds(pl.multiple_of(place_ref[0] * share + j * tile, tile), tile)
+        inner = slice(j * tile, (j + 1) * tile)
+        for i, (hbm, own) in enumerate(((s_hbm, own_s), (t_hbm, own_t))):
+            copy = pltpu.make_async_copy(hbm.at[:, span], buffer.at[i, :, inner], sem.at[i, j])
+            copy.start()
+            copies.append((copy, i, own, inner))
     pack = 2 * count + PAD
     at = 0
     for ref in packs:
@@ -274,13 +292,16 @@
     for k in range(groups):
         start = pl.multiple_of((place_ref[0] ^ k) * slab, slab)
         flipped[k * slab : (k + 1) * slab, :] = turned[pl.ds(start, slab), :]
-    for copy in copies:
+    for copy, i, own, inner in copies:
         copy.wait()
-
-
-def lay_rows(place, packs, ws, wt, count):
+        own[:, inner] = buffer[i, :, inner].astype(bf16)
+
+
+def lay_rows(place, packs, student, teacher, count):
     groups = len(packs) // 2
-    width, cols = ws.shape
+    width, cols = student.shape
+    share = cols // groups
+    tile = min(share, 1024)
     rows = 2 * groups * (packs[0].shape[0] // (2 * count + PAD)) * count
     vmem = pl.BlockSpec(memory_space=pltpu.VMEM)
     hbm = pl.BlockSpec(memory_space=pltpu.HBM)
@@ -289,13 +310,17 @@
         in_specs=[pl.BlockSpec(memory_space=pltpu.SMEM)] + [vmem] * len(packs) + [hbm] * 2,
         out_shape=[jax.ShapeDtypeStruct((rows, width), bf16)] * 2
         + [jax.ShapeDtypeStruct((width, rows), bf16)]
-        + [jax.ShapeDtypeStruct((width, cols // groups), bf16)] * 2,
+        + [jax.ShapeDtypeStruct((width, share), bf16)] * 2,
         out_specs=[vmem] * 5,
-        scratch_shapes=[pltpu.VMEM((width, rows), bf16), pltpu.SemaphoreType.DMA((2,))],
-        compiler_params=params((width * rows * 2 >> 20) + 2),
+        scratch_shapes=[
+            pltpu.VMEM((width, rows), bf16),
+            pltpu.VMEM((2, width, share), f32),
+            pltpu.SemaphoreType.DMA((2, share // tile)),
+        ],
+        compiler_params=params((width * rows * 2 + 8 * width * share >> 20) + 2),
         cost_estimate=cost(0, 4 << 20),
         name="lay_rows",
-    )(place, *packs, in_hbm(ws), in_hbm(wt))
+    )(place, *packs, in_hbm(student), in_hbm(teacher))
 
 
 def pieces(value):
@@ -317,14 +342,23 @@
     seed_ref, refs = refs[0], refs[1:]
     if index:
         carry_ref, refs = refs[0], refs[1:]
+    else:
+        (place_ref, *protos), refs = refs[:3], refs[3:]
+        sem, refs = refs[-1], refs[:-1]
     grads, refs = refs[:groups], refs[groups:]
     if last:
         keep_ref, send_ref, loss_ref, total, loss_sum, shift_s, shift_t = refs
     else:
-        total, loss_ref, loss_sum, shift_s, shift_t = refs
+        total, loss_ref, *slabs, loss_sum, shift_s, shift_t = refs
     rows, width = us.shape
     group_rows = rows // groups
     slab = width // groups
+    copies = []
+    if not index:
+        start = pl.multiple_of(place_ref[0] * slab, slab)
+        for i, (hbm, out) in enumerate(zip(protos, slabs)):
+            copies.append(pltpu.make_async_copy(hbm.at[pl.ds(start, slab), :], out, sem.at[i]))
+            copies[-1].start()
     tile = min(chunk, 512)
     steps = chunk // tile
 
@@ -379,6 +413,8 @@
     done = jnp.sum(jnp.sum(loss_sum[...], axis=1, keepdims=True), axis=0, keepdims=True)
     loss = seed_ref[0:1, 0:1] - done
     loss_ref[...] = jnp.broadcast_to(loss, loss_ref.shape)
+    for copy in copies:
+        copy.wait()
     if last:
         send_ref[rows // 2 :, :] = pieces(loss)
         depth = group_rows // (2 * count)
@@ -390,13 +426,14 @@
                     ref[dst : dst + count, :] = total[src : src + count, :].astype(ref.dtype)
 
 
-def second_pass(us, ut, flipped, ws, wt, centre, stats, carry, index, chunks, count):
+def second_pass(place, us, ut, flipped, ws, wt, centre, stats, carry, student, teacher, index, chunks, count):
     rows, width = us.shape
     groups = len(stats)
     slab = width // groups
     chunk = centre.shape[1] // chunks
     last = index == chunks - 1
     args = [us, ut, flipped, ws, wt, centre, *stats, *carry]
+    in_specs = [pl.BlockSpec(memory_space=pltpu.VMEM)] * len(args)
     out_shape = [jax.ShapeDtypeStruct((slab, chunk), bf16)] * groups
     scratch = [pltpu.VMEM((8, 128), f32)] + [pltpu.VMEM((rows, 128), f32)] * 2
     if last:
@@ -405,10 +442,16 @@
     else:
         out_shape += [jax.ShapeDtypeStruct((rows, width), f32)]
     out_shape += [jax.ShapeDtypeStruct((8, 128), f32)]
+    if not index:
+        args += [place, in_hbm(student), in_hbm(teacher)]
+        in_specs += [pl.BlockSpec(memory_space=pltpu.SMEM)] + [pl.BlockSpec(memory_space=pltpu.HBM)] * 2
+        out_shape += [jax.ShapeDtypeStruct((slab, student.shape[1]), f32)] * 2
+        scratch += [pltpu.SemaphoreType.DMA((2,))]
     held = 2 * rows * 128 * 4 + 2 * rows * width * 4
     return pl.pallas_call(
         functools.partial(second_kernel, groups=groups, index=index, chunk=chunk, last=last, count=count),
-        in_specs=[pl.BlockSpec(memory_space=pltpu.VMEM)] * len(args),
+        in_specs=in_specs,
+        out_specs=[pl.BlockSpec(memory_space=pltpu.VMEM)] * len(out_shape),
         out_shape=out_shape,
         scratch_shapes=scratch,
         compiler_params=params((held >> 20) + 4),
@@ -488,13 +531,13 @@
     total_ref[0, 0] = jnp.sum(loss) / rows_total
 
 
-def step_kernel(place_ref, *refs, groups, index, chunk, share):
-    grads = refs[:groups]
-    student_ref, teacher_ref, first_ref, second_ref = refs[groups : groups + 4]
+def step_kernel(place_ref, *refs, jobs, chunk, share):
+    grads = refs[: len(jobs)]
+    student_ref, teacher_ref, first_ref, second_ref = refs[len(jobs) : len(jobs) + 4]
     outs, stage, sem = refs[-6:-2], refs[-2], refs[-1]
     copies = []
-    for k in range(groups):
-        span = pl.ds(pl.multiple_of((place_ref[0] ^ k) * share + index * chunk, chunk), chunk)
+    for k, (source, index) in enumerate(jobs):
+        span = pl.ds(pl.multiple_of((place_ref[0] ^ source) * share + index * chunk, chunk), chunk)
         grad = grads[k][...].astype(f32)
         first = beta_one * first_ref[:, span] + (1.0 - beta_one) * grad
         second = beta_two * second_ref[:, span] + (1.0 - beta_two) * grad * grad
@@ -510,13 +553,13 @@
         copy.wait()
 
 
-def optimizer(place, grads, student, teacher, first, second, done, index, chunks, share):
-    groups = len(grads)
+def optimizer(place, jobs, student, teacher, first, second, done, share):
+    jobs, grads = list(jobs), list(jobs.values())
     slab, total = first.shape
-    chunk = share // chunks
+    chunk = grads[0].shape[1]
     vmem = pl.BlockSpec(memory_space=pltpu.VMEM)
     hbm = pl.BlockSpec(memory_space=pltpu.HBM)
-    in_specs = [pl.BlockSpec(memory_space=pltpu.SMEM)] + [vmem] * (groups + 4)
+    in_specs = [pl.BlockSpec(memory_space=pltpu.SMEM)] + [vmem] * (len(jobs) + 4)
     args = [place, *grads, student, teacher, first, second]
     aliases = {}
     if done is not None:
@@ -524,14 +567,14 @@
         in_specs += [hbm] * 4
         args += list(done)
     return pl.pallas_call(
-        functools.partial(step_kernel, groups=groups, index=index, chunk=chunk, share=share),
+        functools.partial(step_kernel, jobs=jobs, chunk=chunk, share=share),
         in_specs=in_specs,
         out_specs=[hbm] * 4,
         out_shape=[jax.ShapeDtypeStruct((slab, total), f32)] * 4,
-        scratch_shapes=[pltpu.VMEM((groups, 4, slab, chunk), f32), pltpu.SemaphoreType.DMA((groups, 4))],
+        scratch_shapes=[pltpu.VMEM((len(jobs), 4, slab, chunk), f32), pltpu.SemaphoreType.DMA((len(jobs), 4))],
         input_output_aliases=aliases,
-        compiler_params=params(11),
-        cost_estimate=cost(20 * slab * groups * chunk, 16 * slab * groups * chunk),
+        compiler_params=params((len(jobs) * 16 * slab * chunk >> 20) + 3),
+        cost_estimate=cost(20 * slab * len(jobs) * chunk, 16 * slab * len(jobs) * chunk),
         name="optimizer",
     )(*args)
 
@@ -567,13 +610,13 @@
 
     pack, raw, inv = pick_rows(masked_rows, patch_image, student_patch[0], teacher_patch[0])
     near = [proto_swap(pack, k) for k in range(2, protos, 2)]
-    ws, wt, slab_s, slab_t = round_protos(place, student_proto, teacher_proto, groups)
+    ws, wt = round_protos(student_proto, teacher_proto)
     near, ws, wt = lax.optimization_barrier((near, ws, wt))
     own = jnp.concatenate([pack] + near, axis=0)
     other = proto_swap(own, 1)
     far = [dp_swap(own, k) for k in range(1, groups)]
 
-    stats = first_pass(own, other, ws, wt, centre, count)
+    stats = first_pass(own, other, ws, wt, centre, student_proto, teacher_proto, count)
     stats = pl.pallas_call(
         core_join_kernel,
         out_shape=jax.ShapeDtypeStruct(stats.shape, f32),
@@ -586,7 +629,7 @@
     packs = [own, other]
     for pair in zip(far, far_other):
         packs += list(pair)
-    us, ut, flipped, own_ws, own_wt = lay_rows(place, packs, ws, wt, count)
+    us, ut, flipped, own_ws, own_wt = lay_rows(place, packs, student_proto, teacher_proto, count)
 
     own_centre = lax.dynamic_slice_in_dim(centre, place[0] * share, share, 1)
     near = [proto_swap(stats, k) for k in range(2, protos, 2)]
@@ -602,7 +645,11 @@
     carry = [loss_own]
     sent = []
     for index in range(CHUNKS):
-        out = second_pass(us, ut, flipped, own_ws, own_wt, own_centre, all_stats, carry, index, CHUNKS, count)
+        out = second_pass(
+            place, us, ut, flipped, own_ws, own_wt, own_centre, all_stats, carry, student_proto, teacher_proto, index, CHUNKS, count
+        )
+        if not index:
+            (slab_s, slab_t), out = out[-2:], out[:-2]
         grads, carry = out[:groups], out[: groups - 1 : -1]
         if index + 1 < CHUNKS:
             sent.append([grads[0]] + [dp_swap(grads[k], k) for k in range(1, groups)])
@@ -612,17 +659,13 @@
     out = core_sum(keep, proto_swap(send, 1), loss, depth)
     got = [proto_swap(out[k], 2 * k) for k in range(1, depth)]
     sent.append([grads[0]] + [dp_swap(grads[k], k) for k in range(1, groups)])
-    done = None
-    for index in range(CHUNKS - 1):
-        done = optimizer(
-            place, sent[index], slab_s, slab_t, first_moment, second_moment, done, index, CHUNKS, share
-        )
+    jobs = {(k, index): grad for index, chunk in enumerate(sent) for k, grad in enumerate(chunk)}
+    late = {job: jobs.pop(job) for job in list(jobs) if job[0] and job[1] == CHUNKS - 1}
+    done = optimizer(place, jobs, slab_s, slab_t, first_moment, second_moment, None, share)
     got, done = lax.optimization_barrier((got, done))
     out = axis_sum(out[0], out[-1], got, groups)
     got = [dp_swap(out[k], k) for k in range(1, groups)]
-    done = optimizer(
-        place, sent[-1], slab_s, slab_t, first_moment, second_moment, done, CHUNKS - 1, CHUNKS, share
-    )
+    done = optimizer(place, late, slab_s, slab_t, first_moment, second_moment, done, share)
     got, done = lax.optimization_barrier((got, done))
     row_grad, total = pl.pallas_call(
         functools.partial(row_kernel, sources=len(got), rows_total=rows_total),

time: 124 us -> 121 us (0.976)
  Pallas kernels: 58 us -> 56.1 us
    pallas_call x3, Pallas kernels: 19 us -> 14.1 us  [the longest x2 7.93 us: optimizer(): pl.pallas_call(functools.partial(step_kernel, jobs=jobs, chunk=chunk, sha...]
    pallas_call x2, Pallas kernels: 22.7 us -> 23.9 us  [second_pass(): pl.pallas_call(functools.partial(second_kernel, groups=groups, index=inde...]
  transfers between devices with their start and end apart: 30 -> 30, of which waited for: 8 -> 6; matrix products, arithmetic and copies ran while one was open for 0% -> 0% of each run, Pallas kernels for 36% -> 35%
where the time goes in v5:
time: 121 us; the launch traced here: 120 us
  Pallas kernels  56.1 us (46%)
  starting transfers between devices  52.2 us (43%)
  waiting for transfers between devices  10.9 us (9%)
    ppermute x15, starting transfers between devices, proto_swap(): return lax.ppermute(x, 'proto', xor_pairs(protos, k))  32.5 us
    pallas_call x2, Pallas kernels, second_pass(): pl.pallas_call(functools.partial(second_kernel, groups=groups, index=inde...  23.9 us
    ppermute x15, starting transfers between devices, dp_swap(): return lax.ppermute(x, 'dp', xor_pairs(groups, k))  19.8 us
    pallas_call x1, Pallas kernels, first_pass(): pl.pallas_call(functools.partial(first_kernel, count=count), in_specs=[pl...  12 us
    ppermute x15, waiting for transfers between devices, proto_swap(): return lax.ppermute(x, 'proto', xor_pairs(protos, k))  10.8 us
    pallas_call x2, Pallas kernels, optimizer(): pl.pallas_call(functools.partial(step_kernel, jobs=jobs, chunk=chunk, sha...  7.93 us
    pallas_call x1, Pallas kernels, round_protos(): pl.pallas_call(functools.partial(round_kernel, tile=tile, depth=depth), i...  6.12 us
    pallas_call x1, Pallas kernels, lay_rows(): pl.pallas_call(functools.partial(lay_kernel, count=count, groups=groups),...  3.65 us
  transfers between devices with their start and end apart: 30, of which 6 were waited for; matrix products, arithmetic and copies ran while one was open for 0% of the time, Pallas kernels for 35%

profile of v5, /device:TPU:0, one launch (start us, length us, event | category | flops | bytes accessed | tf_op | source)
XLA Modules:
  0.0 120.4 jit_solution(7680634169426006011)
XLA Ops:
  0.6 1.2 pick_rows.1
  1.8 0.0 copy-start.2
  1.8 5.1 %collective-permute-start.2 = (bf16[144,256]{1,0:T(8,128)(2,1)S(1)}, bf16[144,256]{1,0:T(8,128)(2,1)S(1)}, u32[]{:S(2)}, u32[]{:S(2)}) collective-permute-start(bf16[144,256]{1,0:T(8,128)(2,1)S(1)} %get-tuple-element.81), channel_id=1, source_target_pairs={{0,6},{1,7},{2,4},{3,5},{4,2},{5,3},{6,0},{7,1},{8,14},{9,15},{10,... | collective-permute-start | bytes 221192 | tf_op jit(solution)/shard_map/ppermute | solution.py:606
  7.0 0.6 collective-permute-start
  7.6 6.1 %round_protos.1 = (bf16[256,8192]{1,0:T(8,128)(2,1)S(1)}, bf16[256,8192]{1,0:T(8,128)(2,1)S(1)}) custom-call(f32[256,16384]{1,0:T(8,128)} %refs_6_.2, f32[256,16384]{1,0:T(8,128)} %refs_7_.2), custom_call_target="tpu_custom_call" | custom-call | bytes 25165824 | tf_op jit(solution)/shard_map/round_protos/pallas_call | solution.py:118
  13.8 0.0 collective-permute-done.1
  13.8 0.0 collective-permute-done
  13.8 0.1 collective-permute-start.3
  13.9 2.7 %collective-permute-start.7 = (bf16[576,256]{1,0:T(8,128)(2,1)S(1)}, bf16[576,256]{1,0:T(8,128)(2,1)S(1)}, u32[]{:S(2)}, u32[]{:S(2)}) collective-permute-start(bf16[576,256]{1,0:T(8,128)(2,1)S(1)} %constant_dynamic-update-slice_fusion.own_ref.refs_0_.refs_4_), channel_id=1, source_target_pairs={{0,24},{8,16},{16,8},{24,0},{1,25},{9,17},{17,9},{25,1},{2,26},{10... | collective-permute-start | bytes 884744 | tf_op jit(solution)/shard_map/ppermute | solution.py:609
  16.6 0.5 collective-permute-start.6
  17.1 0.4 collective-permute-start.5
  17.5 12.0 %first_pass.1.own_ref = f32[8,512]{1,0:T(8,128)S(1)} custom-call(bf16[576,256]{1,0:T(8,128)(2,1)S(1)} %constant_dynamic-update-slice_fusion.own_ref.refs_0_.refs_4_, bf16[576,256]{1,0:T(8,128)(2,1)S(1)} %collective-permute-done.3.other_ref.refs_1_.refs_5_, bf16[256,8192]{1,0:T(8,128)(2,1)S(1)} %get-tuple-element.87.ws_ref, ...), custom_call_target="tpu_custom_call" | custom-call | flops 8589934592 | bytes 25165824 | tf_op jit(solution)/shard_map/first_pass/pallas_call | solution.py:217
  29.5 0.1 collective-permute-start.4
  29.6 1.2 collective-permute-done.4.other_ref
  30.8 0.0 collective-permute-done.7.refs_6_
  30.8 0.0 collective-permute-done.5.refs_2_
  30.8 0.2 collective-permute-start.8
  31.1 0.3 collective-permute-start.9
  31.4 0.2 collective-permute-start.10
  31.6 3.7 %collective-permute-start.13 = (f32[8,512]{1,0:T(8,128)S(1)}, f32[8,512]{1,0:T(8,128)S(1)}, u32[]{:S(2)}, u32[]{:S(2)}) collective-permute-start(f32[8,512]{1,0:T(8,128)S(1)} %core_join.1.refs_0_), channel_id=1, source_target_pairs={{0,6},{1,7},{2,4},{3,5},{4,2},{5,3},{6,0},{7,1},{8,14},{9,15},{10,... | collective-permute-start | bytes 49160 | tf_op jit(solution)/shard_map/ppermute | solution.py:606
  35.3 17.0 %collective-permute-start.12 = (f32[8,512]{1,0:T(8,128)S(1)}, f32[8,512]{1,0:T(8,128)S(1)}, u32[]{:S(2)}, u32[]{:S(2)}) collective-permute-start(f32[8,512]{1,0:T(8,128)S(1)} %core_join.1.refs_0_), channel_id=1, source_target_pairs={{0,4},{1,5},{2,6},{3,7},{4,0},{5,1},{6,2},{7,3},{8,12},{9,13},{10,... | collective-permute-start | bytes 49160 | tf_op jit(solution)/shard_map/ppermute | solution.py:606
  52.3 0.0 collective-permute-done.13.refs_3_
  52.3 2.3 %collective-permute-start.11 = (f32[8,512]{1,0:T(8,128)S(1)}, f32[8,512]{1,0:T(8,128)S(1)}, u32[]{:S(2)}, u32[]{:S(2)}) collective-permute-start(f32[8,512]{1,0:T(8,128)S(1)} %core_join.1.refs_0_), channel_id=1, source_target_pairs={{0,2},{1,3},{2,0},{3,1},{4,6},{5,7},{6,4},{7,5},{8,10},{9,11},{10,... | collective-permute-start | bytes 49160 | tf_op jit(solution)/shard_map/ppermute | solution.py:606
  54.6 0.0 collective-permute-done.12.refs_2_
  54.6 1.7 %collective-permute-done.11.refs_1_ = f32[8,512]{1,0:T(8,128)S(1)} collective-permute-done((f32[8,512]{1,0:T(8,128)S(1)}, f32[8,512]{1,0:T(8,128)S(1)}, u32[]{:S(2)}, u32[]{:S(2)}) %collective-permute-start.11) | collective-permute-done | bytes 16416 | tf_op jit(solution)/shard_map/ppermute | solution.py:606
  56.3 0.2 final_join.1
  56.5 0.0 collective-permute-start.16
  56.6 4.2 %collective-permute-start.15 = (f32[8,512]{1,0:T(8,128)S(1)}, f32[8,512]{1,0:T(8,128)S(1)}, u32[]{:S(2)}, u32[]{:S(2)}) collective-permute-start(f32[8,512]{1,0:T(8,128)S(1)} %get-tuple-element.98.refs_0_), channel_id=1, source_target_pairs={{0,16},{8,24},{16,0},{24,8},{1,17},{9,25},{17,1},{25,9},{2,18},{10... | collective-permute-start | bytes 49160 | tf_op jit(solution)/shard_map/ppermute | solution.py:609
  60.7 1.4 %collective-permute-start.14 = (f32[8,512]{1,0:T(8,128)S(1)}, f32[8,512]{1,0:T(8,128)S(1)}, u32[]{:S(2)}, u32[]{:S(2)}) collective-permute-start(f32[8,512]{1,0:T(8,128)S(1)} %get-tuple-element.98.refs_0_), channel_id=1, source_target_pairs={{0,8},{8,0},{16,24},{24,16},{1,9},{9,1},{17,25},{25,17},{2,10},{10... | collective-permute-start | bytes 49160 | tf_op jit(solution)/shard_map/ppermute | solution.py:609
  62.1 0.0 collective-permute-done.9.refs_5_
  62.1 0.0 collective-permute-done.10.refs_7_
  62.1 3.6 %lay_rows.1 = (bf16[2048,256]{1,0:T(8,128)(2,1)S(1)}, bf16[2048,256]{1,0:T(8,128)(2,1)S(1)}, bf16[256,2048]{1,0:T(8,128)(2,1)S(1)}, bf16[256,4096]{1,0:T(8,128)(2,1)S(1)}, bf16[256,4096]{1,0:T(8,128)(2,1)S(1)}) custom-call(s32[1]{0:T(128)} %bitcast.place_ref.refs_5_, bf16[576,256]{1,0:T(8,128)(2,1)S(1)} %constant_dynamic-update-slice_fusion.own_ref.refs_0_.refs_4_, ...), custom_call_target="tpu_custom_call" | custom-call | bytes 4194304 | tf_op jit(solution)/shard_map/lay_rows/pallas_call | solution.py:308
  65.8 0.0 collective-permute-done.16.refs_3_
  65.8 12.0 %second_pass.2 = (bf16[64,2048]{1,0:T(8,128)(2,1)S(1)}, bf16[64,2048]{1,0:T(8,128)(2,1)S(1)}, bf16[64,2048]{1,0:T(8,128)(2,1)S(1)}, bf16[64,2048]{1,0:T(8,128)(2...) custom-call(bf16[2048,256]{1,0:T(8,128)(2,1)S(1)} %get-tuple-element, ...), custom_call_target="tpu_custom_call" | custom-call | flops 8589934592 | bytes 4194304 | tf_op jit(solution)/shard_map/second_pass/pallas_call | solution.py:451
  77.8 0.7 collective-permute-start.17
  78.5 1.5 %collective-permute-start.18 = (bf16[64,2048]{1,0:T(8,128)(2,1)S(1)}, bf16[64,2048]{1,0:T(8,128)(2,1)S(1)}, u32[]{:S(2)}, u32[]{:S(2)}) collective-permute-start(bf16[64,2048]{1,0:T(8,128)(2,1)S(1)} %get-tuple-element.106), channel_id=1, source_target_pairs={{0,16},{8,24},{16,0},{24,8},{1,17},{9,25},{17,1},{25,9},{2,18},{10... | collective-permute-start | bytes 786440 | tf_op jit(solution)/shard_map/ppermute | solution.py:609
  80.0 1.4 %collective-permute-start.19 = (bf16[64,2048]{1,0:T(8,128)(2,1)S(1)}, bf16[64,2048]{1,0:T(8,128)(2,1)S(1)}, u32[]{:S(2)}, u32[]{:S(2)}) collective-permute-start(bf16[64,2048]{1,0:T(8,128)(2,1)S(1)} %get-tuple-element.107), channel_id=1, source_target_pairs={{0,24},{8,16},{16,8},{24,0},{1,25},{9,17},{17,9},{25,1},{2,26},{10... | collective-permute-start | bytes 786440 | tf_op jit(solution)/shard_map/ppermute | solution.py:609
  81.4 12.0 %second_pass.3 = (bf16[64,2048]{1,0:T(8,128)(2,1)S(1)}, bf16[64,2048]{1,0:T(8,128)(2,1)S(1)}, bf16[64,2048]{1,0:T(8,128)(2,1)S(1)}, bf16[64,2048]{1,0:T(8,128)(2...) custom-call(bf16[2048,256]{1,0:T(8,128)(2,1)S(1)} %get-tuple-element.92.us, ...), custom_call_target="tpu_custom_call" | custom-call | flops 8589934592 | bytes 4194304 | tf_op jit(solution)/shard_map/second_pass/pallas_call | solution.py:451
  93.3 0.0 collective-permute-done.18.refs_2_
  93.3 0.0 collective-permute-done.19.refs_3_
  93.4 0.1 collective-permute-start.20
  93.4 1.9 %collective-permute-done.20.got_ref = bf16[1040,256]{1,0:T(8,128)(2,1)S(1)} collective-permute-done((bf16[1040,256]{1,0:T(8,128)(2,1)S(1)}, bf16[1040,256]{1,0:T(8,128)(2,1)S(1)}, u32[]{:S(2)}, u32[]{:S(2)}) %collective-permute-start.20) | collective-permute-done | bytes 532512 | tf_op jit(solution)/shard_map/ppermute | solution.py:606
  95.3 0.1 core_sum.1
  95.5 0.1 collective-permute-start.21
  95.6 2.0 %collective-permute-start.27 = (bf16[64,2048]{1,0:T(8,128)(2,1)S(1)}, bf16[64,2048]{1,0:T(8,128)(2,1)S(1)}, u32[]{:S(2)}, u32[]{:S(2)}) collective-permute-start(bf16[64,2048]{1,0:T(8,128)(2,1)S(1)} %get-tuple-element.136), channel_id=1, source_target_pairs={{0,8},{8,0},{16,24},{24,16},{1,9},{9,1},{17,25},{25,17},{2,10},{10... | collective-permute-start | bytes 786440 | tf_op jit(solution)/shard_map/ppermute | solution.py:609
  97.5 0.2 collective-permute-start.28
  97.7 1.4 %collective-permute-start.29 = (bf16[64,2048]{1,0:T(8,128)(2,1)S(1)}, bf16[64,2048]{1,0:T(8,128)(2,1)S(1)}, u32[]{:S(2)}, u32[]{:S(2)}) collective-permute-start(bf16[64,2048]{1,0:T(8,128)(2,1)S(1)} %get-tuple-element.138), channel_id=1, source_target_pairs={{0,24},{8,16},{16,8},{24,0},{1,25},{9,17},{17,9},{25,1},{2,26},{10... | collective-permute-start | bytes 786440 | tf_op jit(solution)/shard_map/ppermute | solution.py:609
  99.1 0.5 collective-permute-start.22
  99.6 1.7 %collective-permute-done.21.refs_0_ = bf16[272,256]{1,0:T(8,128)(2,1)S(1)} collective-permute-done((bf16[272,256]{1,0:T(8,128)(2,1)S(1)}, bf16[272,256]{1,0:T(8,128)(2,1)S(1)}, u32[]{:S(2)}, u32[]{:S(2)}) %collective-permute-start.21) | collective-permute-done | bytes 139296 | tf_op jit(solution)/shard_map/ppermute | solution.py:606
  101.3 2.2 %collective-permute-start.23 = (bf16[272,256]{1,0:T(8,128)(2,1)S(1)}, bf16[272,256]{1,0:T(8,128)(2,1)S(1)}, u32[]{:S(2)}, u32[]{:S(2)}) collective-permute-start(bf16[272,256]{1,0:T(8,128)(2,1)S(1)} %get-tuple-element.114), channel_id=1, source_target_pairs={{0,6},{1,7},{2,4},{3,5},{4,2},{5,3},{6,0},{7,1},{8,14},{9,15},{10,... | collective-permute-start | bytes 417800 | tf_op jit(solution)/shard_map/ppermute | solution.py:606
  103.4 4.6 %optimizer.2 = (f32[64,16384]{1,0:T(8,128)}, f32[64,16384]{1,0:T(8,128)}, f32[64,16384]{1,0:T(8,128)}, f32[64,16384]{1,0:T(8,128)}) custom-call(s32[1]{0:T(128)} %bitcast.place_ref.refs_5_, bf16[64,2048]{1,0:T(8,128)(2,1)S(1)} %get-tuple-element.115.refs_0_, bf16[64,2048]{1,0:T(8,128)(2,1)S(1)} %collective-permute-done.17.refs_1_, ...), custom_call_target="tpu_custom_call" | custom-call | flops 13107200 | bytes 10485760 | tf_op jit(solution)/shard_map/optimizer/pallas_call | solution.py:569
  108.1 4.3 %collective-permute-done.22.refs_1_ = bf16[272,256]{1,0:T(8,128)(2,1)S(1)} collective-permute-done((bf16[272,256]{1,0:T(8,128)(2,1)S(1)}, bf16[272,256]{1,0:T(8,128)(2,1)S(1)}, u32[]{:S(2)}, u32[]{:S(2)}) %collective-permute-start.22) | collective-permute-done | bytes 139296 | tf_op jit(solution)/shard_map/ppermute | solution.py:606
  112.4 0.0 collective-permute-done.23.refs_2_
  112.4 0.1 axis_sum.1
  112.5 0.7 collective-permute-start.24
  113.2 1.4 %collective-permute-start.25 = (bf16[80,256]{1,0:T(8,128)(2,1)S(1)}, bf16[80,256]{1,0:T(8,128)(2,1)S(1)}, u32[]{:S(2)}, u32[]{:S(2)}) collective-permute-start(bf16[80,256]{1,0:T(8,128)(2,1)S(1)} %get-tuple-element.134), channel_id=1, source_target_pairs={{0,16},{8,24},{16,0},{24,8},{1,17},{9,25},{17,1},{25,9},{2,18},{10... | collective-permute-start | bytes 122888 | tf_op jit(solution)/shard_map/ppermute | solution.py:609
  114.6 0.0 collective-permute-done.27.refs_0_
  114.6 1.5 %collective-permute-start.26 = (bf16[80,256]{1,0:T(8,128)(2,1)S(1)}, bf16[80,256]{1,0:T(8,128)(2,1)S(1)}, u32[]{:S(2)}, u32[]{:S(2)}) collective-permute-start(bf16[80,256]{1,0:T(8,128)(2,1)S(1)} %get-tuple-element.135), channel_id=1, source_target_pairs={{0,24},{8,16},{16,8},{24,0},{1,25},{9,17},{17,9},{25,1},{2,26},{10... | collective-permute-start | bytes 122888 | tf_op jit(solution)/shard_map/ppermute | solution.py:609
  116.0 0.0 collective-permute-done.28.refs_1_
  116.0 0.0 collective-permute-done.29.refs_2_
  116.0 3.3 %optimizer.3 = (f32[64,16384]{1,0:T(8,128)}, f32[64,16384]{1,0:T(8,128)}, f32[64,16384]{1,0:T(8,128)}, f32[64,16384]{1,0:T(8,128)}) custom-call(s32[1]{0:T(128)} %bitcast.place_ref.refs_5_, bf16[64,2048]{1,0:T(8,128)(2,1)S(1)} %collective-permute-done.27.refs_0_, ...), custom_call_target="tpu_custom_call", output_to_operand_aliasing={{0}: (8, {}), {1}: (9, {}), {2}: (10, {}), {3}: (11, {})} | custom-call | flops 7864320 | bytes 6291456 | tf_op jit(solution)/shard_map/optimizer/pallas_call | solution.py:569
  119.4 0.0 collective-permute-done.25.refs_1_
  119.4 0.1 collective-permute-done.26.refs_2_
  119.5 0.8 row_grad.1
  (20 shorter events, 0.1 us)
Async XLA Ops:
  1.8 15.6 %copy-start.2 = (f32[16384]{0:T(1024)S(1)}, f32[16384]{0:T(1024)}, u32[]{:S(2)}) copy-start(f32[16384]{0:T(1024)} %param.17) | copy-start | bytes 196612
  1.8 11.9 %collective-permute-start.2 = (bf16[144,256]{1,0:T(8,128)(2,1)S(1)}, bf16[144,256]{1,0:T(8,128)(2,1)S(1)}, u32[]{:S(2)}, u32[]{:S(2)}) collective-permute-start(bf16[144,256]{1,0:T(8,128)(2,1)S(1)} %get-tuple-element.81), channel_id=1, source_target_pairs={{0,6},{1,7},{2,4},{3,5},{4,2},{5,3},{6,0},{7,1},{8,14},{9,15},{10,... | collective-permute-start | bytes 221192 | tf_op jit(solution)/shard_map/ppermute | solution.py:606
  7.0 6.8 %collective-permute-start.1 = (bf16[144,256]{1,0:T(8,128)(2,1)S(1)}, bf16[144,256]{1,0:T(8,128)(2,1)S(1)}, u32[]{:S(2)}, u32[]{:S(2)}) collective-permute-start(bf16[144,256]{1,0:T(8,128)(2,1)S(1)} %get-tuple-element.81), channel_id=1, source_target_pairs={{0,4},{1,5},{2,6},{3,7},{4,0},{5,1},{6,2},{7,3},{8,12},{9,13},{10,... | collective-permute-start | bytes 221192 | tf_op jit(solution)/shard_map/ppermute | solution.py:606
  7.0 6.8 %collective-permute-start = (bf16[144,256]{1,0:T(8,128)(2,1)S(1)}, bf16[144,256]{1,0:T(8,128)(2,1)S(1)}, u32[]{:S(2)}, u32[]{:S(2)}) collective-permute-start(bf16[144,256]{1,0:T(8,128)(2,1)S(1)} %get-tuple-element.81), channel_id=1, source_target_pairs={{0,2},{1,3},{2,0},{3,1},{4,6},{5,7},{6,4},{7,5},{8,10},{9,11},{10,... | collective-permute-start | bytes 221192 | tf_op jit(solution)/shard_map/ppermute | solution.py:606
  13.8 3.6 %collective-permute-start.3 = (bf16[576,256]{1,0:T(8,128)(2,1)S(1)}, bf16[576,256]{1,0:T(8,128)(2,1)S(1)}, u32[]{:S(2)}, u32[]{:S(2)}) collective-permute-start(bf16[576,256]{1,0:T(8,128)(2,1)S(1)} %constant_dynamic-update-slice_fusion.own_ref.refs_0_.refs_4_), channel_id=1, source_target_pairs={{0,1},{1,0},{2,3},{3,2},{4,5},{5,4},{6,7},{7,6},{8,9},{9,8},{10,11... | collective-permute-start | bytes 884744 | tf_op jit(solution)/shard_map/ppermute | solution.py:606
  13.9 16.9 %collective-permute-start.7 = (bf16[576,256]{1,0:T(8,128)(2,1)S(1)}, bf16[576,256]{1,0:T(8,128)(2,1)S(1)}, u32[]{:S(2)}, u32[]{:S(2)}) collective-permute-start(bf16[576,256]{1,0:T(8,128)(2,1)S(1)} %constant_dynamic-update-slice_fusion.own_ref.refs_0_.refs_4_), channel_id=1, source_target_pairs={{0,24},{8,16},{16,8},{24,0},{1,25},{9,17},{17,9},{25,1},{2,26},{10... | collective-permute-start | bytes 884744 | tf_op jit(solution)/shard_map/ppermute | solution.py:609
  16.6 14.2 %collective-permute-start.6 = (bf16[576,256]{1,0:T(8,128)(2,1)S(1)}, bf16[576,256]{1,0:T(8,128)(2,1)S(1)}, u32[]{:S(2)}, u32[]{:S(2)}) collective-permute-start(bf16[576,256]{1,0:T(8,128)(2,1)S(1)} %constant_dynamic-update-slice_fusion.own_ref.refs_0_.refs_4_), channel_id=1, source_target_pairs={{0,16},{8,24},{16,0},{24,8},{1,17},{9,25},{17,1},{25,9},{2,18},{10... | collective-permute-start | bytes 884744 | tf_op jit(solution)/shard_map/ppermute | solution.py:609
  17.1 13.8 %collective-permute-start.5 = (bf16[576,256]{1,0:T(8,128)(2,1)S(1)}, bf16[576,256]{1,0:T(8,128)(2,1)S(1)}, u32[]{:S(2)}, u32[]{:S(2)}) collective-permute-start(bf16[576,256]{1,0:T(8,128)(2,1)S(1)} %constant_dynamic-update-slice_fusion.own_ref.refs_0_.refs_4_), channel_id=1, source_target_pairs={{0,8},{8,0},{16,24},{24,16},{1,9},{9,1},{17,25},{25,17},{2,10},{10... | collective-permute-start | bytes 884744 | tf_op jit(solution)/shard_map/ppermute | solution.py:609
  29.5 1.2 %collective-permute-start.4 = (f32[8,512]{1,0:T(8,128)S(1)}, f32[8,512]{1,0:T(8,128)S(1)}, u32[]{:S(2)}, u32[]{:S(2)}) collective-permute-start(f32[8,512]{1,0:T(8,128)S(1)} %first_pass.1.own_ref), channel_id=1, source_target_pairs={{0,1},{1,0},{2,3},{3,2},{4,5},{5,4},{6,7},{7,6},{8,9},{9,8},{10,11... | collective-permute-start | bytes 49160 | tf_op jit(solution)/shard_map/ppermute | solution.py:606
  30.8 29.9 %collective-permute-start.8 = (bf16[576,256]{1,0:T(8,128)(2,1)S(1)}, bf16[576,256]{1,0:T(8,128)(2,1)S(1)}, u32[]{:S(2)}, u32[]{:S(2)}) collective-permute-start(bf16[576,256]{1,0:T(8,128)(2,1)S(1)} %collective-permute-done.5.refs_2_), channel_id=1, source_target_pairs={{0,1},{1,0},{2,3},{3,2},{4,5},{5,4},{6,7},{7,6},{8,9},{9,8},{10,11... | collective-permute-start | bytes 884744 | tf_op jit(solution)/shard_map/ppermute | solution.py:606
  31.1 31.1 %collective-permute-start.9 = (bf16[576,256]{1,0:T(8,128)(2,1)S(1)}, bf16[576,256]{1,0:T(8,128)(2,1)S(1)}, u32[]{:S(2)}, u32[]{:S(2)}) collective-permute-start(bf16[576,256]{1,0:T(8,128)(2,1)S(1)} %collective-permute-done.6.refs_4_), channel_id=1, source_target_pairs={{0,1},{1,0},{2,3},{3,2},{4,5},{5,4},{6,7},{7,6},{8,9},{9,8},{10,11... | collective-permute-start | bytes 884744 | tf_op jit(solution)/shard_map/ppermute | solution.py:606
  31.4 30.7 %collective-permute-start.10 = (bf16[576,256]{1,0:T(8,128)(2,1)S(1)}, bf16[576,256]{1,0:T(8,128)(2,1)S(1)}, u32[]{:S(2)}, u32[]{:S(2)}) collective-permute-start(bf16[576,256]{1,0:T(8,128)(2,1)S(1)} %collective-permute-done.7.refs_6_), channel_id=1, source_target_pairs={{0,1},{1,0},{2,3},{3,2},{4,5},{5,4},{6,7},{7,6},{8,9},{9,8},{10,11... | collective-permute-start | bytes 884744 | tf_op jit(solution)/shard_map/ppermute | solution.py:606
  31.6 20.7 %collective-permute-start.13 = (f32[8,512]{1,0:T(8,128)S(1)}, f32[8,512]{1,0:T(8,128)S(1)}, u32[]{:S(2)}, u32[]{:S(2)}) collective-permute-start(f32[8,512]{1,0:T(8,128)S(1)} %core_join.1.refs_0_), channel_id=1, source_target_pairs={{0,6},{1,7},{2,4},{3,5},{4,2},{5,3},{6,0},{7,1},{8,14},{9,15},{10,... | collective-permute-start | bytes 49160 | tf_op jit(solution)/shard_map/ppermute | solution.py:606
  35.3 19.3 %collective-permute-start.12 = (f32[8,512]{1,0:T(8,128)S(1)}, f32[8,512]{1,0:T(8,128)S(1)}, u32[]{:S(2)}, u32[]{:S(2)}) collective-permute-start(f32[8,512]{1,0:T(8,128)S(1)} %core_join.1.refs_0_), channel_id=1, source_target_pairs={{0,4},{1,5},{2,6},{3,7},{4,0},{5,1},{6,2},{7,3},{8,12},{9,13},{10,... | collective-permute-start | bytes 49160 | tf_op jit(solution)/shard_map/ppermute | solution.py:606
  52.3 4.0 %collective-permute-start.11 = (f32[8,512]{1,0:T(8,128)S(1)}, f32[8,512]{1,0:T(8,128)S(1)}, u32[]{:S(2)}, u32[]{:S(2)}) collective-permute-start(f32[8,512]{1,0:T(8,128)S(1)} %core_join.1.refs_0_), channel_id=1, source_target_pairs={{0,2},{1,3},{2,0},{3,1},{4,6},{5,7},{6,4},{7,5},{8,10},{9,11},{10,... | collective-permute-start | bytes 49160 | tf_op jit(solution)/shard_map/ppermute | solution.py:606
  56.5 9.2 %collective-permute-start.16 = (f32[8,512]{1,0:T(8,128)S(1)}, f32[8,512]{1,0:T(8,128)S(1)}, u32[]{:S(2)}, u32[]{:S(2)}) collective-permute-start(f32[8,512]{1,0:T(8,128)S(1)} %get-tuple-element.98.refs_0_), channel_id=1, source_target_pairs={{0,24},{8,16},{16,8},{24,0},{1,25},{9,17},{17,9},{25,1},{2,26},{10... | collective-permute-start | bytes 49160 | tf_op jit(solution)/shard_map/ppermute | solution.py:609
  56.6 9.2 %collective-permute-start.15 = (f32[8,512]{1,0:T(8,128)S(1)}, f32[8,512]{1,0:T(8,128)S(1)}, u32[]{:S(2)}, u32[]{:S(2)}) collective-permute-start(f32[8,512]{1,0:T(8,128)S(1)} %get-tuple-element.98.refs_0_), channel_id=1, source_target_pairs={{0,16},{8,24},{16,0},{24,8},{1,17},{9,25},{17,1},{25,9},{2,18},{10... | collective-permute-start | bytes 49160 | tf_op jit(solution)/shard_map/ppermute | solution.py:609
  60.7 5.1 %collective-permute-start.14 = (f32[8,512]{1,0:T(8,128)S(1)}, f32[8,512]{1,0:T(8,128)S(1)}, u32[]{:S(2)}, u32[]{:S(2)}) collective-permute-start(f32[8,512]{1,0:T(8,128)S(1)} %get-tuple-element.98.refs_0_), channel_id=1, source_target_pairs={{0,8},{8,0},{16,24},{24,16},{1,9},{9,1},{17,25},{25,17},{2,10},{10... | collective-permute-start | bytes 49160 | tf_op jit(solution)/shard_map/ppermute | solution.py:609
  77.8 15.5 %collective-permute-start.17 = (bf16[64,2048]{1,0:T(8,128)(2,1)S(1)}, bf16[64,2048]{1,0:T(8,128)(2,1)S(1)}, u32[]{:S(2)}, u32[]{:S(2)}) collective-permute-start(bf16[64,2048]{1,0:T(8,128)(2,1)S(1)} %get-tuple-element.105), channel_id=1, source_target_pairs={{0,8},{8,0},{16,24},{24,16},{1,9},{9,1},{17,25},{25,17},{2,10},{10... | collective-permute-start | bytes 786440 | tf_op jit(solution)/shard_map/ppermute | solution.py:609
  78.5 14.8 %collective-permute-start.18 = (bf16[64,2048]{1,0:T(8,128)(2,1)S(1)}, bf16[64,2048]{1,0:T(8,128)(2,1)S(1)}, u32[]{:S(2)}, u32[]{:S(2)}) collective-permute-start(bf16[64,2048]{1,0:T(8,128)(2,1)S(1)} %get-tuple-element.106), channel_id=1, source_target_pairs={{0,16},{8,24},{16,0},{24,8},{1,17},{9,25},{17,1},{25,9},{2,18},{10... | collective-permute-start | bytes 786440 | tf_op jit(solution)/shard_map/ppermute | solution.py:609
  80.0 13.4 %collective-permute-start.19 = (bf16[64,2048]{1,0:T(8,128)(2,1)S(1)}, bf16[64,2048]{1,0:T(8,128)(2,1)S(1)}, u32[]{:S(2)}, u32[]{:S(2)}) collective-permute-start(bf16[64,2048]{1,0:T(8,128)(2,1)S(1)} %get-tuple-element.107), channel_id=1, source_target_pairs={{0,24},{8,16},{16,8},{24,0},{1,25},{9,17},{17,9},{25,1},{2,26},{10... | collective-permute-start | bytes 786440 | tf_op jit(solution)/shard_map/ppermute | solution.py:609
  81.4 22.1 %copy-start = (f32[64,16384]{1,0:T(8,128)S(1)}, f32[64,16384]{1,0:T(8,128)}, u32[]{:S(2)}) copy-start(f32[64,16384]{1,0:T(8,128)} %refs_5_.1) | copy-start | bytes 12582916
  81.4 22.1 %copy-start.1 = (f32[64,16384]{1,0:T(8,128)S(1)}, f32[64,16384]{1,0:T(8,128)}, u32[]{:S(2)}) copy-start(f32[64,16384]{1,0:T(8,128)} %refs_6_.3) | copy-start | bytes 12582916
  93.4 2.0 %collective-permute-start.20 = (bf16[1040,256]{1,0:T(8,128)(2,1)S(1)}, bf16[1040,256]{1,0:T(8,128)(2,1)S(1)}, u32[]{:S(2)}, u32[]{:S(2)}) collective-permute-start(bf16[1040,256]{1,0:T(8,128)(2,1)S(1)} %get-tuple-element.108), channel_id=1, source_target_pairs={{0,1},{1,0},{2,3},{3,2},{4,5},{5,4},{6,7},{7,6},{8,9},{9,8},{10,11... | collective-permute-start | bytes 1597448 | tf_op jit(solution)/shard_map/ppermute | solution.py:606
  95.5 5.8 %collective-permute-start.21 = (bf16[272,256]{1,0:T(8,128)(2,1)S(1)}, bf16[272,256]{1,0:T(8,128)(2,1)S(1)}, u32[]{:S(2)}, u32[]{:S(2)}) collective-permute-start(bf16[272,256]{1,0:T(8,128)(2,1)S(1)} %get-tuple-element.112), channel_id=1, source_target_pairs={{0,2},{1,3},{2,0},{3,1},{4,6},{5,7},{6,4},{7,5},{8,10},{9,11},{10,... | collective-permute-start | bytes 417800 | tf_op jit(solution)/shard_map/ppermute | solution.py:606
  95.6 19.0 %collective-permute-start.27 = (bf16[64,2048]{1,0:T(8,128)(2,1)S(1)}, bf16[64,2048]{1,0:T(8,128)(2,1)S(1)}, u32[]{:S(2)}, u32[]{:S(2)}) collective-permute-start(bf16[64,2048]{1,0:T(8,128)(2,1)S(1)} %get-tuple-element.136), channel_id=1, source_target_pairs={{0,8},{8,0},{16,24},{24,16},{1,9},{9,1},{17,25},{25,17},{2,10},{10... | collective-permute-start | bytes 786440 | tf_op jit(solution)/shard_map/ppermute | solution.py:609
  97.5 18.5 %collective-permute-start.28 = (bf16[64,2048]{1,0:T(8,128)(2,1)S(1)}, bf16[64,2048]{1,0:T(8,128)(2,1)S(1)}, u32[]{:S(2)}, u32[]{:S(2)}) collective-permute-start(bf16[64,2048]{1,0:T(8,128)(2,1)S(1)} %get-tuple-element.137), channel_id=1, source_target_pairs={{0,16},{8,24},{16,0},{24,8},{1,17},{9,25},{17,1},{25,9},{2,18},{10... | collective-permute-start | bytes 786440 | tf_op jit(solution)/shard_map/ppermute | solution.py:609
  97.7 18.3 %collective-permute-start.29 = (bf16[64,2048]{1,0:T(8,128)(2,1)S(1)}, bf16[64,2048]{1,0:T(8,128)(2,1)S(1)}, u32[]{:S(2)}, u32[]{:S(2)}) collective-permute-start(bf16[64,2048]{1,0:T(8,128)(2,1)S(1)} %get-tuple-element.138), channel_id=1, source_target_pairs={{0,24},{8,16},{16,8},{24,0},{1,25},{9,17},{17,9},{25,1},{2,26},{10... | collective-permute-start | bytes 786440 | tf_op jit(solution)/shard_map/ppermute | solution.py:609
  99.1 13.3 %collective-permute-start.22 = (bf16[272,256]{1,0:T(8,128)(2,1)S(1)}, bf16[272,256]{1,0:T(8,128)(2,1)S(1)}, u32[]{:S(2)}, u32[]{:S(2)}) collective-permute-start(bf16[272,256]{1,0:T(8,128)(2,1)S(1)} %get-tuple-element.113), channel_id=1, source_target_pairs={{0,4},{1,5},{2,6},{3,7},{4,0},{5,1},{6,2},{7,3},{8,12},{9,13},{10,... | collective-permute-start | bytes 417800 | tf_op jit(solution)/shard_map/ppermute | solution.py:606
  101.3 11.1 %collective-permute-start.23 = (bf16[272,256]{1,0:T(8,128)(2,1)S(1)}, bf16[272,256]{1,0:T(8,128)(2,1)S(1)}, u32[]{:S(2)}, u32[]{:S(2)}) collective-permute-start(bf16[272,256]{1,0:T(8,128)(2,1)S(1)} %get-tuple-element.114), channel_id=1, source_target_pairs={{0,6},{1,7},{2,4},{3,5},{4,2},{5,3},{6,0},{7,1},{8,14},{9,15},{10,... | collective-permute-start | bytes 417800 | tf_op jit(solution)/shard_map/ppermute | solution.py:606
  112.5 6.9 %collective-permute-start.24 = (bf16[80,256]{1,0:T(8,128)(2,1)S(1)}, bf16[80,256]{1,0:T(8,128)(2,1)S(1)}, u32[]{:S(2)}, u32[]{:S(2)}) collective-permute-start(bf16[80,256]{1,0:T(8,128)(2,1)S(1)} %get-tuple-element.133), channel_id=1, source_target_pairs={{0,8},{8,0},{16,24},{24,16},{1,9},{9,1},{17,25},{25,17},{2,10},{10... | collective-permute-start | bytes 122888 | tf_op jit(solution)/shard_map/ppermute | solution.py:609
  113.2 6.2 %collective-permute-start.25 = (bf16[80,256]{1,0:T(8,128)(2,1)S(1)}, bf16[80,256]{1,0:T(8,128)(2,1)S(1)}, u32[]{:S(2)}, u32[]{:S(2)}) collective-permute-start(bf16[80,256]{1,0:T(8,128)(2,1)S(1)} %get-tuple-element.134), channel_id=1, source_target_pairs={{0,16},{8,24},{16,0},{24,8},{1,17},{9,25},{17,1},{25,9},{2,18},{10... | collective-permute-start | bytes 122888 | tf_op jit(solution)/shard_map/ppermute | solution.py:609
  114.6 4.9 %collective-permute-start.26 = (bf16[80,256]{1,0:T(8,128)(2,1)S(1)}, bf16[80,256]{1,0:T(8,128)(2,1)S(1)}, u32[]{:S(2)}, u32[]{:S(2)}) collective-permute-start(bf16[80,256]{1,0:T(8,128)(2,1)S(1)} %get-tuple-element.135), channel_id=1, source_target_pairs={{0,24},{8,16},{16,8},{24,0},{1,25},{9,17},{17,9},{25,1},{2,26},{10... | collective-permute-start | bytes 122888 | tf_op jit(solution)/shard_map/ppermute | solution.py:609

commit v6 on v5

--- a/solution.py
+++ b/solution.py
@@ -244,7 +244,7 @@
 
 
 def final_join_kernel(*refs, count, images, ratio):
-    stats, (own_ref, other_ref), (out_ref, loss_ref) = refs[:-4], refs[-4:-2], refs[-2:]
+    stats, (own_ref, other_ref, _), (out_ref, loss_ref) = refs[:-5], refs[-5:-2], refs[-2:]
     rows = stats[0].shape[1]
     pack = 2 * count + PAD
     lse = join([swap_blocks(ref[...], k, count) for k, ref in enumerate(stats)])
@@ -266,19 +266,64 @@
     loss_ref[...] = jnp.broadcast_to(own, loss_ref.shape)
 
 
+def share_kernel(place_ref, _, s_hbm, t_hbm, out_s, out_t, done_ref, buffer, rounded, sem, *, tile):
+    share = out_s.shape[1]
+    pairs = ((s_hbm, out_s), (t_hbm, out_t))
+    jobs = [(i, j) for j in range(share // tile) for i in range(2)]
+    leaving = []
+
+    def fetch(i, j):
+        span = pl.ds(pl.multiple_of(place_ref[0] * share + j * tile, tile), tile)
+        return pltpu.make_async_copy(pairs[i][0].at[:, span], buffer.at[i, j], sem.at[0, i, j])
+
+    for job in jobs:
+        fetch(*job).start()
+    for i, j in jobs:
+        fetch(i, j).wait()
+        rounded[i, j] = buffer[i, j].astype(bf16)
+        leaving.append(
+            pltpu.make_async_copy(rounded.at[i, j], pairs[i][1].at[:, pl.ds(j * tile, tile)], sem.at[1, i, j])
+        )
+        leaving[-1].start()
+    done_ref[...] = jnp.zeros_like(done_ref)
+    for copy in leaving:
+        copy.wait()
+
+
+def round_share(place, stats, student, teacher, groups):
+    width, cols = student.shape
+    share = cols // groups
+    tile = min(share, 1024)
+    steps = share // tile
+    vmem = pl.BlockSpec(memory_space=pltpu.VMEM)
+    hbm = pl.BlockSpec(memory_space=pltpu.HBM)
+    return pl.pallas_call(
+        functools.partial(share_kernel, tile=tile),
+        in_specs=[pl.BlockSpec(memory_space=pltpu.SMEM), vmem, hbm, hbm],
+        out_specs=[hbm, hbm, vmem],
+        out_shape=[pltpu.HBM((width, share), bf16)] * 2 + [jax.ShapeDtypeStruct((8, 128), f32)],
+        scratch_shapes=[
+            pltpu.VMEM((2, steps, width, tile), f32),
+            pltpu.VMEM((2, steps, width, tile), bf16),
+            pltpu.SemaphoreType.DMA((2, 2, steps)),
+        ],
+        compiler_params=params((12 * width * share >> 20) + 2),
+        cost_estimate=cost(0, 12 * width * share),
+        name="round_share",
+    )(place, stats, in_hbm(student), in_hbm(teacher))
+
+
 def lay_kernel(place_ref, *refs, count, groups):
     packs, (s_hbm, t_hbm), refs = refs[: 2 * groups], refs[2 * groups : 2 * groups + 2], refs[2 * groups + 2 :]
-    us, ut, flipped, own_s, own_t, turned, buffer, sem = refs
+    us, ut, flipped, own_s, own_t, turned, sem = refs
     share = own_s.shape[1]
     tile = share // sem.shape[1]
     copies = []
     for j in range(share // tile):
-        span = pl.ds(pl.multiple_of(place_ref[0] * share + j * tile, tile), tile)
-        inner = slice(j * tile, (j + 1) * tile)
+        inner = pl.ds(j * tile, tile)
         for i, (hbm, own) in enumerate(((s_hbm, own_s), (t_hbm, own_t))):
-            copy = pltpu.make_async_copy(hbm.at[:, span], buffer.at[i, :, inner], sem.at[i, j])
-            copy.start()
-            copies.append((copy, i, own, inner))
+            copies.append(pltpu.make_async_copy(hbm.at[:, inner], own.at[:, inner], sem.at[i, j]))
+            copies[-1].start()
     pack = 2 * count + PAD
     at = 0
     for ref in packs:
@@ -292,15 +337,13 @@
     for k in range(groups):
         start = pl.multiple_of((place_ref[0] ^ k) * slab, slab)
         flipped[k * slab : (k + 1) * slab, :] = turned[pl.ds(start, slab), :]
-    for copy, i, own, inner in copies:
+    for copy in copies:
         copy.wait()
-        own[:, inner] = buffer[i, :, inner].astype(bf16)
-
-
-def lay_rows(place, packs, student, teacher, count):
+
+
+def lay_rows(place, packs, own_s, own_t, count):
     groups = len(packs) // 2
-    width, cols = student.shape
-    share = cols // groups
+    width, share = own_s.shape
     tile = min(share, 1024)
     rows = 2 * groups * (packs[0].shape[0] // (2 * count + PAD)) * count
     vmem = pl.BlockSpec(memory_space=pltpu.VMEM)
@@ -314,13 +357,12 @@
         out_specs=[vmem] * 5,
         scratch_shapes=[
             pltpu.VMEM((width, rows), bf16),
-            pltpu.VMEM((2, width, share), f32),
             pltpu.SemaphoreType.DMA((2, share // tile)),
         ],
-        compiler_params=params((width * rows * 2 + 8 * width * share >> 20) + 2),
+        compiler_params=params((width * rows * 2 >> 20) + 2),
         cost_estimate=cost(0, 4 << 20),
         name="lay_rows",
-    )(place, *packs, in_hbm(student), in_hbm(teacher))
+    )(place, *packs, in_hbm(own_s), in_hbm(own_t))
 
 
 def pieces(value):
@@ -629,7 +671,8 @@
     packs = [own, other]
     for pair in zip(far, far_other):
         packs += list(pair)
-    us, ut, flipped, own_ws, own_wt = lay_rows(place, packs, student_proto, teacher_proto, count)
+    share_s, share_t, rounded = round_share(place, stats, student_proto, teacher_proto, groups)
+    us, ut, flipped, own_ws, own_wt = lay_rows(place, packs, share_s, share_t, count)
 
     own_centre = lax.dynamic_slice_in_dim(centre, place[0] * share, share, 1)
     near = [proto_swap(stats, k) for k in range(2, protos, 2)]
@@ -639,7 +682,7 @@
         compiler_params=params(3),
         cost_estimate=cost(0, 1 << 20),
         name="final_join",
-    )(stats, *near, own, other)
+    )(stats, *near, own, other, rounded)
     all_stats = [stats] + [dp_swap(stats, k) for k in range(1, groups)]
 
     carry = [loss_own]

time: 121 us -> 123 us (1.017)
  Pallas kernels: 56.1 us -> 60.1 us
    pallas_call x0 -> x1, Pallas kernels: none -> 5.34 us  [round_share(): pl.pallas_call(functools.partial(share_kernel, tile=tile), in_specs=[pl.B...]
    ppermute x15, waiting for transfers between devices: 10.8 us -> 7.9 us  [proto_swap(): return lax.ppermute(x, 'proto', xor_pairs(protos, k))]
    ppermute x15, starting transfers between devices: 19.8 us -> 17.7 us  [dp_swap(): return lax.ppermute(x, 'dp', xor_pairs(groups, k))]
    ppermute x15, waiting for transfers between devices: 0.13 us -> 1.9 us  [dp_swap(): return lax.ppermute(x, 'dp', xor_pairs(groups, k))]
    pallas_call x1, Pallas kernels: 3.65 us -> 2.31 us  [lay_rows(): pl.pallas_call(functools.partial(lay_kernel, count=count, groups=groups),...]
  transfers between devices with their start and end apart: 30 -> 30, of which waited for: 6 -> 6; matrix products, arithmetic and copies ran while one was open for 0% -> 0% of each run, Pallas kernels for 35% -> 38%
where the time goes in v6:
time: 123 us; the launch traced here: 122 us
  Pallas kernels  60.1 us (49%)
  starting transfers between devices  51.1 us (42%)
  waiting for transfers between devices  9.79 us (8%)
    ppermute x15, starting transfers between devices, proto_swap(): return lax.ppermute(x, 'proto', xor_pairs(protos, k))  33.4 us
    pallas_call x2, Pallas kernels, second_pass(): pl.pallas_call(functools.partial(second_kernel, groups=groups, index=inde...  23.9 us
    ppermute x15, starting transfers between devices, dp_swap(): return lax.ppermute(x, 'dp', xor_pairs(groups, k))  17.7 us
    pallas_call x1, Pallas kernels, first_pass(): pl.pallas_call(functools.partial(first_kernel, count=count), in_specs=[pl...  12 us
    pallas_call x2, Pallas kernels, optimizer(): pl.pallas_call(functools.partial(step_kernel, jobs=jobs, chunk=chunk, sha...  7.93 us
    ppermute x15, waiting for transfers between devices, proto_swap(): return lax.ppermute(x, 'proto', xor_pairs(protos, k))  7.9 us
    pallas_call x1, Pallas kernels, round_protos(): pl.pallas_call(functools.partial(round_kernel, tile=tile, depth=depth), i...  6.12 us
    pallas_call x1, Pallas kernels, round_share(): pl.pallas_call(functools.partial(share_kernel, tile=tile), in_specs=[pl.B...  5.34 us
  transfers between devices with their start and end apart: 30, of which 6 were waited for; matrix products, arithmetic and copies ran while one was open for 0% of the time, Pallas kernels for 38%

profile of v6, /device:TPU:0, one launch (start us, length us, event | category | flops | bytes accessed | tf_op | source)
XLA Modules:
  0.0 122.2 jit_solution(17073152367432749639)
XLA Ops:
  0.6 1.2 pick_rows.1
  1.8 0.0 copy-start.2
  1.8 5.1 %collective-permute-start.2 = (bf16[144,256]{1,0:T(8,128)(2,1)S(1)}, bf16[144,256]{1,0:T(8,128)(2,1)S(1)}, u32[]{:S(2)}, u32[]{:S(2)}) collective-permute-start(bf16[144,256]{1,0:T(8,128)(2,1)S(1)} %get-tuple-element.84), channel_id=1, source_target_pairs={{0,6},{1,7},{2,4},{3,5},{4,2},{5,3},{6,0},{7,1},{8,14},{9,15},{10,... | collective-permute-start | bytes 221192 | tf_op jit(solution)/shard_map/ppermute | solution.py:648
  7.0 0.0 collective-permute-start.1
  7.0 0.6 collective-permute-start
  7.6 6.1 %round_protos.1 = (bf16[256,8192]{1,0:T(8,128)(2,1)S(1)}, bf16[256,8192]{1,0:T(8,128)(2,1)S(1)}) custom-call(f32[256,16384]{1,0:T(8,128)} %refs_6_.2, f32[256,16384]{1,0:T(8,128)} %refs_7_.2), custom_call_target="tpu_custom_call" | custom-call | bytes 25165824 | tf_op jit(solution)/shard_map/round_protos/pallas_call | solution.py:118
  13.8 0.0 collective-permute-done
  13.8 0.1 collective-permute-start.3
  13.9 2.7 %collective-permute-start.7 = (bf16[576,256]{1,0:T(8,128)(2,1)S(1)}, bf16[576,256]{1,0:T(8,128)(2,1)S(1)}, u32[]{:S(2)}, u32[]{:S(2)}) collective-permute-start(bf16[576,256]{1,0:T(8,128)(2,1)S(1)} %constant_dynamic-update-slice_fusion.own_ref.refs_0_.refs_4_), channel_id=1, source_target_pairs={{0,24},{8,16},{16,8},{24,0},{1,25},{9,17},{17,9},{25,1},{2,26},{10... | collective-permute-start | bytes 884744 | tf_op jit(solution)/shard_map/ppermute | solution.py:651
  16.6 0.5 collective-permute-start.6
  17.1 0.4 collective-permute-start.5
  17.5 0.0 collective-permute-done.3.other_ref.refs_1_.refs_5_
  17.5 12.0 %first_pass.1.own_ref = f32[8,512]{1,0:T(8,128)S(1)} custom-call(bf16[576,256]{1,0:T(8,128)(2,1)S(1)} %constant_dynamic-update-slice_fusion.own_ref.refs_0_.refs_4_, bf16[576,256]{1,0:T(8,128)(2,1)S(1)} %collective-permute-done.3.other_ref.refs_1_.refs_5_, bf16[256,8192]{1,0:T(8,128)(2,1)S(1)} %get-tuple-element.90.ws_ref, ...), custom_call_target="tpu_custom_call" | custom-call | flops 8589934592 | bytes 25165824 | tf_op jit(solution)/shard_map/first_pass/pallas_call | solution.py:217
  29.5 0.1 collective-permute-start.4
  29.6 1.2 collective-permute-done.4.other_ref
  30.8 0.0 collective-permute-done.7.refs_6_
  30.8 0.0 collective-permute-done.5.refs_2_
  30.8 0.2 collective-permute-start.8
  31.1 0.3 collective-permute-start.9
  31.4 0.2 collective-permute-start.10
  31.6 3.7 %collective-permute-start.13 = (f32[8,512]{1,0:T(8,128)S(1)}, f32[8,512]{1,0:T(8,128)S(1)}, u32[]{:S(2)}, u32[]{:S(2)}) collective-permute-start(f32[8,512]{1,0:T(8,128)S(1)} %core_join.1._.refs_0_), channel_id=1, source_target_pairs={{0,6},{1,7},{2,4},{3,5},{4,2},{5,3},{6,0},{7,1},{8,14},{9,15},{10,... | collective-permute-start | bytes 49160 | tf_op jit(solution)/shard_map/ppermute | solution.py:648
  35.3 17.0 %collective-permute-start.12 = (f32[8,512]{1,0:T(8,128)S(1)}, f32[8,512]{1,0:T(8,128)S(1)}, u32[]{:S(2)}, u32[]{:S(2)}) collective-permute-start(f32[8,512]{1,0:T(8,128)S(1)} %core_join.1._.refs_0_), channel_id=1, source_target_pairs={{0,4},{1,5},{2,6},{3,7},{4,0},{5,1},{6,2},{7,3},{8,12},{9,13},{10,... | collective-permute-start | bytes 49160 | tf_op jit(solution)/shard_map/ppermute | solution.py:648
  52.3 0.0 collective-permute-done.13.refs_3_
  52.3 2.3 %collective-permute-start.11 = (f32[8,512]{1,0:T(8,128)S(1)}, f32[8,512]{1,0:T(8,128)S(1)}, u32[]{:S(2)}, u32[]{:S(2)}) collective-permute-start(f32[8,512]{1,0:T(8,128)S(1)} %core_join.1._.refs_0_), channel_id=1, source_target_pairs={{0,2},{1,3},{2,0},{3,1},{4,6},{5,7},{6,4},{7,5},{8,10},{9,11},{10,... | collective-permute-start | bytes 49160 | tf_op jit(solution)/shard_map/ppermute | solution.py:648
  54.6 5.3 %round_share.1 = (bf16[256,4096]{1,0:T(8,128)(2,1)}, bf16[256,4096]{1,0:T(8,128)(2,1)}, f32[8,128]{1,0:T(8,128)S(1)}) custom-call(s32[1]{0:T(128)} %bitcast.place_ref.refs_5_, f32[8,512]{1,0:T(8,128)S(1)} %core_join.1._.refs_0_, f32[256,16384]{1,0:T(8,128)} %refs_6_.2, f32[256,16384]{1,0:T(8,128)} %refs_7_.2), custom_call_target="tpu_custom_call" | custom-call | bytes 12582912 | tf_op jit(solution)/shard_map/round_share/pallas_call | solution.py:300
  59.9 0.0 collective-permute-done.12.refs_2_
  60.0 0.2 final_join.1
  60.2 0.0 collective-permute-start.16
  60.2 3.5 %collective-permute-start.15 = (f32[8,512]{1,0:T(8,128)S(1)}, f32[8,512]{1,0:T(8,128)S(1)}, u32[]{:S(2)}, u32[]{:S(2)}) collective-permute-start(f32[8,512]{1,0:T(8,128)S(1)} %get-tuple-element.104.refs_0_), channel_id=1, source_target_pairs={{0,16},{8,24},{16,0},{24,8},{1,17},{9,25},{17,1},{25,9},{2,18},{10... | collective-permute-start | bytes 49160 | tf_op jit(solution)/shard_map/ppermute | solution.py:651
  63.7 0.0 collective-permute-start.14
  63.8 2.3 %lay_rows.1 = (bf16[2048,256]{1,0:T(8,128)(2,1)S(1)}, bf16[2048,256]{1,0:T(8,128)(2,1)S(1)}, bf16[256,2048]{1,0:T(8,128)(2,1)S(1)}, bf16[256,4096]{1,0:T(8,128)(2,1)S(1)}, bf16[256,4096]{1,0:T(8,128)(2,1)S(1)}) custom-call(s32[1]{0:T(128)} %bitcast.place_ref.refs_5_, bf16[576,256]{1,0:T(8,128)(2,1)S(1)} %constant_dynamic-update-slice_fusion.own_ref.refs_0_.refs_4_, ...), custom_call_target="tpu_custom_call" | custom-call | bytes 4194304 | tf_op jit(solution)/shard_map/lay_rows/pallas_call | solution.py:351
  66.1 0.0 collective-permute-done.16.refs_3_
  66.1 1.4 %collective-permute-done.14.refs_1_ = f32[8,512]{1,0:T(8,128)S(1)} collective-permute-done((f32[8,512]{1,0:T(8,128)S(1)}, f32[8,512]{1,0:T(8,128)S(1)}, u32[]{:S(2)}, u32[]{:S(2)}) %collective-permute-start.14) | collective-permute-done | bytes 16416 | tf_op jit(solution)/shard_map/ppermute | solution.py:651
  67.5 12.0 %second_pass.2 = (bf16[64,2048]{1,0:T(8,128)(2,1)S(1)}, bf16[64,2048]{1,0:T(8,128)(2,1)S(1)}, bf16[64,2048]{1,0:T(8,128)(2,1)S(1)}, bf16[64,2048]{1,0:T(8,128)(2...) custom-call(bf16[2048,256]{1,0:T(8,128)(2,1)S(1)} %get-tuple-element, ...), custom_call_target="tpu_custom_call" | custom-call | flops 8589934592 | bytes 4194304 | tf_op jit(solution)/shard_map/second_pass/pallas_call | solution.py:493
  79.4 0.7 collective-permute-start.17
  80.2 1.4 %collective-permute-start.18 = (bf16[64,2048]{1,0:T(8,128)(2,1)S(1)}, bf16[64,2048]{1,0:T(8,128)(2,1)S(1)}, u32[]{:S(2)}, u32[]{:S(2)}) collective-permute-start(bf16[64,2048]{1,0:T(8,128)(2,1)S(1)} %get-tuple-element.112), channel_id=1, source_target_pairs={{0,16},{8,24},{16,0},{24,8},{1,17},{9,25},{17,1},{25,9},{2,18},{10... | collective-permute-start | bytes 786440 | tf_op jit(solution)/shard_map/ppermute | solution.py:651
  81.6 1.4 %collective-permute-start.19 = (bf16[64,2048]{1,0:T(8,128)(2,1)S(1)}, bf16[64,2048]{1,0:T(8,128)(2,1)S(1)}, u32[]{:S(2)}, u32[]{:S(2)}) collective-permute-start(bf16[64,2048]{1,0:T(8,128)(2,1)S(1)} %get-tuple-element.113), channel_id=1, source_target_pairs={{0,24},{8,16},{16,8},{24,0},{1,25},{9,17},{17,9},{25,1},{2,26},{10... | collective-permute-start | bytes 786440 | tf_op jit(solution)/shard_map/ppermute | solution.py:651
  83.0 12.0 %second_pass.3 = (bf16[64,2048]{1,0:T(8,128)(2,1)S(1)}, bf16[64,2048]{1,0:T(8,128)(2,1)S(1)}, bf16[64,2048]{1,0:T(8,128)(2,1)S(1)}, bf16[64,2048]{1,0:T(8,128)(2...) custom-call(bf16[2048,256]{1,0:T(8,128)(2,1)S(1)} %get-tuple-element.98.us, ...), custom_call_target="tpu_custom_call" | custom-call | flops 8589934592 | bytes 4194304 | tf_op jit(solution)/shard_map/second_pass/pallas_call | solution.py:493
  95.0 0.0 collective-permute-done.18.refs_2_
  95.0 0.0 collective-permute-done.19.refs_3_
  95.0 0.1 collective-permute-start.20
  95.1 1.9 %collective-permute-done.20.got_ref = bf16[1040,256]{1,0:T(8,128)(2,1)S(1)} collective-permute-done((bf16[1040,256]{1,0:T(8,128)(2,1)S(1)}, bf16[1040,256]{1,0:T(8,128)(2,1)S(1)}, u32[]{:S(2)}, u32[]{:S(2)}) %collective-permute-start.20) | collective-permute-done | bytes 532512 | tf_op jit(solution)/shard_map/ppermute | solution.py:648
  97.0 0.1 core_sum.1
  97.1 0.8 collective-permute-start.21
  97.9 1.4 %collective-permute-start.27 = (bf16[64,2048]{1,0:T(8,128)(2,1)S(1)}, bf16[64,2048]{1,0:T(8,128)(2,1)S(1)}, u32[]{:S(2)}, u32[]{:S(2)}) collective-permute-start(bf16[64,2048]{1,0:T(8,128)(2,1)S(1)} %get-tuple-element.142), channel_id=1, source_target_pairs={{0,8},{8,0},{16,24},{24,16},{1,9},{9,1},{17,25},{25,17},{2,10},{10... | collective-permute-start | bytes 786440 | tf_op jit(solution)/shard_map/ppermute | solution.py:651
  99.2 2.0 %collective-permute-start.28 = (bf16[64,2048]{1,0:T(8,128)(2,1)S(1)}, bf16[64,2048]{1,0:T(8,128)(2,1)S(1)}, u32[]{:S(2)}, u32[]{:S(2)}) collective-permute-start(bf16[64,2048]{1,0:T(8,128)(2,1)S(1)} %get-tuple-element.143), channel_id=1, source_target_pairs={{0,16},{8,24},{16,0},{24,8},{1,17},{9,25},{17,1},{25,9},{2,18},{10... | collective-permute-start | bytes 786440 | tf_op jit(solution)/shard_map/ppermute | solution.py:651
  101.2 0.1 collective-permute-start.29
  101.4 0.8 collective-permute-start.22
  102.1 0.7 collective-permute-done.21.refs_0_
  102.9 2.2 %collective-permute-start.23 = (bf16[272,256]{1,0:T(8,128)(2,1)S(1)}, bf16[272,256]{1,0:T(8,128)(2,1)S(1)}, u32[]{:S(2)}, u32[]{:S(2)}) collective-permute-start(bf16[272,256]{1,0:T(8,128)(2,1)S(1)} %get-tuple-element.120), channel_id=1, source_target_pairs={{0,6},{1,7},{2,4},{3,5},{4,2},{5,3},{6,0},{7,1},{8,14},{9,15},{10,... | collective-permute-start | bytes 417800 | tf_op jit(solution)/shard_map/ppermute | solution.py:648
  105.0 4.6 %optimizer.2 = (f32[64,16384]{1,0:T(8,128)}, f32[64,16384]{1,0:T(8,128)}, f32[64,16384]{1,0:T(8,128)}, f32[64,16384]{1,0:T(8,128)}) custom-call(s32[1]{0:T(128)} %bitcast.place_ref.refs_5_, bf16[64,2048]{1,0:T(8,128)(2,1)S(1)} %get-tuple-element.121.refs_0_, bf16[64,2048]{1,0:T(8,128)(2,1)S(1)} %collective-permute-done.17.refs_1_, ...), custom_call_target="tpu_custom_call" | custom-call | flops 13107200 | bytes 10485760 | tf_op jit(solution)/shard_map/optimizer/pallas_call | solution.py:611
  109.7 4.1 %collective-permute-done.22.refs_1_ = bf16[272,256]{1,0:T(8,128)(2,1)S(1)} collective-permute-done((bf16[272,256]{1,0:T(8,128)(2,1)S(1)}, bf16[272,256]{1,0:T(8,128)(2,1)S(1)}, u32[]{:S(2)}, u32[]{:S(2)}) %collective-permute-start.22) | collective-permute-done | bytes 139296 | tf_op jit(solution)/shard_map/ppermute | solution.py:648
  113.7 0.0 collective-permute-done.23.refs_2_
  113.7 0.1 axis_sum.1
  113.8 1.0 collective-permute-start.24
  114.9 1.5 %collective-permute-start.25 = (bf16[80,256]{1,0:T(8,128)(2,1)S(1)}, bf16[80,256]{1,0:T(8,128)(2,1)S(1)}, u32[]{:S(2)}, u32[]{:S(2)}) collective-permute-start(bf16[80,256]{1,0:T(8,128)(2,1)S(1)} %get-tuple-element.140), channel_id=1, source_target_pairs={{0,16},{8,24},{16,0},{24,8},{1,17},{9,25},{17,1},{25,9},{2,18},{10... | collective-permute-start | bytes 122888 | tf_op jit(solution)/shard_map/ppermute | solution.py:651
  116.3 0.0 collective-permute-done.27.refs_0_
  116.3 1.1 collective-permute-start.26
  117.4 0.0 collective-permute-done.28.refs_1_
  117.4 0.0 collective-permute-done.29.refs_2_
  117.4 3.3 %optimizer.3 = (f32[64,16384]{1,0:T(8,128)}, f32[64,16384]{1,0:T(8,128)}, f32[64,16384]{1,0:T(8,128)}, f32[64,16384]{1,0:T(8,128)}) custom-call(s32[1]{0:T(128)} %bitcast.place_ref.refs_5_, bf16[64,2048]{1,0:T(8,128)(2,1)S(1)} %collective-permute-done.27.refs_0_, ...), custom_call_target="tpu_custom_call", output_to_operand_aliasing={{0}: (8, {}), {1}: (9, {}), {2}: (10, {}), {3}: (11, {})} | custom-call | flops 7864320 | bytes 6291456 | tf_op jit(solution)/shard_map/optimizer/pallas_call | solution.py:611
  120.7 0.0 collective-permute-done.25.refs_1_
  120.7 0.5 collective-permute-done.26.refs_2_
  121.2 0.8 row_grad.1
  (21 shorter events, 0.1 us)
Async XLA Ops:
  1.8 15.6 %copy-start.2 = (f32[16384]{0:T(1024)S(1)}, f32[16384]{0:T(1024)}, u32[]{:S(2)}) copy-start(f32[16384]{0:T(1024)} %param.17) | copy-start | bytes 196612
  1.8 11.9 %collective-permute-start.2 = (bf16[144,256]{1,0:T(8,128)(2,1)S(1)}, bf16[144,256]{1,0:T(8,128)(2,1)S(1)}, u32[]{:S(2)}, u32[]{:S(2)}) collective-permute-start(bf16[144,256]{1,0:T(8,128)(2,1)S(1)} %get-tuple-element.84), channel_id=1, source_target_pairs={{0,6},{1,7},{2,4},{3,5},{4,2},{5,3},{6,0},{7,1},{8,14},{9,15},{10,... | collective-permute-start | bytes 221192 | tf_op jit(solution)/shard_map/ppermute | solution.py:648
  7.0 6.8 %collective-permute-start.1 = (bf16[144,256]{1,0:T(8,128)(2,1)S(1)}, bf16[144,256]{1,0:T(8,128)(2,1)S(1)}, u32[]{:S(2)}, u32[]{:S(2)}) collective-permute-start(bf16[144,256]{1,0:T(8,128)(2,1)S(1)} %get-tuple-element.84), channel_id=1, source_target_pairs={{0,4},{1,5},{2,6},{3,7},{4,0},{5,1},{6,2},{7,3},{8,12},{9,13},{10,... | collective-permute-start | bytes 221192 | tf_op jit(solution)/shard_map/ppermute | solution.py:648
  7.0 6.8 %collective-permute-start = (bf16[144,256]{1,0:T(8,128)(2,1)S(1)}, bf16[144,256]{1,0:T(8,128)(2,1)S(1)}, u32[]{:S(2)}, u32[]{:S(2)}) collective-permute-start(bf16[144,256]{1,0:T(8,128)(2,1)S(1)} %get-tuple-element.84), channel_id=1, source_target_pairs={{0,2},{1,3},{2,0},{3,1},{4,6},{5,7},{6,4},{7,5},{8,10},{9,11},{10,... | collective-permute-start | bytes 221192 | tf_op jit(solution)/shard_map/ppermute | solution.py:648
  13.8 3.6 %collective-permute-start.3 = (bf16[576,256]{1,0:T(8,128)(2,1)S(1)}, bf16[576,256]{1,0:T(8,128)(2,1)S(1)}, u32[]{:S(2)}, u32[]{:S(2)}) collective-permute-start(bf16[576,256]{1,0:T(8,128)(2,1)S(1)} %constant_dynamic-update-slice_fusion.own_ref.refs_0_.refs_4_), channel_id=1, source_target_pairs={{0,1},{1,0},{2,3},{3,2},{4,5},{5,4},{6,7},{7,6},{8,9},{9,8},{10,11... | collective-permute-start | bytes 884744 | tf_op jit(solution)/shard_map/ppermute | solution.py:648
  13.9 16.9 %collective-permute-start.7 = (bf16[576,256]{1,0:T(8,128)(2,1)S(1)}, bf16[576,256]{1,0:T(8,128)(2,1)S(1)}, u32[]{:S(2)}, u32[]{:S(2)}) collective-permute-start(bf16[576,256]{1,0:T(8,128)(2,1)S(1)} %constant_dynamic-update-slice_fusion.own_ref.refs_0_.refs_4_), channel_id=1, source_target_pairs={{0,24},{8,16},{16,8},{24,0},{1,25},{9,17},{17,9},{25,1},{2,26},{10... | collective-permute-start | bytes 884744 | tf_op jit(solution)/shard_map/ppermute | solution.py:651
  16.6 14.2 %collective-permute-start.6 = (bf16[576,256]{1,0:T(8,128)(2,1)S(1)}, bf16[576,256]{1,0:T(8,128)(2,1)S(1)}, u32[]{:S(2)}, u32[]{:S(2)}) collective-permute-start(bf16[576,256]{1,0:T(8,128)(2,1)S(1)} %constant_dynamic-update-slice_fusion.own_ref.refs_0_.refs_4_), channel_id=1, source_target_pairs={{0,16},{8,24},{16,0},{24,8},{1,17},{9,25},{17,1},{25,9},{2,18},{10... | collective-permute-start | bytes 884744 | tf_op jit(solution)/shard_map/ppermute | solution.py:651
  17.1 13.8 %collective-permute-start.5 = (bf16[576,256]{1,0:T(8,128)(2,1)S(1)}, bf16[576,256]{1,0:T(8,128)(2,1)S(1)}, u32[]{:S(2)}, u32[]{:S(2)}) collective-permute-start(bf16[576,256]{1,0:T(8,128)(2,1)S(1)} %constant_dynamic-update-slice_fusion.own_ref.refs_0_.refs_4_), channel_id=1, source_target_pairs={{0,8},{8,0},{16,24},{24,16},{1,9},{9,1},{17,25},{25,17},{2,10},{10... | collective-permute-start | bytes 884744 | tf_op jit(solution)/shard_map/ppermute | solution.py:651
  29.5 1.2 %collective-permute-start.4 = (f32[8,512]{1,0:T(8,128)S(1)}, f32[8,512]{1,0:T(8,128)S(1)}, u32[]{:S(2)}, u32[]{:S(2)}) collective-permute-start(f32[8,512]{1,0:T(8,128)S(1)} %first_pass.1.own_ref), channel_id=1, source_target_pairs={{0,1},{1,0},{2,3},{3,2},{4,5},{5,4},{6,7},{7,6},{8,9},{9,8},{10,11... | collective-permute-start | bytes 49160 | tf_op jit(solution)/shard_map/ppermute | solution.py:648
  30.8 32.9 %collective-permute-start.8 = (bf16[576,256]{1,0:T(8,128)(2,1)S(1)}, bf16[576,256]{1,0:T(8,128)(2,1)S(1)}, u32[]{:S(2)}, u32[]{:S(2)}) collective-permute-start(bf16[576,256]{1,0:T(8,128)(2,1)S(1)} %collective-permute-done.5.refs_2_), channel_id=1, source_target_pairs={{0,1},{1,0},{2,3},{3,2},{4,5},{5,4},{6,7},{7,6},{8,9},{9,8},{10,11... | collective-permute-start | bytes 884744 | tf_op jit(solution)/shard_map/ppermute | solution.py:648
  31.1 32.7 %collective-permute-start.9 = (bf16[576,256]{1,0:T(8,128)(2,1)S(1)}, bf16[576,256]{1,0:T(8,128)(2,1)S(1)}, u32[]{:S(2)}, u32[]{:S(2)}) collective-permute-start(bf16[576,256]{1,0:T(8,128)(2,1)S(1)} %collective-permute-done.6.refs_4_), channel_id=1, source_target_pairs={{0,1},{1,0},{2,3},{3,2},{4,5},{5,4},{6,7},{7,6},{8,9},{9,8},{10,11... | collective-permute-start | bytes 884744 | tf_op jit(solution)/shard_map/ppermute | solution.py:648
  31.4 32.4 %collective-permute-start.10 = (bf16[576,256]{1,0:T(8,128)(2,1)S(1)}, bf16[576,256]{1,0:T(8,128)(2,1)S(1)}, u32[]{:S(2)}, u32[]{:S(2)}) collective-permute-start(bf16[576,256]{1,0:T(8,128)(2,1)S(1)} %collective-permute-done.7.refs_6_), channel_id=1, source_target_pairs={{0,1},{1,0},{2,3},{3,2},{4,5},{5,4},{6,7},{7,6},{8,9},{9,8},{10,11... | collective-permute-start | bytes 884744 | tf_op jit(solution)/shard_map/ppermute | solution.py:648
  31.6 20.7 %collective-permute-start.13 = (f32[8,512]{1,0:T(8,128)S(1)}, f32[8,512]{1,0:T(8,128)S(1)}, u32[]{:S(2)}, u32[]{:S(2)}) collective-permute-start(f32[8,512]{1,0:T(8,128)S(1)} %core_join.1._.refs_0_), channel_id=1, source_target_pairs={{0,6},{1,7},{2,4},{3,5},{4,2},{5,3},{6,0},{7,1},{8,14},{9,15},{10,... | collective-permute-start | bytes 49160 | tf_op jit(solution)/shard_map/ppermute | solution.py:648
  35.3 24.6 %collective-permute-start.12 = (f32[8,512]{1,0:T(8,128)S(1)}, f32[8,512]{1,0:T(8,128)S(1)}, u32[]{:S(2)}, u32[]{:S(2)}) collective-permute-start(f32[8,512]{1,0:T(8,128)S(1)} %core_join.1._.refs_0_), channel_id=1, source_target_pairs={{0,4},{1,5},{2,6},{3,7},{4,0},{5,1},{6,2},{7,3},{8,12},{9,13},{10,... | collective-permute-start | bytes 49160 | tf_op jit(solution)/shard_map/ppermute | solution.py:648
  52.3 7.7 %collective-permute-start.11 = (f32[8,512]{1,0:T(8,128)S(1)}, f32[8,512]{1,0:T(8,128)S(1)}, u32[]{:S(2)}, u32[]{:S(2)}) collective-permute-start(f32[8,512]{1,0:T(8,128)S(1)} %core_join.1._.refs_0_), channel_id=1, source_target_pairs={{0,2},{1,3},{2,0},{3,1},{4,6},{5,7},{6,4},{7,5},{8,10},{9,11},{10,... | collective-permute-start | bytes 49160 | tf_op jit(solution)/shard_map/ppermute | solution.py:648
  60.2 5.9 %collective-permute-start.16 = (f32[8,512]{1,0:T(8,128)S(1)}, f32[8,512]{1,0:T(8,128)S(1)}, u32[]{:S(2)}, u32[]{:S(2)}) collective-permute-start(f32[8,512]{1,0:T(8,128)S(1)} %get-tuple-element.104.refs_0_), channel_id=1, source_target_pairs={{0,24},{8,16},{16,8},{24,0},{1,25},{9,17},{17,9},{25,1},{2,26},{10... | collective-permute-start | bytes 49160 | tf_op jit(solution)/shard_map/ppermute | solution.py:651
  60.2 5.9 %collective-permute-start.15 = (f32[8,512]{1,0:T(8,128)S(1)}, f32[8,512]{1,0:T(8,128)S(1)}, u32[]{:S(2)}, u32[]{:S(2)}) collective-permute-start(f32[8,512]{1,0:T(8,128)S(1)} %get-tuple-element.104.refs_0_), channel_id=1, source_target_pairs={{0,16},{8,24},{16,0},{24,8},{1,17},{9,25},{17,1},{25,9},{2,18},{10... | collective-permute-start | bytes 49160 | tf_op jit(solution)/shard_map/ppermute | solution.py:651
  63.7 3.7 %collective-permute-start.14 = (f32[8,512]{1,0:T(8,128)S(1)}, f32[8,512]{1,0:T(8,128)S(1)}, u32[]{:S(2)}, u32[]{:S(2)}) collective-permute-start(f32[8,512]{1,0:T(8,128)S(1)} %get-tuple-element.104.refs_0_), channel_id=1, source_target_pairs={{0,8},{8,0},{16,24},{24,16},{1,9},{9,1},{17,25},{25,17},{2,10},{10... | collective-permute-start | bytes 49160 | tf_op jit(solution)/shard_map/ppermute | solution.py:651
  79.4 15.5 %collective-permute-start.17 = (bf16[64,2048]{1,0:T(8,128)(2,1)S(1)}, bf16[64,2048]{1,0:T(8,128)(2,1)S(1)}, u32[]{:S(2)}, u32[]{:S(2)}) collective-permute-start(bf16[64,2048]{1,0:T(8,128)(2,1)S(1)} %get-tuple-element.111), channel_id=1, source_target_pairs={{0,8},{8,0},{16,24},{24,16},{1,9},{9,1},{17,25},{25,17},{2,10},{10... | collective-permute-start | bytes 786440 | tf_op jit(solution)/shard_map/ppermute | solution.py:651
  80.2 14.8 %collective-permute-start.18 = (bf16[64,2048]{1,0:T(8,128)(2,1)S(1)}, bf16[64,2048]{1,0:T(8,128)(2,1)S(1)}, u32[]{:S(2)}, u32[]{:S(2)}) collective-permute-start(bf16[64,2048]{1,0:T(8,128)(2,1)S(1)} %get-tuple-element.112), channel_id=1, source_target_pairs={{0,16},{8,24},{16,0},{24,8},{1,17},{9,25},{17,1},{25,9},{2,18},{10... | collective-permute-start | bytes 786440 | tf_op jit(solution)/shard_map/ppermute | solution.py:651
  81.6 13.4 %collective-permute-start.19 = (bf16[64,2048]{1,0:T(8,128)(2,1)S(1)}, bf16[64,2048]{1,0:T(8,128)(2,1)S(1)}, u32[]{:S(2)}, u32[]{:S(2)}) collective-permute-start(bf16[64,2048]{1,0:T(8,128)(2,1)S(1)} %get-tuple-element.113), channel_id=1, source_target_pairs={{0,24},{8,16},{16,8},{24,0},{1,25},{9,17},{17,9},{25,1},{2,26},{10... | collective-permute-start | bytes 786440 | tf_op jit(solution)/shard_map/ppermute | solution.py:651
  83.0 22.1 %copy-start = (f32[64,16384]{1,0:T(8,128)S(1)}, f32[64,16384]{1,0:T(8,128)}, u32[]{:S(2)}) copy-start(f32[64,16384]{1,0:T(8,128)} %refs_5_.1) | copy-start | bytes 12582916
  83.0 22.1 %copy-start.1 = (f32[64,16384]{1,0:T(8,128)S(1)}, f32[64,16384]{1,0:T(8,128)}, u32[]{:S(2)}) copy-start(f32[64,16384]{1,0:T(8,128)} %refs_6_.3) | copy-start | bytes 12582916
  95.0 2.0 %collective-permute-start.20 = (bf16[1040,256]{1,0:T(8,128)(2,1)S(1)}, bf16[1040,256]{1,0:T(8,128)(2,1)S(1)}, u32[]{:S(2)}, u32[]{:S(2)}) collective-permute-start(bf16[1040,256]{1,0:T(8,128)(2,1)S(1)} %get-tuple-element.114), channel_id=1, source_target_pairs={{0,1},{1,0},{2,3},{3,2},{4,5},{5,4},{6,7},{7,6},{8,9},{9,8},{10,11... | collective-permute-start | bytes 1597448 | tf_op jit(solution)/shard_map/ppermute | solution.py:648
  97.1 5.8 %collective-permute-start.21 = (bf16[272,256]{1,0:T(8,128)(2,1)S(1)}, bf16[272,256]{1,0:T(8,128)(2,1)S(1)}, u32[]{:S(2)}, u32[]{:S(2)}) collective-permute-start(bf16[272,256]{1,0:T(8,128)(2,1)S(1)} %get-tuple-element.118), channel_id=1, source_target_pairs={{0,2},{1,3},{2,0},{3,1},{4,6},{5,7},{6,4},{7,5},{8,10},{9,11},{10,... | collective-permute-start | bytes 417800 | tf_op jit(solution)/shard_map/ppermute | solution.py:648
  97.9 18.5 %collective-permute-start.27 = (bf16[64,2048]{1,0:T(8,128)(2,1)S(1)}, bf16[64,2048]{1,0:T(8,128)(2,1)S(1)}, u32[]{:S(2)}, u32[]{:S(2)}) collective-permute-start(bf16[64,2048]{1,0:T(8,128)(2,1)S(1)} %get-tuple-element.142), channel_id=1, source_target_pairs={{0,8},{8,0},{16,24},{24,16},{1,9},{9,1},{17,25},{25,17},{2,10},{10... | collective-permute-start | bytes 786440 | tf_op jit(solution)/shard_map/ppermute | solution.py:651
  99.2 18.2 %collective-permute-start.28 = (bf16[64,2048]{1,0:T(8,128)(2,1)S(1)}, bf16[64,2048]{1,0:T(8,128)(2,1)S(1)}, u32[]{:S(2)}, u32[]{:S(2)}) collective-permute-start(bf16[64,2048]{1,0:T(8,128)(2,1)S(1)} %get-tuple-element.143), channel_id=1, source_target_pairs={{0,16},{8,24},{16,0},{24,8},{1,17},{9,25},{17,1},{25,9},{2,18},{10... | collective-permute-start | bytes 786440 | tf_op jit(solution)/shard_map/ppermute | solution.py:651
  101.2 16.2 %collective-permute-start.29 = (bf16[64,2048]{1,0:T(8,128)(2,1)S(1)}, bf16[64,2048]{1,0:T(8,128)(2,1)S(1)}, u32[]{:S(2)}, u32[]{:S(2)}) collective-permute-start(bf16[64,2048]{1,0:T(8,128)(2,1)S(1)} %get-tuple-element.144), channel_id=1, source_target_pairs={{0,24},{8,16},{16,8},{24,0},{1,25},{9,17},{17,9},{25,1},{2,26},{10... | collective-permute-start | bytes 786440 | tf_op jit(solution)/shard_map/ppermute | solution.py:651
  101.4 12.4 %collective-permute-start.22 = (bf16[272,256]{1,0:T(8,128)(2,1)S(1)}, bf16[272,256]{1,0:T(8,128)(2,1)S(1)}, u32[]{:S(2)}, u32[]{:S(2)}) collective-permute-start(bf16[272,256]{1,0:T(8,128)(2,1)S(1)} %get-tuple-element.119), channel_id=1, source_target_pairs={{0,4},{1,5},{2,6},{3,7},{4,0},{5,1},{6,2},{7,3},{8,12},{9,13},{10,... | collective-permute-start | bytes 417800 | tf_op jit(solution)/shard_map/ppermute | solution.py:648
  102.9 10.9 %collective-permute-start.23 = (bf16[272,256]{1,0:T(8,128)(2,1)S(1)}, bf16[272,256]{1,0:T(8,128)(2,1)S(1)}, u32[]{:S(2)}, u32[]{:S(2)}) collective-permute-start(bf16[272,256]{1,0:T(8,128)(2,1)S(1)} %get-tuple-element.120), channel_id=1, source_target_pairs={{0,6},{1,7},{2,4},{3,5},{4,2},{5,3},{6,0},{7,1},{8,14},{9,15},{10,... | collective-permute-start | bytes 417800 | tf_op jit(solution)/shard_map/ppermute | solution.py:648
  113.8 6.9 %collective-permute-start.24 = (bf16[80,256]{1,0:T(8,128)(2,1)S(1)}, bf16[80,256]{1,0:T(8,128)(2,1)S(1)}, u32[]{:S(2)}, u32[]{:S(2)}) collective-permute-start(bf16[80,256]{1,0:T(8,128)(2,1)S(1)} %get-tuple-element.139), channel_id=1, source_target_pairs={{0,8},{8,0},{16,24},{24,16},{1,9},{9,1},{17,25},{25,17},{2,10},{10... | collective-permute-start | bytes 122888 | tf_op jit(solution)/shard_map/ppermute | solution.py:651
  114.9 5.9 %collective-permute-start.25 = (bf16[80,256]{1,0:T(8,128)(2,1)S(1)}, bf16[80,256]{1,0:T(8,128)(2,1)S(1)}, u32[]{:S(2)}, u32[]{:S(2)}) collective-permute-start(bf16[80,256]{1,0:T(8,128)(2,1)S(1)} %get-tuple-element.140), channel_id=1, source_target_pairs={{0,16},{8,24},{16,0},{24,8},{1,17},{9,25},{17,1},{25,9},{2,18},{10... | collective-permute-start | bytes 122888 | tf_op jit(solution)/shard_map/ppermute | solution.py:651
  116.3 4.9 %collective-permute-start.26 = (bf16[80,256]{1,0:T(8,128)(2,1)S(1)}, bf16[80,256]{1,0:T(8,128)(2,1)S(1)}, u32[]{:S(2)}, u32[]{:S(2)}) collective-permute-start(bf16[80,256]{1,0:T(8,128)(2,1)S(1)} %get-tuple-element.141), channel_id=1, source_target_pairs={{0,24},{8,16},{16,8},{24,0},{1,25},{9,17},{17,9},{25,1},{2,26},{10... | collective-permute-start | bytes 122888 | tf_op jit(solution)/shard_map/ppermute | solution.py:651
